TPU v7x, 256 devices: a whole 4x4x8 slice. The times are simulated.
256 devices in a mesh: seq: 64 (over y, z, core), tp: 4 (over x).
Axes of the slice: x: 4, y: 4, z: 8, core: 2. Of those that a mesh axis runs over, the one named last changes fastest.
Arguments:
- signal: float32 [32, 1048576], P(None, ('seq', 'tp')), may hold values from -6 to 6
- filter_taps: float32 [32, 1048576], P(None, ('seq', 'tp')), as said below
- skip_gain: float32 [32], P('tp'), may hold values from -4 to 4
Outputs:
- output: float32 [32, 1048576], P('tp', 'seq')
Inputs may be any that keep to these rules, and one draw needn't show every extreme that they name: `filter_taps`: filter taps are real values of both signs.
All inputs are finite; a program needn't handle non-finite values.
Results may differ from a plain program's by a relative error of at most 0.000082.
Values sent between devices are 32-bit elements; how exact they have to be, the bound alone decides.
No kernel may reach another device: no remote copies, remote signals or barrier semaphores. Data moves between devices by JAX's collectives and lax.ppermute only.
A program may use at most 64 MiB of HBM per device.

v0:
```python
import math

import jax
import jax.numpy as jnp
from jax import lax
from jax.sharding import PartitionSpec as P

HIGHEST = lax.Precision.HIGHEST
block_radix = 128


def phase_table(product, modulus):
    angle = (product % modulus).astype(jnp.float32) * (2.0 * math.pi / modulus)
    return (jnp.cos(angle), jnp.sin(angle))


def rotate_sum(pattern, spectrum, tables, turn_sign):
    real_part, imag_part = spectrum
    cosine, sine_table = tables
    cos_real = jnp.einsum(pattern, real_part, cosine, precision=HIGHEST)
    cos_imag = jnp.einsum(pattern, imag_part, cosine, precision=HIGHEST)
    sin_real = jnp.einsum(pattern, real_part, sine_table, precision=HIGHEST)
    sin_imag = jnp.einsum(pattern, imag_part, sine_table, precision=HIGHEST)
    return (cos_real - turn_sign * sin_imag, cos_imag + turn_sign * sin_real)


def rotate(spectrum, tables, turn_sign):
    real_part, imag_part = spectrum
    cosine, sine_table = tables
    return (
        real_part * cosine - turn_sign * imag_part * sine_table,
        imag_part * cosine + turn_sign * real_part * sine_table,
    )


def body(signal, filter_taps, skip_gain):
    seq_count = lax.axis_size("seq")
    seq_index = lax.axis_index("seq")
    tp_count = lax.axis_size("tp")
    channels = signal.shape[0] // tp_count
    slab_signal, slab_filter = (
        lax.all_to_all(signal, "tp", split_axis=0, concat_axis=1, tiled=True),
        lax.all_to_all(filter_taps, "tp", split_axis=0, concat_axis=1, tiled=True),
    )
    slab_rows = jnp.concatenate([slab_signal, slab_filter], axis=0)
    all_rows = slab_rows.shape[0]
    tokens = slab_rows.shape[1]
    block_width = tokens // seq_count
    freq_rows = 2 * seq_count
    fft_length = freq_rows * tokens
    inner_count = tokens // block_radix
    row_index = jnp.arange(freq_rows, dtype=jnp.int32)
    token_index = jnp.arange(block_width, dtype=jnp.int32) + seq_index * block_width
    shift_table = phase_table(row_index[:, None] * token_index[None, :], fft_length)
    source_rows = (
        jnp.arange(2, dtype=jnp.int32)[:, None] * seq_count
        + jnp.arange(seq_count, dtype=jnp.int32)[None, :]
    )
    zero_block = jnp.zeros_like(slab_rows)
    padded = jnp.stack([jnp.stack([slab_rows, zero_block]), jnp.stack([zero_block, zero_block])])
    pieces = lax.all_to_all(
        padded.reshape(2, 2, all_rows, 1, seq_count, block_width),
        "seq",
        split_axis=4,
        concat_axis=3,
        tiled=True,
    )
    columns = pieces.reshape(2, 2, all_rows, seq_count, block_width)
    tables = phase_table(source_rows[:, :, None] * row_index[None, None, :], freq_rows)
    spectrum = rotate_sum("hxjm,hjk->xkm", (columns[0], columns[1]), tables, -1.0)
    spectrum = rotate(spectrum, shift_table, -1.0)
    stacked = jnp.stack(spectrum).reshape(2, all_rows, freq_rows, 1, block_width)
    row_planes = lax.all_to_all(stacked, "seq", split_axis=2, concat_axis=3, tiled=True)
    planes = row_planes.reshape(2, all_rows, 2, inner_count, block_radix)
    inner_range = jnp.arange(inner_count, dtype=jnp.int32)
    radix_range = jnp.arange(block_radix, dtype=jnp.int32)
    outer_table = phase_table(inner_range[:, None] * inner_range[None, :], inner_count)
    radix_table = phase_table(radix_range[:, None] * radix_range[None, :], block_radix)
    twist_table = phase_table(inner_range[:, None] * radix_range[None, :], tokens)
    spectrum = rotate_sum("xrba,bk->xrka", (planes[0], planes[1]), outer_table, -1.0)
    spectrum = rotate(spectrum, twist_table, -1.0)
    spectrum = rotate_sum("xrka,ac->xrkc", spectrum, radix_table, -1.0)
    sig_real, sig_imag = (spectrum[0][:channels], spectrum[1][:channels])
    fil_real, fil_imag = (spectrum[0][channels:], spectrum[1][channels:])
    spectrum = (
        sig_real * fil_real - sig_imag * fil_imag,
        sig_real * fil_imag + sig_imag * fil_real,
    )
    spectrum = rotate_sum("xrkc,ca->xrka", spectrum, radix_table, 1.0)
    spectrum = rotate(spectrum, twist_table, 1.0)
    spectrum = rotate_sum("xrka,kb->xrba", spectrum, outer_table, 1.0)
    inverse = jnp.stack(spectrum).reshape(2, channels, 2, seq_count, block_width)
    gathered = lax.all_to_all(inverse, "seq", split_axis=3, concat_axis=2, tiled=True)
    gathered = gathered.reshape(2, channels, freq_rows, block_width)
    spectrum = rotate((gathered[0], gathered[1]), shift_table, 1.0)
    tables = phase_table(row_index[:, None, None] * source_rows[None, :, :], freq_rows)
    spectrum = rotate_sum("xkm,khj->xhjm", spectrum, tables, 1.0)
    stacked = jnp.stack(spectrum).reshape(2, channels, 2, seq_count, 1, block_width)
    arrived = lax.all_to_all(stacked, "seq", split_axis=3, concat_axis=4, tiled=True)
    result = arrived[0, :, 0].reshape(channels, tokens)
    return result / fft_length + skip_gain[:, None] * slab_signal


def solution(mesh):
    placed = (P(None, ("seq", "tp")), P(None, ("seq", "tp")), P("tp"))
    return jax.shard_map(
        body, mesh=mesh, in_specs=placed, out_specs=P("tp", "seq"), check_vma=False
    )
```

profile of v0, /device:TPU:1, one launch (start us, length us, event | category | flops | bytes accessed | tf_op | source)
XLA Modules:
  0.0 445.9 jit_solution(14319236365581633981)
XLA Ops:
  0.0 12.5 %all_to_all.89 = f32[4,8,4096]{2,1,0:T(8,128)S(1)} all-to-all(f32[4,8,4096]{2,1,0:T(8,128)} %bitcast.228), channel_id=1, replica_groups=mesh['seq'=64,'tp'=4] {'tp'}, dimensions={0} | all-to-all | bytes 1048576 | tf_op jit(solution)/shard_map/all_to_all | solution.py:42
  12.5 10.4 %all_to_all.90 = f32[4,8,4096]{2,1,0:T(8,128)S(1)} all-to-all(f32[4,8,4096]{2,1,0:T(8,128)} %bitcast.229), channel_id=1, replica_groups=mesh['seq'=64,'tp'=4] {'tp'}, dimensions={0} | all-to-all | bytes 1048576 | tf_op jit(solution)/shard_map/all_to_all | solution.py:43
  23.4 1.3 copy.91
  24.6 5.2 %copy.40 = f32[2,2,16,1,64,256]{5,1,2,3,0,4:T(2,128)} copy(f32[2,2,16,1,64,256]{5,4,2,1,0,3:T(8,128)S(1)} %bitcast.221) | data formatting | bytes 8388608 | tf_op jit(solution)/shard_map/reshape | solution.py:62
  29.8 16.7 %all-to-all-start.2 = ((f32[2,2,16,1,64,256]{5,1,2,3,0,4:T(2,128)}), f32[2,2,16,1,64,256]{5,1,2,3,0,4:T(2,128)}, u32[]{:S(2)}, u32[]{:S(2)}) async-start(f32[2,2,16,1,64,256]{5,1,2,3,0,4:T(2,128)} %copy.40), calls=%async_computation.2 | async-start | bytes 8388608 | tf_op jit(solution)/shard_map/all_to_all | solution.py:61
  46.6 0.5 fusion.80
  47.2 94.8 %all-to-all-done.2 = f32[2,2,16,1,64,256]{5,1,2,3,0,4:T(2,128)} async-done(((f32[2,2,16,1,64,256]{5,1,2,3,0,4:T(2,128)}), f32[2,2,16,1,64,256]{5,1,2,3,0,4:T(2,128)}, u32[]{:S(2)}, u32[]{:S(2)}) %all-to-all-start.2) | async-done | bytes 4194336 | tf_op jit(solution)/shard_map/all_to_all | solution.py:61
  142.0 3.9 fusion.224
  145.8 3.3 fusion.10
  149.2 3.3 fusion.11
  152.5 3.5 fusion.8
  155.9 4.1 subtract_bitcast_fusion
  160.5 4.4 copy.43
  164.9 5.9 %all-to-all-start.3 = ((f32[2,16,128,1,256]{4,1,0,3,2:T(8,128)}), f32[2,16,128,1,256]{4,1,0,3,2:T(8,128)}, u32[]{:S(2)}, u32[]{:S(2)}) async-start(f32[2,16,128,1,256]{4,1,0,3,2:T(8,128)} %copy.43), calls=%async_computation.3 | async-start | bytes 8388608 | tf_op jit(solution)/shard_map/all_to_all | solution.py:73
  172.0 94.8 %all-to-all-done.3 = f32[2,16,128,1,256]{4,1,0,3,2:T(8,128)} async-done(((f32[2,16,128,1,256]{4,1,0,3,2:T(8,128)}), f32[2,16,128,1,256]{4,1,0,3,2:T(8,128)}, u32[]{:S(2)}, u32[]{:S(2)}) %all-to-all-start.3) | async-done | bytes 4194336 | tf_op jit(solution)/shard_map/all_to_all | solution.py:73
  266.8 4.6 %copy.122 = f32[2,16,64,2,1,256]{5,2,3,1,4,0:T(8,128)S(1)} copy(f32[2,16,64,2,1,256]{5,1,0,3,2,4:T(8,128)} %bitcast.30) | data formatting | bytes 8388608 | tf_op jit(solution)/shard_map/all_to_all | solution.py:73
  271.4 2.3 fusion.223
  273.7 1.6 squeeze.21
  275.3 3.5 fusion.76
  278.7 3.0 squeeze.20
  281.8 3.8 fusion.78
  285.7 2.3 multiply_add_fusion.2
  288.0 2.3 multiply_subtract_fusion.2
  290.3 2.2 fusion.2
  292.5 2.2 fusion
  294.7 2.4 multiply_subtract_fusion
  297.2 2.3 multiply_add_fusion
  299.8 1.2 fusion.68
  301.0 1.2 fusion.70
  302.2 1.2 convolution_add_fusion.2
  303.5 1.2 convolution_subtract_fusion.2
  304.7 1.3 fusion.34
  306.0 2.3 fusion.35
  308.3 2.5 fusion.21
  310.8 2.5 stack.47
  313.3 3.1 copy.57
  316.4 2.3 fusion.20
  318.8 1.6 stack.48
  320.4 0.8 copy.58
  321.2 1.4 pad_maximum_fusion
  322.6 56.8 %all_to_all.91 = f32[2,8,2,64,256]{4,2,1,0,3:T(2,128)S(1)} all-to-all(f32[2,8,2,64,256]{4,2,1,0,3:T(2,128)S(1)} %pad_maximum_fusion), channel_id=1, replica_groups=mesh['seq'=64,'tp'=4] {'seq'}, dimensions={3} | all-to-all | bytes 4194304 | tf_op jit(solution)/shard_map/all_to_all | solution.py:93
  380.1 1.6 fusion.26
  381.7 1.6 fusion.22
  383.3 1.6 fusion.19
  384.9 1.6 fusion.18
  386.6 1.2 copy.64
  387.8 56.9 %all_to_all.92 = f32[2,8,2,64,1,256]{5,1,2,0,4,3:T(8,128)S(1)} all-to-all(f32[2,8,2,64,1,256]{5,1,2,0,4,3:T(8,128)S(1)} %copy.64), channel_id=1, replica_groups=mesh['seq'=64,'tp'=4] {'seq'}, dimensions={3} | all-to-all | bytes 4194304 | tf_op jit(solution)/shard_map/all_to_all | solution.py:99
  444.8 0.9 multiply_add_fusion.7
  (29 shorter events, 3.3 us)
Async XLA Ops:
  29.8 112.1 %all-to-all-start.2 = ((f32[2,2,16,1,64,256]{5,1,2,3,0,4:T(2,128)}), f32[2,2,16,1,64,256]{5,1,2,3,0,4:T(2,128)}, u32[]{:S(2)}, u32[]{:S(2)}) async-start(f32[2,2,16,1,64,256]{5,1,2,3,0,4:T(2,128)} %copy.40), calls=%async_computation.2 | async-start | bytes 8388608 | tf_op jit(solution)/shard_map/all_to_all | solution.py:61
  164.9 101.8 %all-to-all-start.3 = ((f32[2,16,128,1,256]{4,1,0,3,2:T(8,128)}), f32[2,16,128,1,256]{4,1,0,3,2:T(8,128)}, u32[]{:S(2)}, u32[]{:S(2)}) async-start(f32[2,16,128,1,256]{4,1,0,3,2:T(8,128)} %copy.43), calls=%async_computation.3 | async-start | bytes 8388608 | tf_op jit(solution)/shard_map/all_to_all | solution.py:73
  281.8 3.9 copy-start
  281.8 3.9 copy-start.1
  313.3 3.1 copy-start.2
  318.8 2.5 copy-start.3
  387.8 56.9 %copy-start.4 = (f32[8]{0:T(128)S(1)}, f32[8]{0:T(128)}, u32[]{:S(2)}) copy-start(f32[8]{0:T(128)} %param.5) | copy-start | bytes 100
where the time goes:
time: 451 us; the launch traced here: 446 us
  waiting for transfers between devices  190 us (42%)
  blocking collectives  137 us (30%)
  matrix products  54.8 us (12%)
  local copies, waits for them, and re-layouts  36.6 us (8%)
  starting transfers between devices  22.6 us (5%)
  other arithmetic  5.11 us (1%)
    all_to_all x1, waiting for transfers between devices, body(): lax.all_to_all(stacked, 'seq', split_axis=2, concat_axis=3, tiled=True)  94.8 us
    all_to_all x1, waiting for transfers between devices, body(): lax.all_to_all(padded.reshape(2, 2, all_rows, 1, seq_count, block_width),...  94.8 us
    all_to_all x1, blocking collectives, body(): lax.all_to_all(stacked, 'seq', split_axis=3, concat_axis=4, tiled=True)  56.9 us
    all_to_all x1, blocking collectives, body(): lax.all_to_all(inverse, 'seq', split_axis=3, concat_axis=2, tiled=True)  56.8 us
    all_to_all x1, starting transfers between devices, body(): lax.all_to_all(padded.reshape(2, 2, all_rows, 1, seq_count, block_width),...  16.7 us
    dot_general x6, matrix products, rotate_sum(): cos_imag = jnp.einsum(pattern, imag_part, cosine, precision=HIGHEST)  14.2 us
    dot_general x6, matrix products, rotate_sum(): sin_imag = jnp.einsum(pattern, imag_part, sine_table, precision=HIGHEST)  14 us
    dot_general x6, matrix products, rotate_sum(): cos_real = jnp.einsum(pattern, real_part, cosine, precision=HIGHEST)  13.7 us
  transfers between devices with their start and end apart: 2, of which 2 were waited for; matrix products, arithmetic and copies ran while one was open for 0% of the time, Pallas kernels for 0%

commit v1 on v0

v1 whole, which is shorter than its diff:
```python
import functools
import math

import jax
import jax.numpy as jnp
import ml_dtypes
import numpy as np
from jax import lax
from jax.experimental import pallas as pl
from jax.experimental.pallas import tpu as pltpu
from jax.sharding import PartitionSpec as P

LENGTH = 1 << 20
BLOCKS = 256
LANES = 128
AXES = ("seq", "tp")
VMEM = pl.BlockSpec(memory_space=pltpu.VMEM)
SMEM = pl.BlockSpec(memory_space=pltpu.SMEM)
PARAMS = pltpu.CompilerParams(vmem_limit_bytes=48 * 1024 * 1024)


def device(y, z, core, x):
    return (((y % 4) * 8 + z % 8) * 2 + core) * 4 + x % 4


def member(slab, row, g):
    core = slab % 2
    y = 2 * (row // 4) + core + (g >> 2)
    z = 2 * (row % 4) + core + ((g >> 1) & 1)
    return device(y, z, core, slab + (g & 1))


def keeper(slab, row, o):
    return device(2 * (row // 4) + (o >> 2), 2 * (row % 4) + ((o >> 1) & 1), o & 1, slab)


GROUPS = [(slab, row) for slab in range(4) for row in range(8)]


def among_members(flip):
    return [(member(s, r, g), member(s, r, g ^ flip)) for s, r in GROUPS for g in range(8)]


def to_keepers(flip):
    return [(member(s, r, g), keeper(s, r, first_range(s % 2, g) ^ flip)) for s, r in GROUPS for g in range(8)]


def first_range(core, g):
    return (g & 6) | ((g & 1) ^ core)


def halves(x):
    high = x.astype(ml_dtypes.bfloat16)
    low = (x - high.astype(np.float64)).astype(ml_dtypes.bfloat16)
    return high, low


@functools.cache
def tables():
    j = np.arange(BLOCKS)[:, None]
    k = np.arange(BLOCKS)[None, :] + 0.25
    angle = 2.0 * math.pi * ((j * k) % BLOCKS) / BLOCKS
    cos, sin = np.cos(angle), np.sin(angle)
    ahead_high, ahead_low = halves(np.concatenate([cos.T, -sin.T], axis=0))
    back_high, back_low = halves(np.concatenate([cos, -sin], axis=1) / LENGTH)
    t = np.arange(4096)[:, None]
    angle = (2.0 * math.pi / LENGTH) * (t * k)
    turn = np.stack([np.cos(angle), -np.sin(angle)])
    turn = turn.reshape(2, 8, 512, BLOCKS).transpose(1, 0, 3, 2).astype(np.float32)
    b = np.arange(LANES)
    angle = 2.0 * math.pi * ((b[:, None] * b[None, :]) % LANES) / LANES
    cos, sin = np.cos(angle), np.sin(angle)
    lane_high, lane_low = halves(np.block([[cos, -sin], [sin, cos]]))
    unlane_high, unlane_low = halves(np.block([[cos, sin], [-sin, cos]]))
    angle = (2.0 * math.pi / 4096) * (np.arange(32)[:, None] * b[None, :])
    twist = np.stack([np.cos(angle), -np.sin(angle)], axis=1)
    twist = np.broadcast_to(twist[:, :, None, :], (32, 2, 8, LANES)).astype(np.float32)
    return dict(
        ahead=np.concatenate([ahead_high, ahead_high, ahead_low], axis=1),
        back=np.concatenate([back_high, back_high, back_low], axis=1),
        turn=turn,
        lane=np.concatenate([lane_high, lane_high, lane_low], axis=0),
        unlane=np.concatenate([unlane_high, unlane_high, unlane_low], axis=0),
        twist=np.ascontiguousarray(twist),
    )


def split(x):
    high = x.astype(jnp.bfloat16)
    return high, (x - high.astype(jnp.float32)).astype(jnp.bfloat16)


def dot(a, b):
    return lax.dot_general(a, b, (((1,), (0,)), ((), ())), preferred_element_type=jnp.float32)


def times(re, im, factor):
    c, s = factor.real, factor.imag
    if abs(s) < 1e-12:
        return (re, im) if c > 0 else (-re, -im)
    if abs(c) < 1e-12:
        return (-im, re) if s > 0 else (im, -re)
    if abs(abs(c) - abs(s)) < 1e-12:
        p, q = np.sign(c), np.sign(s)
        first = re - im if p == q else re + im
        second = im + re if p == q else im - re
        return first * np.float32(c), second * np.float32(c)
    c, s = np.float32(c), np.float32(s)
    return re * c - im * s, re * s + im * c


def fourier(values, sign):
    size = len(values)
    if size == 1:
        return values
    even, odd = fourier(values[0::2], sign), fourier(values[1::2], sign)
    first, second = [], []
    for i in range(size // 2):
        angle = sign * 2.0 * math.pi * i / size
        re, im = times(*odd[i], complex(math.cos(angle), math.sin(angle)))
        first.append((even[i][0] + re, even[i][1] + im))
        second.append((even[i][0] - re, even[i][1] - im))
    return first + second


def unit(sign, numerator, denominator):
    angle = sign * 2.0 * math.pi * numerator / denominator
    return complex(math.cos(angle), math.sin(angle))


def pack_kernel(signal_ref, taps_ref, out_ref, rows_ref):
    for at, ref in enumerate((signal_ref, taps_ref)):
        for cb in range(4):
            for col in range(32):
                rows_ref[at, pl.ds((cb * 32 + col) * 8, 8), :] = ref[pl.ds(8 * cb, 8), pl.ds(128 * col, 128)]
    for slab in range(4):
        for row in range(8):
            for g in range(8):
                to = member(slab, row, g)
                for at in range(2):
                    start = (slab * 32 + 4 * g) * 8 + row
                    out_ref[to, pl.ds(4 * at, 4), :] = rows_ref[at, pl.ds(start, 4, stride=8), :]


def pack(signal, taps):
    return pl.pallas_call(
        pack_kernel,
        out_shape=jax.ShapeDtypeStruct((256, 8, LANES), jnp.float32),
        in_specs=[VMEM, VMEM],
        out_specs=VMEM,
        scratch_shapes=[pltpu.VMEM((2, 1024, LANES), jnp.float32)],
        compiler_params=PARAMS,
    )(signal, taps)


def ahead_kernel(place_ref, gain_ref, x_ref, ahead_ref, turn_ref, *rest):
    outs, (x2_ref, y_ref) = rest[:8], rest[8:]
    g = place_ref[0]
    for s in range(8):
        x = x_ref[pl.ds(s, 256, stride=8), :]
        if s == 4:
            row = lax.broadcasted_iota(jnp.int32, x.shape, 0)
            lane = lax.broadcasted_iota(jnp.int32, x.shape, 1)
            x = x + jnp.where((row == 0) & (lane == 0), gain_ref[0], 0.0)
        high, low = split(x)
        x2_ref[pl.ds(0, 256), pl.ds(128 * s, 128)] = high
        x2_ref[pl.ds(256, 256), pl.ds(128 * s, 128)] = low
    for n in range(4):
        cols = pl.ds(256 * n, 256)
        y_ref[:, cols] = dot(ahead_ref[:, :512], x2_ref[:, cols]) + dot(ahead_ref[:, 512:], x2_ref[:256, cols])
    for flip in range(8):
        to = pl.multiple_of((g ^ flip) * 32, 32)
        for a in range(4):
            tr = turn_ref[0, 0, pl.ds(to, 32), pl.ds(128 * a, 128)]
            ti = turn_ref[0, 1, pl.ds(to, 32), pl.ds(128 * a, 128)]
            for sf in range(2):
                cols = pl.ds(512 * sf + 128 * a, 128)
                re, im = y_ref[pl.ds(to, 32), cols], y_ref[pl.ds(256 + to, 32), cols]
                outs[flip][0, sf, a] = re * tr - im * ti
                outs[flip][1, sf, a] = re * ti + im * tr


def whole(shape):
    return pl.BlockSpec(shape, lambda i, place: (0,) * len(shape))


def ahead(place, gain, x, table, turn):
    block = (2, 2, 4, 32, LANES)
    return pl.pallas_call(
        ahead_kernel,
        out_shape=[jax.ShapeDtypeStruct(block, jnp.float32)] * 8,
        grid_spec=pltpu.PrefetchScalarGridSpec(
            num_scalar_prefetch=1,
            grid=(1,),
            in_specs=[
                SMEM,
                whole((2048, LANES)),
                whole((512, 768)),
                pl.BlockSpec((1, 2, 256, 512), lambda i, place: (place[0], 0, 0, 0)),
            ],
            out_specs=[whole(block)] * 8,
            scratch_shapes=[pltpu.VMEM((512, 1024), jnp.bfloat16), pltpu.VMEM((512, 1024), jnp.float32)],
        ),
        compiler_params=PARAMS,
    )(place, gain, x, table, turn)


def middle_kernel(place_ref, *refs):
    ins, (lane_ref, unlane_ref, twist_ref) = refs[:8], refs[8:11]
    outs, (x_ref, m_ref, d_ref, y_ref) = refs[11:19], refs[19:]
    g, o = place_ref[0], place_ref[1]
    for flip in range(8):
        x_ref[g ^ flip] = ins[flip][...]

    def step(kb, carry):
        rows = pl.ds(pl.multiple_of(kb * 8, 8), 8)
        for sf in range(2):
            for a in range(4):
                values = [(x_ref[s, 0, sf, a, rows, :], x_ref[s, 1, sf, a, rows, :]) for s in range(8)]
                for m1, value in enumerate(fourier(values, -1)):
                    re, im = times(*value, unit(-1, a * m1, 32))
                    m_ref[m1, a, 0], m_ref[m1, a, 1] = re, im
            for m1 in range(8):
                values = fourier([(m_ref[m1, a, 0], m_ref[m1, a, 1]) for a in range(4)], -1)
                for m2, (re, im) in enumerate(values):
                    m = m1 + 8 * m2
                    tr, ti = twist_ref[m, 0], twist_ref[m, 1]
                    d_ref[pl.ds(256 * sf + 8 * m, 8), :128] = re * tr - im * ti
                    d_ref[pl.ds(256 * sf + 8 * m, 8), 128:] = re * ti + im * tr
        high, low = split(d_ref[...])
        d = dot(jnp.concatenate([high, low, high], axis=1), lane_ref[...])
        sr, si, fr, fi = d[:256, :128], d[:256, 128:], d[256:, :128], d[256:, 128:]
        high, low = split(jnp.concatenate([sr * fr - si * fi, sr * fi + si * fr], axis=1))
        d_ref[pl.ds(0, 256), :] = dot(jnp.concatenate([high, low, high], axis=1), unlane_ref[...])
        for m1 in range(8):
            values = []
            for m2 in range(4):
                m = m1 + 8 * m2
                tr, ti = twist_ref[m, 0], twist_ref[m, 1]
                re, im = d_ref[pl.ds(8 * m, 8), :128], d_ref[pl.ds(8 * m, 8), 128:]
                values.append((re * tr + im * ti, im * tr - re * ti))
            for a, value in enumerate(fourier(values, 1)):
                re, im = times(*value, unit(1, a * m1, 32))
                m_ref[m1, a, 0], m_ref[m1, a, 1] = re, im
        for a in range(4):
            values = fourier([(m_ref[m1, a, 0], m_ref[m1, a, 1]) for m1 in range(8)], 1)
            for at, (re, im) in enumerate(values):
                y_ref[at, 0, a, rows, :], y_ref[at, 1, a, rows, :] = re, im
        return carry

    lax.fori_loop(0, 4, step, 0)
    for flip in range(8):
        outs[flip][...] = y_ref[o ^ flip]


def middle(place, blocks, lane, unlane, twist):
    block = (2, 4, 32, LANES)
    return pl.pallas_call(
        middle_kernel,
        out_shape=[jax.ShapeDtypeStruct(block, jnp.float32)] * 8,
        in_specs=[SMEM] + [VMEM] * 11,
        out_specs=[VMEM] * 8,
        scratch_shapes=[
            pltpu.VMEM((8, 2, 2, 4, 32, LANES), jnp.float32),
            pltpu.VMEM((8, 4, 2, 8, LANES), jnp.float32),
            pltpu.VMEM((512, 256), jnp.float32),
            pltpu.VMEM((8, 2, 4, 32, LANES), jnp.float32),
        ],
        compiler_params=PARAMS,
    )(place, *blocks, lane, unlane, twist)


def back_kernel(place_ref, *refs):
    ins, (back_ref, turn_ref), out_ref, (y2_ref,) = refs[:8], refs[8:10], refs[10], refs[11:]
    g = place_ref[2]
    for flip in range(8):
        at = pl.multiple_of((g ^ flip) * 32, 32)
        for a in range(4):
            cols = pl.ds(128 * a, 128)
            tr, ti = turn_ref[0, 0, pl.ds(at, 32), cols], turn_ref[0, 1, pl.ds(at, 32), cols]
            re, im = ins[flip][0, a], ins[flip][1, a]
            for part, value in enumerate((re * tr + im * ti, im * tr - re * ti)):
                high, low = split(value)
                y2_ref[pl.ds(256 * part + at, 32), cols] = high
                y2_ref[pl.ds(512 + 256 * part + at, 32), cols] = low
    for n in range(2):
        cols = pl.ds(256 * n, 256)
        y = dot(back_ref[:, :1024], y2_ref[:, cols]) + dot(back_ref[:, 1024:], y2_ref[:512, cols])
        for a in range(2):
            out_ref[pl.ds(2 * n + a, 256, stride=4), :] = y[:, 128 * a : 128 * (a + 1)]


def back(place, blocks, table, turn):
    return pl.pallas_call(
        back_kernel,
        out_shape=jax.ShapeDtypeStruct((1024, LANES), jnp.float32),
        grid_spec=pltpu.PrefetchScalarGridSpec(
            num_scalar_prefetch=1,
            grid=(1,),
            in_specs=[whole((2, 4, 32, LANES))] * 8
            + [whole((256, 1536)), pl.BlockSpec((1, 2, 256, 512), lambda i, place: (place[3], 0, 0, 0))],
            out_specs=whole((1024, LANES)),
            scratch_shapes=[pltpu.VMEM((1024, 512), jnp.bfloat16)],
        ),
        compiler_params=PARAMS,
    )(place, *blocks, table, turn)


def unpack_kernel(x_ref, out_ref):
    for jl in range(4):
        for o in range(8):
            for a in range(4):
                start = (16 * (o >> 2) + 2 * ((o >> 1) & 1) + (o & 1)) * 16 + jl * 4 + a
                cols = pl.ds(128 * (jl * 32 + 4 * o + a), 128)
                for half in range(2):
                    out_ref[pl.ds(4 * half, 4), cols] = x_ref[pl.ds(start + 512 * half, 4, stride=64), :]


def unpack(x):
    return pl.pallas_call(
        unpack_kernel,
        out_shape=jax.ShapeDtypeStruct((8, 16384), jnp.float32),
        in_specs=[VMEM],
        out_specs=VMEM,
        compiler_params=PARAMS,
    )(x)


def body(signal, filter_taps, skip_gain):
    known = tables()
    seq, x = lax.axis_index("seq"), lax.axis_index("tp")
    y, z, core = seq // 16, (seq // 2) % 8, seq % 2
    dy, dz, dx = (y - core) % 2, (z - core) % 2, (x - core) % 2
    g = 4 * dy + 2 * dz + dx
    row = ((y - core) % 4) // 2 * 4 + ((z - core) % 8) // 2
    first = 4 * dy + 2 * dz + (dx ^ core)
    o = 4 * (y % 2) + 2 * (z % 2) + core
    source = 4 * (y % 2) + 2 * (z % 2) + (core ^ (x % 2))
    place = jnp.stack([g, first, source, o]).astype(jnp.int32)
    gain = jnp.where(g == 0, skip_gain[row], 0.0).reshape(1)

    packed = pack(signal, filter_taps)
    tokens = lax.all_to_all(packed, AXES, split_axis=0, concat_axis=0, tiled=True)
    turn = jnp.asarray(known["turn"])
    parts = ahead(place, gain, tokens.reshape(2048, LANES), jnp.asarray(known["ahead"]), turn)
    parts = [parts[0]] + [lax.ppermute(parts[i], AXES, among_members(i)) for i in range(1, 8)]
    parts = middle(place, parts, jnp.asarray(known["lane"]), jnp.asarray(known["unlane"]), jnp.asarray(known["twist"]))
    parts = [lax.ppermute(parts[i], AXES, to_keepers(i)) for i in range(8)]
    result = back(place, parts, jnp.asarray(known["back"]), turn)
    result = lax.all_to_all(result.reshape(64, 16, LANES), "seq", split_axis=0, concat_axis=0, tiled=True)
    return unpack(result.reshape(1024, LANES))


def solution(mesh):
    placed = (P(None, ("seq", "tp")), P(None, ("seq", "tp")), P("tp"))
    return jax.shard_map(
        body, mesh=mesh, in_specs=placed, out_specs=P("tp", "seq"), check_vma=False
    )
```

time: 451 us -> 137 us (0.30)
  waiting for transfers between devices: 190 us -> 41.6 us
  blocking collectives: 137 us -> 21.9 us
  matrix products: 54.8 us -> 0 us
  local copies, waits for them, and re-layouts: 36.6 us -> 4.47 us
  starting transfers between devices: 22.6 us -> 53.6 us
  Pallas kernels: 0 us -> 12.6 us
  other arithmetic: 5.11 us -> 0.08 us
    all_to_all x2 -> x1, waiting for transfers between devices: 190 us -> 30.3 us  [body(): lax.all_to_all(packed, AXES, split_axis=0, concat_axis=0, tiled=True)]
    all_to_all x4 -> x1, blocking collectives: 137 us -> 21.9 us  [body(): lax.all_to_all(result.reshape(64, 16, LANES), 'seq', split_axis=0, concat...]
    dot_general x24 -> x0, matrix products: 54.8 us -> none  [the longest x6 14.2 us: rotate_sum(): cos_imag = jnp.einsum(pattern, imag_part, cosine, precision=HIGHEST)]
    ppermute x0 -> x15, starting transfers between devices: none -> 37.9 us  [the longest x8 23.2 us: body(): parts = [lax.ppermute(parts[i], AXES, to_keepers(i)) for i in range(8)]]
    pallas_call x0 -> x5, Pallas kernels: none -> 12.6 us  [the longest x1 4.27 us: middle(): pl.pallas_call(middle_kernel, out_shape=[jax.ShapeDtypeStruct(block, jnp....]
    ppermute x0 -> x15, waiting for transfers between devices: none -> 11.3 us  [the longest x7 6.56 us: body(): lax.ppermute(parts[i], AXES, among_members(i))]
    reshape x3 -> x0, local copies, waits for them, and re-layouts: 10.8 us -> none  [the longest x1 5.2 us: body(): padded.reshape(2, 2, all_rows, 1, seq_count, block_width)]
    another operation x6 -> x0, local copies, waits for them, and re-layouts: 8.45 us -> none  [the longest x4 8.04 us: body(): jnp.stack(spectrum).reshape(2, channels, 2, seq_count, block_width)]
  transfers between devices with their start and end apart: 2 -> 16, of which waited for: 2 -> 7; matrix products, arithmetic and copies ran while one was open for 0% -> 1% of each run, Pallas kernels for 0% -> 0%
where the time goes in v1:
time: 137 us; the launch traced here: 135 us
  starting transfers between devices  53.6 us (39%)
  waiting for transfers between devices  41.6 us (30%)
  blocking collectives  21.9 us (16%)
  Pallas kernels  12.6 us (9%)
  local copies, waits for them, and re-layouts  4.47 us (3%)
    all_to_all x1, waiting for transfers between devices, body(): lax.all_to_all(packed, AXES, split_axis=0, concat_axis=0, tiled=True)  30.3 us
    ppermute x8, starting transfers between devices, body(): parts = [lax.ppermute(parts[i], AXES, to_keepers(i)) for i in range(8)]  23.2 us
    all_to_all x1, blocking collectives, body(): lax.all_to_all(result.reshape(64, 16, LANES), 'seq', split_axis=0, concat...  21.9 us
    all_to_all x1, starting transfers between devices, body(): lax.all_to_all(packed, AXES, split_axis=0, concat_axis=0, tiled=True)  15.7 us
    ppermute x7, starting transfers between devices, body(): lax.ppermute(parts[i], AXES, among_members(i))  14.7 us
    ppermute x7, waiting for transfers between devices, body(): lax.ppermute(parts[i], AXES, among_members(i))  6.56 us
    ppermute x8, waiting for transfers between devices, body(): parts = [lax.ppermute(parts[i], AXES, to_keepers(i)) for i in range(8)]  4.74 us
    pallas_call x1, Pallas kernels, middle(): pl.pallas_call(middle_kernel, out_shape=[jax.ShapeDtypeStruct(block, jnp....  4.27 us
  transfers between devices with their start and end apart: 16, of which 7 were waited for; matrix products, arithmetic and copies ran while one was open for 1% of the time, Pallas kernels for 0%

profile of v1, /device:TPU:1, one launch (start us, length us, event | category | flops | bytes accessed | tf_op | source)
XLA Modules:
  0.0 135.1 jit_solution(4798910074520485832)
XLA Ops:
  0.0 0.0 copy-start.2
  0.0 1.0 copy-done.2
  1.0 1.0 copy-done.3
  2.1 1.3 shard_map.91
  3.4 15.7 %all-to-all-start = ((f32[256,8,128]{2,1,0:T(8,128)}), f32[256,8,128]{2,1,0:T(8,128)S(1)}, u32[]{:S(2)}, u32[]{:S(2)}) async-start(f32[256,8,128]{2,1,0:T(8,128)} %shard_map.91), calls=%async_computation | async-start | bytes 2097152 | tf_op jit(solution)/shard_map/all_to_all | solution.py:343
  19.3 1.2 dynamic_slice.3
  21.1 0.1 pad_add_fusion.place_ref
  21.2 30.3 %all-to-all-done = f32[256,8,128]{2,1,0:T(8,128)S(1)} async-done(((f32[256,8,128]{2,1,0:T(8,128)}), f32[256,8,128]{2,1,0:T(8,128)S(1)}, u32[]{:S(2)}, u32[]{:S(2)}) %all-to-all-start) | async-done | bytes 1048608 | tf_op jit(solution)/shard_map/all_to_all | solution.py:343
  51.6 1.1 copy-done.1
  52.7 3.2 %shard_map.92 = (f32[2,2,4,32,128]{4,3,2,1,0:T(8,128)S(1)}, f32[2,2,4,32,128]{4,3,2,1,0:T(8,128)S(1)}, f32[2,2,4,32,128]{4,3,2,1,0:T(8,128)S(1)}, f32[2,2,4,32,1...) custom-call(s32[4]{0:T(128)S(1)} %pad_add_fusion.place_ref, ...), custom_call_target="tpu_custom_call" | custom-call | tf_op jit(solution)/shard_map/pallas_call | solution.py:189
  55.9 0.1 collective-permute-start
  56.0 0.5 collective-permute-start.1
  56.5 4.6 %collective-permute-start.2 = (f32[2,2,4,32,128]{4,3,2,1,0:T(8,128)S(1)}, f32[2,2,4,32,128]{4,3,2,1,0:T(8,128)S(1)}, u32[]{:S(2)}, u32[]{:S(2)}) collective-permute-start(f32[2,2,4,32,128]{4,3,2,1,0:T(8,128)S(1)} %get-tuple-element.24), channel_id=1, source_target_pairs={{0,9},{1,8},{8,1},{9,0},{64,73},{65,72},{72,65},{73,64},{16,25},{1... | collective-permute-start | bytes 786440 | tf_op jit(solution)/shard_map/ppermute | solution.py:346
  61.0 0.5 collective-permute-start.3
  61.5 2.0 %collective-permute-start.4 = (f32[2,2,4,32,128]{4,3,2,1,0:T(8,128)S(1)}, f32[2,2,4,32,128]{4,3,2,1,0:T(8,128)S(1)}, u32[]{:S(2)}, u32[]{:S(2)}) collective-permute-start(f32[2,2,4,32,128]{4,3,2,1,0:T(8,128)S(1)} %get-tuple-element.26), channel_id=1, source_target_pairs={{0,65},{1,64},{8,73},{9,72},{64,1},{65,0},{72,9},{73,8},{16,81},{1... | collective-permute-start | bytes 786440 | tf_op jit(solution)/shard_map/ppermute | solution.py:346
  63.5 0.0 collective-permute-done.refs_1_
  63.5 1.2 collective-permute-start.5
  64.7 0.0 collective-permute-done.1.refs_2_
  64.7 5.9 %collective-permute-start.6 = (f32[2,2,4,32,128]{4,3,2,1,0:T(8,128)S(1)}, f32[2,2,4,32,128]{4,3,2,1,0:T(8,128)S(1)}, u32[]{:S(2)}, u32[]{:S(2)}) collective-permute-start(f32[2,2,4,32,128]{4,3,2,1,0:T(8,128)S(1)} %get-tuple-element.28), channel_id=1, source_target_pairs={{0,73},{1,72},{8,65},{9,64},{64,9},{65,8},{72,1},{73,0},{16,89},{1... | collective-permute-start | bytes 786440 | tf_op jit(solution)/shard_map/ppermute | solution.py:346
  70.6 0.0 collective-permute-done.2.refs_3_
  70.6 0.0 collective-permute-done.3.refs_4_
  70.6 1.4 %collective-permute-done.4.refs_5_ = f32[2,2,4,32,128]{4,3,2,1,0:T(8,128)S(1)} collective-permute-done((f32[2,2,4,32,128]{4,3,2,1,0:T(8,128)S(1)}, f32[2,2,4,32,128]{4,3,2,1,0:T(8,128)S(1)}, u32[]{:S(2)}, u32[]{:S(2)}) %collective-permute-start.4) | collective-permute-done | bytes 262176 | tf_op jit(solution)/shard_map/ppermute | solution.py:346
  72.0 1.4 %collective-permute-done.5.refs_6_ = f32[2,2,4,32,128]{4,3,2,1,0:T(8,128)S(1)} collective-permute-done((f32[2,2,4,32,128]{4,3,2,1,0:T(8,128)S(1)}, f32[2,2,4,32,128]{4,3,2,1,0:T(8,128)S(1)}, u32[]{:S(2)}, u32[]{:S(2)}) %collective-permute-start.5) | collective-permute-done | bytes 262176 | tf_op jit(solution)/shard_map/ppermute | solution.py:346
  73.4 3.7 %collective-permute-done.6.refs_7_ = f32[2,2,4,32,128]{4,3,2,1,0:T(8,128)S(1)} collective-permute-done((f32[2,2,4,32,128]{4,3,2,1,0:T(8,128)S(1)}, f32[2,2,4,32,128]{4,3,2,1,0:T(8,128)S(1)}, u32[]{:S(2)}, u32[]{:S(2)}) %collective-permute-start.6) | collective-permute-done | bytes 262176 | tf_op jit(solution)/shard_map/ppermute | solution.py:346
  77.2 0.0 copy-done.4
  77.2 0.0 copy-done.5
  77.2 0.0 copy-done.6
  77.2 4.3 %shard_map.93 = (f32[2,4,32,128]{3,2,1,0:T(8,128)S(1)}, f32[2,4,32,128]{3,2,1,0:T(8,128)S(1)}, f32[2,4,32,128]{3,2,1,0:T(8,128)S(1)}, f32[2,4,32,128]{3,2,1,0:T(...) custom-call(s32[4]{0:T(128)S(1)} %pad_add_fusion.place_ref, ...), custom_call_target="tpu_custom_call" | custom-call | tf_op jit(solution)/shard_map/pallas_call | solution.py:258
  81.5 1.9 %collective-permute-start.7 = (f32[2,4,32,128]{3,2,1,0:T(8,128)S(1)}, f32[2,4,32,128]{3,2,1,0:T(8,128)S(1)}, u32[]{:S(2)}, u32[]{:S(2)}) collective-permute-start(f32[2,4,32,128]{3,2,1,0:T(8,128)S(1)} %get-tuple-element.29), channel_id=1, source_target_pairs={{0,0},{1,4},{8,8},{9,12},{64,64},{65,68},{72,72},{73,76},{16,16},{... | collective-permute-start | bytes 393224 | tf_op jit(solution)/shard_map/ppermute | solution.py:348
  83.4 4.2 %collective-permute-start.8 = (f32[2,4,32,128]{3,2,1,0:T(8,128)S(1)}, f32[2,4,32,128]{3,2,1,0:T(8,128)S(1)}, u32[]{:S(2)}, u32[]{:S(2)}) collective-permute-start(f32[2,4,32,128]{3,2,1,0:T(8,128)S(1)} %get-tuple-element.30), channel_id=1, source_target_pairs={{0,4},{1,0},{8,12},{9,8},{64,68},{65,64},{72,76},{73,72},{16,20},{... | collective-permute-start | bytes 393224 | tf_op jit(solution)/shard_map/ppermute | solution.py:348
  87.6 0.0 collective-permute-start.9
  87.6 0.0 collective-permute-start.10
  87.6 0.3 collective-permute-start.11
  87.9 0.1 collective-permute-done.7.refs_0_
  88.0 3.9 %collective-permute-start.12 = (f32[2,4,32,128]{3,2,1,0:T(8,128)S(1)}, f32[2,4,32,128]{3,2,1,0:T(8,128)S(1)}, u32[]{:S(2)}, u32[]{:S(2)}) collective-permute-start(f32[2,4,32,128]{3,2,1,0:T(8,128)S(1)} %get-tuple-element.34), channel_id=1, source_target_pairs={{0,68},{1,64},{8,76},{9,72},{64,4},{65,0},{72,12},{73,8},{16,84},{... | collective-permute-start | bytes 393224 | tf_op jit(solution)/shard_map/ppermute | solution.py:348
  91.9 0.0 collective-permute-done.8.refs_1_
  91.9 12.1 %collective-permute-start.13 = (f32[2,4,32,128]{3,2,1,0:T(8,128)S(1)}, f32[2,4,32,128]{3,2,1,0:T(8,128)S(1)}, u32[]{:S(2)}, u32[]{:S(2)}) collective-permute-start(f32[2,4,32,128]{3,2,1,0:T(8,128)S(1)} %get-tuple-element.35), channel_id=1, source_target_pairs={{0,72},{1,76},{8,64},{9,68},{64,8},{65,12},{72,0},{73,4},{16,88},{... | collective-permute-start | bytes 393224 | tf_op jit(solution)/shard_map/ppermute | solution.py:348
  104.0 0.0 collective-permute-done.9.refs_2_
  104.0 0.8 collective-permute-start.14
  104.8 0.0 collective-permute-done.10.refs_3_
  104.8 0.0 collective-permute-done.11.refs_4_
  104.8 0.0 collective-permute-done.12.refs_5_
  104.8 1.1 collective-permute-done.13.refs_6_
  105.9 3.5 %collective-permute-done.14.refs_7_ = f32[2,4,32,128]{3,2,1,0:T(8,128)S(1)} collective-permute-done((f32[2,4,32,128]{3,2,1,0:T(8,128)S(1)}, f32[2,4,32,128]{3,2,1,0:T(8,128)S(1)}, u32[]{:S(2)}, u32[]{:S(2)}) %collective-permute-start.14) | collective-permute-done | bytes 131104 | tf_op jit(solution)/shard_map/ppermute | solution.py:348
  109.4 0.0 copy-done
  109.4 2.6 %shard_map.94 = f32[1024,128]{1,0:T(8,128)S(1)} custom-call(s32[4]{0:T(128)S(1)} %pad_add_fusion.place_ref, f32[2,4,32,128]{3,2,1,0:T(8,128)S(1)} %collective-permute-done.7.refs_0_, f32[2,4,32,128]{3,2,1,0:T(8,128)S(1)} %collective-permute-done.8.refs_1_, f32[2,4,32,128]{3,2,1,0:T(8,128)S(1)} %collective-permute-done.9.refs_2_, ...), custom_call_target="tpu_custom_call" | custom-call | tf_op jit(solution)/shard_map/pallas_call | solution.py:294
  112.1 21.9 %all_to_all.10 = f32[64,16,128]{2,1,0:T(8,128)S(1)} all-to-all(f32[64,16,128]{2,1,0:T(8,128)S(1)} %bitcast.11), channel_id=1, replica_groups=mesh['seq'=64,'tp'=4] {'seq'}, dimensions={0} | all-to-all | bytes 1048576 | tf_op jit(solution)/shard_map/all_to_all | solution.py:350
  134.0 1.2 shard_map.95
  (6 shorter events, 0.0 us)
Async XLA Ops:
  0.0 1.0 copy-start.2
  1.0 1.0 copy-start.3
  2.1 75.1 %copy-start.4 = (bf16[768,256]{1,0:T(8,128)(2,1)S(1)}, bf16[768,256]{1,0:T(8,128)(2,1)}, u32[]{:S(2)}) copy-start(bf16[768,256]{1,0:T(8,128)(2,1)} %constant.127.clone.refs_9_) | copy-start | bytes 1179652
  2.1 75.1 %copy-start.5 = (bf16[768,256]{1,0:T(8,128)(2,1)S(1)}, bf16[768,256]{1,0:T(8,128)(2,1)}, u32[]{:S(2)}) copy-start(bf16[768,256]{1,0:T(8,128)(2,1)} %constant.126.clone.refs_8_) | copy-start | bytes 1179652
  2.1 75.1 %copy-start.6 = (f32[32,2,8,128]{3,2,1,0:T(8,128)S(1)}, f32[32,2,8,128]{3,2,1,0:T(8,128)}, u32[]{:S(2)}) copy-start(f32[32,2,8,128]{3,2,1,0:T(8,128)} %constant.128.clone.refs_10_) | copy-start | bytes 786436
  3.4 106.0 %copy-start = (bf16[256,1536]{1,0:T(8,128)(2,1)S(1)}, bf16[256,1536]{1,0:T(8,128)(2,1)}, u32[]{:S(2)}) copy-start(bf16[256,1536]{1,0:T(8,128)(2,1)} %constant.129.clone.refs_8_) | copy-start | bytes 2359300
  3.4 48.1 %all-to-all-start = ((f32[256,8,128]{2,1,0:T(8,128)}), f32[256,8,128]{2,1,0:T(8,128)S(1)}, u32[]{:S(2)}, u32[]{:S(2)}) async-start(f32[256,8,128]{2,1,0:T(8,128)} %shard_map.91), calls=%async_computation | async-start | bytes 2097152 | tf_op jit(solution)/shard_map/all_to_all | solution.py:343
  51.6 1.1 copy-start.1
  55.9 7.7 %collective-permute-start = (f32[2,2,4,32,128]{4,3,2,1,0:T(8,128)S(1)}, f32[2,2,4,32,128]{4,3,2,1,0:T(8,128)S(1)}, u32[]{:S(2)}, u32[]{:S(2)}) collective-permute-start(f32[2,2,4,32,128]{4,3,2,1,0:T(8,128)S(1)} %get-tuple-element.22), channel_id=1, source_target_pairs={{0,1},{1,0},{8,9},{9,8},{64,65},{65,64},{72,73},{73,72},{16,17},{1... | collective-permute-start | bytes 786440 | tf_op jit(solution)/shard_map/ppermute | solution.py:346
  56.0 8.7 %collective-permute-start.1 = (f32[2,2,4,32,128]{4,3,2,1,0:T(8,128)S(1)}, f32[2,2,4,32,128]{4,3,2,1,0:T(8,128)S(1)}, u32[]{:S(2)}, u32[]{:S(2)}) collective-permute-start(f32[2,2,4,32,128]{4,3,2,1,0:T(8,128)S(1)} %get-tuple-element.23), channel_id=1, source_target_pairs={{0,8},{1,9},{8,0},{9,1},{64,72},{65,73},{72,64},{73,65},{16,24},{1... | collective-permute-start | bytes 786440 | tf_op jit(solution)/shard_map/ppermute | solution.py:346
  56.5 14.2 %collective-permute-start.2 = (f32[2,2,4,32,128]{4,3,2,1,0:T(8,128)S(1)}, f32[2,2,4,32,128]{4,3,2,1,0:T(8,128)S(1)}, u32[]{:S(2)}, u32[]{:S(2)}) collective-permute-start(f32[2,2,4,32,128]{4,3,2,1,0:T(8,128)S(1)} %get-tuple-element.24), channel_id=1, source_target_pairs={{0,9},{1,8},{8,1},{9,0},{64,73},{65,72},{72,65},{73,64},{16,25},{1... | collective-permute-start | bytes 786440 | tf_op jit(solution)/shard_map/ppermute | solution.py:346
  61.0 9.6 %collective-permute-start.3 = (f32[2,2,4,32,128]{4,3,2,1,0:T(8,128)S(1)}, f32[2,2,4,32,128]{4,3,2,1,0:T(8,128)S(1)}, u32[]{:S(2)}, u32[]{:S(2)}) collective-permute-start(f32[2,2,4,32,128]{4,3,2,1,0:T(8,128)S(1)} %get-tuple-element.25), channel_id=1, source_target_pairs={{0,64},{1,65},{8,72},{9,73},{64,0},{65,1},{72,8},{73,9},{16,80},{1... | collective-permute-start | bytes 786440 | tf_op jit(solution)/shard_map/ppermute | solution.py:346
  61.5 10.4 %collective-permute-start.4 = (f32[2,2,4,32,128]{4,3,2,1,0:T(8,128)S(1)}, f32[2,2,4,32,128]{4,3,2,1,0:T(8,128)S(1)}, u32[]{:S(2)}, u32[]{:S(2)}) collective-permute-start(f32[2,2,4,32,128]{4,3,2,1,0:T(8,128)S(1)} %get-tuple-element.26), channel_id=1, source_target_pairs={{0,65},{1,64},{8,73},{9,72},{64,1},{65,0},{72,9},{73,8},{16,81},{1... | collective-permute-start | bytes 786440 | tf_op jit(solution)/shard_map/ppermute | solution.py:346
  63.5 9.9 %collective-permute-start.5 = (f32[2,2,4,32,128]{4,3,2,1,0:T(8,128)S(1)}, f32[2,2,4,32,128]{4,3,2,1,0:T(8,128)S(1)}, u32[]{:S(2)}, u32[]{:S(2)}) collective-permute-start(f32[2,2,4,32,128]{4,3,2,1,0:T(8,128)S(1)} %get-tuple-element.27), channel_id=1, source_target_pairs={{0,72},{1,73},{8,64},{9,65},{64,8},{65,9},{72,0},{73,1},{16,88},{1... | collective-permute-start | bytes 786440 | tf_op jit(solution)/shard_map/ppermute | solution.py:346
  64.7 12.5 %collective-permute-start.6 = (f32[2,2,4,32,128]{4,3,2,1,0:T(8,128)S(1)}, f32[2,2,4,32,128]{4,3,2,1,0:T(8,128)S(1)}, u32[]{:S(2)}, u32[]{:S(2)}) collective-permute-start(f32[2,2,4,32,128]{4,3,2,1,0:T(8,128)S(1)} %get-tuple-element.28), channel_id=1, source_target_pairs={{0,73},{1,72},{8,65},{9,64},{64,9},{65,8},{72,1},{73,0},{16,89},{1... | collective-permute-start | bytes 786440 | tf_op jit(solution)/shard_map/ppermute | solution.py:346
  81.5 6.6 %collective-permute-start.7 = (f32[2,4,32,128]{3,2,1,0:T(8,128)S(1)}, f32[2,4,32,128]{3,2,1,0:T(8,128)S(1)}, u32[]{:S(2)}, u32[]{:S(2)}) collective-permute-start(f32[2,4,32,128]{3,2,1,0:T(8,128)S(1)} %get-tuple-element.29), channel_id=1, source_target_pairs={{0,0},{1,4},{8,8},{9,12},{64,64},{65,68},{72,72},{73,76},{16,16},{... | collective-permute-start | bytes 393224 | tf_op jit(solution)/shard_map/ppermute | solution.py:348
  83.4 8.5 %collective-permute-start.8 = (f32[2,4,32,128]{3,2,1,0:T(8,128)S(1)}, f32[2,4,32,128]{3,2,1,0:T(8,128)S(1)}, u32[]{:S(2)}, u32[]{:S(2)}) collective-permute-start(f32[2,4,32,128]{3,2,1,0:T(8,128)S(1)} %get-tuple-element.30), channel_id=1, source_target_pairs={{0,4},{1,0},{8,12},{9,8},{64,68},{65,64},{72,76},{73,72},{16,20},{... | collective-permute-start | bytes 393224 | tf_op jit(solution)/shard_map/ppermute | solution.py:348
  87.6 16.5 %collective-permute-start.9 = (f32[2,4,32,128]{3,2,1,0:T(8,128)S(1)}, f32[2,4,32,128]{3,2,1,0:T(8,128)S(1)}, u32[]{:S(2)}, u32[]{:S(2)}) collective-permute-start(f32[2,4,32,128]{3,2,1,0:T(8,128)S(1)} %get-tuple-element.31), channel_id=1, source_target_pairs={{0,8},{1,12},{8,0},{9,4},{64,72},{65,76},{72,64},{73,68},{16,24},{... | collective-permute-start | bytes 393224 | tf_op jit(solution)/shard_map/ppermute | solution.py:348
  87.6 17.2 %collective-permute-start.10 = (f32[2,4,32,128]{3,2,1,0:T(8,128)S(1)}, f32[2,4,32,128]{3,2,1,0:T(8,128)S(1)}, u32[]{:S(2)}, u32[]{:S(2)}) collective-permute-start(f32[2,4,32,128]{3,2,1,0:T(8,128)S(1)} %get-tuple-element.32), channel_id=1, source_target_pairs={{0,12},{1,8},{8,4},{9,0},{64,76},{65,72},{72,68},{73,64},{16,28},{... | collective-permute-start | bytes 393224 | tf_op jit(solution)/shard_map/ppermute | solution.py:348
  87.6 17.2 %collective-permute-start.11 = (f32[2,4,32,128]{3,2,1,0:T(8,128)S(1)}, f32[2,4,32,128]{3,2,1,0:T(8,128)S(1)}, u32[]{:S(2)}, u32[]{:S(2)}) collective-permute-start(f32[2,4,32,128]{3,2,1,0:T(8,128)S(1)} %get-tuple-element.33), channel_id=1, source_target_pairs={{0,64},{1,68},{8,72},{9,76},{64,0},{65,4},{72,8},{73,12},{16,80},{... | collective-permute-start | bytes 393224 | tf_op jit(solution)/shard_map/ppermute | solution.py:348
  88.0 16.8 %collective-permute-start.12 = (f32[2,4,32,128]{3,2,1,0:T(8,128)S(1)}, f32[2,4,32,128]{3,2,1,0:T(8,128)S(1)}, u32[]{:S(2)}, u32[]{:S(2)}) collective-permute-start(f32[2,4,32,128]{3,2,1,0:T(8,128)S(1)} %get-tuple-element.34), channel_id=1, source_target_pairs={{0,68},{1,64},{8,76},{9,72},{64,4},{65,0},{72,12},{73,8},{16,84},{... | collective-permute-start | bytes 393224 | tf_op jit(solution)/shard_map/ppermute | solution.py:348
  91.9 14.0 %collective-permute-start.13 = (f32[2,4,32,128]{3,2,1,0:T(8,128)S(1)}, f32[2,4,32,128]{3,2,1,0:T(8,128)S(1)}, u32[]{:S(2)}, u32[]{:S(2)}) collective-permute-start(f32[2,4,32,128]{3,2,1,0:T(8,128)S(1)} %get-tuple-element.35), channel_id=1, source_target_pairs={{0,72},{1,76},{8,64},{9,68},{64,8},{65,12},{72,0},{73,4},{16,88},{... | collective-permute-start | bytes 393224 | tf_op jit(solution)/shard_map/ppermute | solution.py:348
  104.0 5.4 %collective-permute-start.14 = (f32[2,4,32,128]{3,2,1,0:T(8,128)S(1)}, f32[2,4,32,128]{3,2,1,0:T(8,128)S(1)}, u32[]{:S(2)}, u32[]{:S(2)}) collective-permute-start(f32[2,4,32,128]{3,2,1,0:T(8,128)S(1)} %get-tuple-element.36), channel_id=1, source_target_pairs={{0,76},{1,72},{8,68},{9,64},{64,12},{65,8},{72,4},{73,0},{16,92},{... | collective-permute-start | bytes 393224 | tf_op jit(solution)/shard_map/ppermute | solution.py:348

commit v2 on v1

v2 whole, which is shorter than its diff:
```python
import functools
import math

import jax
import jax.numpy as jnp
import ml_dtypes
import numpy as np
from jax import lax
from jax.experimental import pallas as pl
from jax.experimental.pallas import tpu as pltpu
from jax.sharding import PartitionSpec as P

LENGTH = 1 << 20
BLOCKS = 256
LANES = 128
AXES = ("seq", "tp")
FLIPS = (7, 6, 5, 3, 4, 2, 1, 0)
VMEM = pl.BlockSpec(memory_space=pltpu.VMEM)
HBM = pl.BlockSpec(memory_space=pltpu.HBM)
SMEM = pl.BlockSpec(memory_space=pltpu.SMEM)
PARAMS = pltpu.CompilerParams(vmem_limit_bytes=48 * 1024 * 1024)


def device(y, z, core, x):
    return (((y % 4) * 8 + z % 8) * 2 + core) * 4 + x % 4


def member(slab, row, g):
    core = slab % 2
    y = 2 * (row // 4) + core + (g >> 2)
    z = 2 * (row % 4) + core + ((g >> 1) & 1)
    return device(y, z, core, slab + (g & 1))


def keeper(slab, row, o):
    odd = slab % 2
    return device(2 * (row // 4) + odd + (o >> 2), 2 * (row % 4) + odd + ((o >> 1) & 1), o & 1, slab)


GROUPS = [(slab, row) for slab in range(4) for row in range(8)]


def among_members(flip):
    return [(member(s, r, g), member(s, r, g ^ flip)) for s, r in GROUPS for g in range(8)]


def to_keepers(flip):
    return [(member(s, r, g), keeper(s, r, first_range(s % 2, g) ^ flip)) for s, r in GROUPS for g in range(8)]


def first_range(core, g):
    return (g & 6) | ((g & 1) ^ core)


def halves(x):
    high = x.astype(ml_dtypes.bfloat16)
    low = (x - high.astype(np.float64)).astype(ml_dtypes.bfloat16)
    return high, low


@functools.cache
def tables():
    j = np.arange(BLOCKS)[:, None]
    k = np.arange(BLOCKS)[None, :] + 0.25
    angle = 2.0 * math.pi * ((j * k) % BLOCKS) / BLOCKS
    cos, sin = np.cos(angle), np.sin(angle)
    ahead_high, ahead_low = halves(np.concatenate([cos.T, -sin.T], axis=0))
    back_high, back_low = halves(np.concatenate([cos, -sin], axis=1) / LENGTH)
    t = np.arange(4096)[:, None]
    angle = (2.0 * math.pi / LENGTH) * (t * k)
    turn = np.stack([np.cos(angle), -np.sin(angle)])
    turn = turn.reshape(2, 8, 512, BLOCKS).transpose(1, 0, 3, 2).astype(np.float32)
    b = np.arange(LANES)
    angle = 2.0 * math.pi * ((b[:, None] * b[None, :]) % LANES) / LANES
    cos, sin = np.cos(angle), np.sin(angle)
    lane_high, lane_low = halves(np.block([[cos, -sin], [sin, cos]]))
    unlane_high, unlane_low = halves(np.block([[cos, sin], [-sin, cos]]))
    angle = (2.0 * math.pi / 4096) * (np.arange(32)[:, None] * b[None, :])
    twist = np.stack([np.cos(angle), -np.sin(angle)], axis=1)
    return dict(
        ahead=np.concatenate([ahead_high, ahead_low], axis=1),
        back=np.concatenate([back_high, back_low], axis=1),
        turn=turn,
        lane=np.concatenate([lane_high, lane_low], axis=1),
        unlane=np.concatenate([unlane_high, unlane_low], axis=1),
        twist=twist.astype(np.float32).reshape(64, LANES),
    )


def split(x):
    high = x.astype(jnp.bfloat16)
    return high, (x - high.astype(jnp.float32)).astype(jnp.bfloat16)


def dot(a, b):
    return lax.dot_general(a, b, (((1,), (0,)), ((), ())), preferred_element_type=jnp.float32)


def three(a_high, a_low, b_high, b_low):
    return dot(a_high, b_high) + (dot(a_high, b_low) + dot(a_low, b_high))


def times(re, im, factor):
    c, s = factor.real, factor.imag
    if abs(s) < 1e-12:
        return (re, im) if c > 0 else (-re, -im)
    if abs(c) < 1e-12:
        return (-im, re) if s > 0 else (im, -re)
    if abs(abs(c) - abs(s)) < 1e-12:
        p, q = np.sign(c), np.sign(s)
        first = re - im if p == q else re + im
        second = im + re if p == q else im - re
        return first * np.float32(c), second * np.float32(c)
    c, s = np.float32(c), np.float32(s)
    return re * c - im * s, re * s + im * c


def fourier(values, sign):
    size = len(values)
    if size == 1:
        return values
    even, odd = fourier(values[0::2], sign), fourier(values[1::2], sign)
    first, second = [], []
    for i in range(size // 2):
        angle = sign * 2.0 * math.pi * i / size
        re, im = times(*odd[i], complex(math.cos(angle), math.sin(angle)))
        first.append((even[i][0] + re, even[i][1] + im))
        second.append((even[i][0] - re, even[i][1] - im))
    return first + second


def unit(sign, numerator, denominator):
    angle = sign * 2.0 * math.pi * numerator / denominator
    return complex(math.cos(angle), math.sin(angle))


def pack_kernel(signal_ref, taps_ref, out_ref, rows_ref, sems):
    def load(at, ref, slab):
        rows = pl.ds(256 * slab, 256)
        return pltpu.make_async_copy(ref.at[rows, :], rows_ref.at[at, rows, :], sems.at[at, slab])

    copies = [[load(at, ref, slab) for slab in range(4)] for at, ref in enumerate((signal_ref, taps_ref))]
    for slab in range(4):
        for at in range(2):
            copies[at][slab].start()
    for slab in range(4):
        for at in range(2):
            copies[at][slab].wait()
        for row in range(8):
            for g in range(8):
                to = member(slab, row, g)
                for at in range(2):
                    start = (slab * 32 + 4 * g) * 8 + row
                    out_ref[to, pl.ds(4 * at, 4), :] = rows_ref[at, pl.ds(start, 4, stride=8), :]


def tiles(x):
    return x.reshape(4, 8, 32, LANES).swapaxes(1, 2).reshape(1024, LANES)


def pack(signal, taps):
    return pl.pallas_call(
        pack_kernel,
        out_shape=jax.ShapeDtypeStruct((256, 8, LANES), jnp.float32),
        in_specs=[HBM, HBM],
        out_specs=VMEM,
        scratch_shapes=[pltpu.VMEM((2, 1024, LANES), jnp.float32), pltpu.SemaphoreType.DMA((2, 4))],
        compiler_params=pltpu.CompilerParams(vmem_limit_bytes=60 * 1024 * 1024),
    )(tiles(signal), tiles(taps))


def turn_copies(turn_ref, at, to_ref, sems):
    parts = [(i, pl.ds(128 * h, 128)) for i in range(2) for h in range(2)]
    return [
        pltpu.make_async_copy(turn_ref.at[at, i, rows], to_ref.at[i, rows], sems.at[n])
        for n, (i, rows) in enumerate(parts)
    ]


def ahead_kernel(place_ref, gain_ref, x_ref, ahead_ref, turn_ref, *rest):
    outs, (angle_ref, x2_ref, y_ref, sems) = rest[:8], rest[8:]
    g = place_ref[0]
    copies = turn_copies(turn_ref, g, angle_ref, sems)
    for copy in copies:
        copy.start()
    for s in range(8):
        x = x_ref[pl.ds(s, 256, stride=8), :]
        if s == 4:
            row = lax.broadcasted_iota(jnp.int32, x.shape, 0)
            lane = lax.broadcasted_iota(jnp.int32, x.shape, 1)
            x = x + jnp.where((row == 0) & (lane == 0), gain_ref[0], 0.0)
        high, low = split(x)
        x2_ref[pl.ds(0, 256), pl.ds(128 * s, 128)] = high
        x2_ref[pl.ds(256, 256), pl.ds(128 * s, 128)] = low
    for n in range(4):
        cols = pl.ds(256 * n, 256)
        y_ref[:, cols] = three(ahead_ref[:, :256], ahead_ref[:, 256:], x2_ref[:256, cols], x2_ref[256:, cols])
    for copy in copies:
        copy.wait()
    for i, flip in enumerate(FLIPS):
        to = pl.multiple_of((g ^ flip) * 32, 32)
        for a in range(4):
            tr = angle_ref[0, pl.ds(to, 32), pl.ds(128 * a, 128)]
            ti = angle_ref[1, pl.ds(to, 32), pl.ds(128 * a, 128)]
            for sf in range(2):
                cols = pl.ds(512 * sf + 128 * a, 128)
                re, im = y_ref[pl.ds(to, 32), cols], y_ref[pl.ds(256 + to, 32), cols]
                outs[i][0, sf, a] = re * tr - im * ti
                outs[i][1, sf, a] = re * ti + im * tr


def ahead(place, gain, x, table, turn):
    block = (2, 2, 4, 32, LANES)
    return pl.pallas_call(
        ahead_kernel,
        out_shape=[jax.ShapeDtypeStruct(block, jnp.float32)] * 8,
        in_specs=[SMEM, SMEM, VMEM, VMEM, HBM],
        out_specs=[VMEM] * 8,
        scratch_shapes=[
            pltpu.VMEM((2, 256, 512), jnp.float32),
            pltpu.VMEM((512, 1024), jnp.bfloat16),
            pltpu.VMEM((512, 1024), jnp.float32),
            pltpu.SemaphoreType.DMA((4,)),
        ],
        compiler_params=PARAMS,
    )(place, gain, x, table, turn)


def middle_kernel(place_ref, *refs):
    ins, (lane_ref, unlane_ref, twist_ref, turn_ref) = refs[:8], refs[8:12]
    outs, angle_ref, (x_ref, m_ref, d_ref, y_ref, sems) = refs[12:20], refs[20], refs[21:]
    g, o = place_ref[0], place_ref[1]
    copies = turn_copies(turn_ref, place_ref[3], angle_ref, sems)
    for copy in copies:
        copy.start()
    for i, flip in enumerate(FLIPS):
        x_ref[g ^ flip] = ins[i][...]

    def step(kb, carry):
        rows = pl.ds(pl.multiple_of(kb * 8, 8), 8)
        for sf in range(2):
            for a in range(4):
                values = [(x_ref[s, 0, sf, a, rows, :], x_ref[s, 1, sf, a, rows, :]) for s in range(8)]
                for m1, value in enumerate(fourier(values, -1)):
                    re, im = times(*value, unit(-1, a * m1, 32))
                    m_ref[m1, a, 0], m_ref[m1, a, 1] = re, im
            for m1 in range(8):
                values = fourier([(m_ref[m1, a, 0], m_ref[m1, a, 1]) for a in range(4)], -1)
                for m2, (re, im) in enumerate(values):
                    m = m1 + 8 * m2
                    tr, ti = twist_ref[2 * m : 2 * m + 1, :], twist_ref[2 * m + 1 : 2 * m + 2, :]
                    d_ref[pl.ds(256 * sf + 8 * m, 8), :128] = re * tr - im * ti
                    d_ref[pl.ds(256 * sf + 8 * m, 8), 128:] = re * ti + im * tr
        high, low = split(d_ref[...])
        d = three(high, low, lane_ref[:, :256], lane_ref[:, 256:])
        sr, si, fr, fi = d[:256, :128], d[:256, 128:], d[256:, :128], d[256:, 128:]
        high, low = split(jnp.concatenate([sr * fr - si * fi, sr * fi + si * fr], axis=1))
        d_ref[pl.ds(0, 256), :] = three(high, low, unlane_ref[:, :256], unlane_ref[:, 256:])
        for m1 in range(8):
            values = []
            for m2 in range(4):
                m = m1 + 8 * m2
                tr, ti = twist_ref[2 * m : 2 * m + 1, :], twist_ref[2 * m + 1 : 2 * m + 2, :]
                re, im = d_ref[pl.ds(8 * m, 8), :128], d_ref[pl.ds(8 * m, 8), 128:]
                values.append((re * tr + im * ti, im * tr - re * ti))
            for a, value in enumerate(fourier(values, 1)):
                re, im = times(*value, unit(1, a * m1, 32))
                m_ref[m1, a, 0], m_ref[m1, a, 1] = re, im
        for a in range(4):
            values = fourier([(m_ref[m1, a, 0], m_ref[m1, a, 1]) for m1 in range(8)], 1)
            for at, (re, im) in enumerate(values):
                y_ref[at, 0, a, rows, :], y_ref[at, 1, a, rows, :] = re, im
        return carry

    lax.fori_loop(0, 4, step, 0)
    for i, flip in enumerate(FLIPS):
        outs[i][...] = y_ref[o ^ flip]
    for copy in copies:
        copy.wait()


def middle(place, blocks, lane, unlane, twist, turn):
    block = (2, 4, 32, LANES)
    return pl.pallas_call(
        middle_kernel,
        out_shape=[jax.ShapeDtypeStruct(block, jnp.float32)] * 8
        + [jax.ShapeDtypeStruct((2, 256, 512), jnp.float32)],
        in_specs=[SMEM] + [VMEM] * 11 + [HBM],
        out_specs=[VMEM] * 9,
        scratch_shapes=[
            pltpu.VMEM((8, 2, 2, 4, 32, LANES), jnp.float32),
            pltpu.VMEM((8, 4, 2, 8, LANES), jnp.float32),
            pltpu.VMEM((512, 256), jnp.float32),
            pltpu.VMEM((8, 2, 4, 32, LANES), jnp.float32),
            pltpu.SemaphoreType.DMA((4,)),
        ],
        compiler_params=PARAMS,
    )(place, *blocks, lane, unlane, twist, turn)


def back_kernel(place_ref, *refs):
    ins, (back_ref, turn_ref), out_ref, (y2_ref,) = refs[:8], refs[8:10], refs[10], refs[11:]
    g = place_ref[2]
    for i, flip in enumerate(FLIPS):
        at = pl.multiple_of((g ^ flip) * 32, 32)
        for a in range(4):
            cols = pl.ds(128 * a, 128)
            tr, ti = turn_ref[0, pl.ds(at, 32), cols], turn_ref[1, pl.ds(at, 32), cols]
            re, im = ins[i][0, a], ins[i][1, a]
            for part, value in enumerate((re * tr + im * ti, im * tr - re * ti)):
                high, low = split(value)
                y2_ref[pl.ds(256 * part + at, 32), cols] = high
                y2_ref[pl.ds(512 + 256 * part + at, 32), cols] = low
    for n in range(2):
        cols = pl.ds(256 * n, 256)
        y = three(back_ref[:, :512], back_ref[:, 512:], y2_ref[:512, cols], y2_ref[512:, cols])
        for a in range(2):
            out_ref[pl.ds(2 * n + a, 256, stride=4), :] = y[:, 128 * a : 128 * (a + 1)]


def back(place, blocks, table, turn):
    return pl.pallas_call(
        back_kernel,
        out_shape=jax.ShapeDtypeStruct((1024, LANES), jnp.float32),
        in_specs=[SMEM] + [VMEM] * 10,
        out_specs=VMEM,
        scratch_shapes=[pltpu.VMEM((1024, 512), jnp.bfloat16)],
        compiler_params=PARAMS,
    )(place, *blocks, table, turn)


def unpack_kernel(place_ref, x_ref, out_ref, rows_ref):
    odd = place_ref[4]
    for y in range(4):
        for z in range(8):
            start = pl.multiple_of((((y + odd) & 3) * 8 + ((z + odd) & 7)) * 32, 32)
            rows_ref[pl.ds((y * 8 + z) * 32, 32), :] = x_ref[pl.ds(start, 32), :]
    for jl in range(4):
        for o in range(8):
            for a in range(4):
                start = (16 * (o >> 2) + 2 * ((o >> 1) & 1) + (o & 1)) * 16 + jl * 4 + a
                cols = pl.ds(128 * (jl * 32 + 4 * o + a), 128)
                for half in range(2):
                    out_ref[pl.ds(4 * half, 4), cols] = rows_ref[pl.ds(start + 512 * half, 4, stride=64), :]


def unpack(place, x):
    return pl.pallas_call(
        unpack_kernel,
        out_shape=jax.ShapeDtypeStruct((8, 16384), jnp.float32),
        in_specs=[SMEM, VMEM],
        out_specs=VMEM,
        scratch_shapes=[pltpu.VMEM((1024, LANES), jnp.float32)],
        compiler_params=PARAMS,
    )(place, x)


def exchange(parts, pairs, count):
    moved = [lax.ppermute(part, AXES, pairs(flip)) for part, flip in zip(parts[:count], FLIPS)]
    return moved + list(parts[count:])


def body(signal, filter_taps, skip_gain):
    known = tables()
    seq, x = lax.axis_index("seq"), lax.axis_index("tp")
    y, z, core = seq // 16, (seq // 2) % 8, seq % 2
    dy, dz, dx = (y - core) % 2, (z - core) % 2, (x - core) % 2
    g = 4 * dy + 2 * dz + dx
    row = ((y - core) % 4) // 2 * 4 + ((z - core) % 8) // 2
    first = 4 * dy + 2 * dz + (dx ^ core)
    odd = x % 2
    o = 4 * ((y - odd) % 2) + 2 * ((z - odd) % 2) + core
    place = jnp.stack([g, first, o ^ odd, o, odd]).astype(jnp.int32)
    gain = jnp.where(g == 0, skip_gain[row], 0.0).reshape(1)

    packed = pack(signal, filter_taps)
    tokens = lax.all_to_all(packed, AXES, split_axis=0, concat_axis=0, tiled=True)
    names = ("turn", "ahead", "lane", "unlane", "twist", "back")
    turn, table, lane, unlane, twist, untable = (jnp.asarray(known[name]) for name in names)
    parts = ahead(place, gain, tokens.reshape(2048, LANES), table, turn)
    parts = exchange(parts, among_members, 7)
    *parts, turn = middle(place, parts, lane, unlane, twist, turn)
    parts = exchange(parts, to_keepers, 8)
    result = back(place, parts, untable, turn)
    result = lax.all_to_all(result.reshape(64, 16, LANES), "seq", split_axis=0, concat_axis=0, tiled=True)
    return unpack(place, result.reshape(1024, LANES))


def solution(mesh):
    placed = (P(None, ("seq", "tp")), P(None, ("seq", "tp")), P("tp"))
    return jax.shard_map(
        body, mesh=mesh, in_specs=placed, out_specs=P("tp", "seq"), check_vma=False
    )
```

time: 137 us -> 124 us (0.905); the launches traced: 135 us -> 124 us
  starting transfers between devices: 53.6 us -> 39 us
  waiting for transfers between devices: 41.6 us -> 47.5 us
  local copies, waits for them, and re-layouts: 4.47 us -> 2.41 us
    ppermute x15, starting transfers between devices: 37.9 us -> 23.3 us  [exchange(): lax.ppermute(part, AXES, pairs(flip))]
    ppermute x15, waiting for transfers between devices: 11.3 us -> 17.3 us  [exchange(): lax.ppermute(part, AXES, pairs(flip))]
    unnamed x14 -> x10, local copies, waits for them, and re-layouts: 3.23 us -> 1.06 us
  transfers between devices with their start and end apart: 16 -> 16, of which waited for: 7 -> 10; matrix products, arithmetic and copies ran while one was open for 1% -> 1% of each run, Pallas kernels for 0% -> 0%
where the time goes in v2:
time: 124 us
  waiting for transfers between devices  47.5 us (38%)
  starting transfers between devices  39 us (31%)
  blocking collectives  21.2 us (17%)
  Pallas kernels  12.7 us (10%)
  local copies, waits for them, and re-layouts  2.41 us (2%)
    all_to_all x1, waiting for transfers between devices, body(): lax.all_to_all(packed, AXES, split_axis=0, concat_axis=0, tiled=True)  30.2 us
    ppermute x15, starting transfers between devices, exchange(): lax.ppermute(part, AXES, pairs(flip))  23.3 us
    all_to_all x1, blocking collectives, body(): lax.all_to_all(result.reshape(64, 16, LANES), 'seq', split_axis=0, concat...  21.2 us
    ppermute x15, waiting for transfers between devices, exchange(): lax.ppermute(part, AXES, pairs(flip))  17.3 us
    all_to_all x1, starting transfers between devices, body(): lax.all_to_all(packed, AXES, split_axis=0, concat_axis=0, tiled=True)  15.7 us
    pallas_call x1, Pallas kernels, middle(): pl.pallas_call(middle_kernel, out_shape=[jax.ShapeDtypeStruct(block, jnp....  4.31 us
    pallas_call x1, Pallas kernels, ahead(): pl.pallas_call(ahead_kernel, out_shape=[jax.ShapeDtypeStruct(block, jnp.f...  2.81 us
  transfers between devices with their start and end apart: 16, of which 10 were waited for; matrix products, arithmetic and copies ran while one was open for 1% of the time, Pallas kernels for 0%

profile of v2, /device:TPU:1, one launch (start us, length us, event | category | flops | bytes accessed | tf_op | source)
XLA Modules:
  0.0 123.7 jit_solution(17664850920707226776)
XLA Ops:
  0.0 0.0 copy-start.4
  0.0 0.0 copy-start.2
  0.0 0.0 copy-start.3
  0.0 2.5 %shard_map.91 = f32[256,8,128]{2,1,0:T(8,128)} custom-call(f32[1024,128]{1,0:T(8,128)} %bitcast.23, f32[1024,128]{1,0:T(8,128)} %bitcast.24), custom_call_target="tpu_custom_call" | custom-call | tf_op jit(solution)/shard_map/pallas_call | solution.py:162
  2.5 15.7 %all-to-all-start = ((f32[256,8,128]{2,1,0:T(8,128)}), f32[256,8,128]{2,1,0:T(8,128)S(1)}, u32[]{:S(2)}, u32[]{:S(2)}) async-start(f32[256,8,128]{2,1,0:T(8,128)} %shard_map.91), calls=%async_computation | async-start | bytes 2097152 | tf_op jit(solution)/shard_map/all_to_all | solution.py:377
  18.4 1.3 %dynamic_slice.3 = f32[1]{0:T(128)} dynamic-slice(f32[8]{0:T(128)} %param.11, s32[]{:T(128)S(6)} %select_n.77), dynamic_slice_sizes={1} | dynamic-slice | bytes 12 | tf_op jit(solution)/shard_map/dynamic_slice | solution.py:374
  20.3 0.1 stack.23.place_ref
  20.4 30.2 %all-to-all-done = f32[256,8,128]{2,1,0:T(8,128)S(1)} async-done(((f32[256,8,128]{2,1,0:T(8,128)}), f32[256,8,128]{2,1,0:T(8,128)S(1)}, u32[]{:S(2)}, u32[]{:S(2)}) %all-to-all-start) | async-done | bytes 1048608 | tf_op jit(solution)/shard_map/all_to_all | solution.py:377
  50.6 1.0 copy-done
  51.6 2.8 %shard_map.92 = (f32[2,2,4,32,128]{4,3,2,1,0:T(8,128)S(1)}, f32[2,2,4,32,128]{4,3,2,1,0:T(8,128)S(1)}, f32[2,2,4,32,128]{4,3,2,1,0:T(8,128)S(1)}, f32[2,2,4,32,1...) custom-call(s32[5]{0:T(128)S(1)} %stack.23.place_ref, ...), custom_call_target="tpu_custom_call" | custom-call | tf_op jit(solution)/shard_map/pallas_call | solution.py:214
  54.5 1.1 collective-permute-start
  55.5 3.5 %collective-permute-start.1 = (f32[2,2,4,32,128]{4,3,2,1,0:T(8,128)S(1)}, f32[2,2,4,32,128]{4,3,2,1,0:T(8,128)S(1)}, u32[]{:S(2)}, u32[]{:S(2)}) collective-permute-start(f32[2,2,4,32,128]{4,3,2,1,0:T(8,128)S(1)} %get-tuple-element.23), channel_id=1, source_target_pairs={{0,72},{1,73},{8,64},{9,65},{64,8},{65,9},{72,0},{73,1},{16,88},{1... | collective-permute-start | bytes 786440 | tf_op jit(solution)/shard_map/ppermute | solution.py:359
  59.1 2.9 %collective-permute-start.2 = (f32[2,2,4,32,128]{4,3,2,1,0:T(8,128)S(1)}, f32[2,2,4,32,128]{4,3,2,1,0:T(8,128)S(1)}, u32[]{:S(2)}, u32[]{:S(2)}) collective-permute-start(f32[2,2,4,32,128]{4,3,2,1,0:T(8,128)S(1)} %get-tuple-element.24), channel_id=1, source_target_pairs={{0,65},{1,64},{8,73},{9,72},{64,1},{65,0},{72,9},{73,8},{16,81},{1... | collective-permute-start | bytes 786440 | tf_op jit(solution)/shard_map/ppermute | solution.py:359
  62.0 0.8 collective-permute-start.3
  62.7 1.6 %collective-permute-start.4 = (f32[2,2,4,32,128]{4,3,2,1,0:T(8,128)S(1)}, f32[2,2,4,32,128]{4,3,2,1,0:T(8,128)S(1)}, u32[]{:S(2)}, u32[]{:S(2)}) collective-permute-start(f32[2,2,4,32,128]{4,3,2,1,0:T(8,128)S(1)} %get-tuple-element.26), channel_id=1, source_target_pairs={{0,64},{1,65},{8,72},{9,73},{64,0},{65,1},{72,8},{73,9},{16,80},{1... | collective-permute-start | bytes 786440 | tf_op jit(solution)/shard_map/ppermute | solution.py:359
  64.3 3.4 %collective-permute-done.refs_0_ = f32[2,2,4,32,128]{4,3,2,1,0:T(8,128)S(1)} collective-permute-done((f32[2,2,4,32,128]{4,3,2,1,0:T(8,128)S(1)}, f32[2,2,4,32,128]{4,3,2,1,0:T(8,128)S(1)}, u32[]{:S(2)}, u32[]{:S(2)}) %collective-permute-start) | collective-permute-done | bytes 262176 | tf_op jit(solution)/shard_map/ppermute | solution.py:359
  67.8 0.0 collective-permute-start.5
  67.8 0.8 collective-permute-done.1.refs_1_
  68.5 0.7 collective-permute-start.6
  69.2 4.0 %collective-permute-done.2.refs_2_ = f32[2,2,4,32,128]{4,3,2,1,0:T(8,128)S(1)} collective-permute-done((f32[2,2,4,32,128]{4,3,2,1,0:T(8,128)S(1)}, f32[2,2,4,32,128]{4,3,2,1,0:T(8,128)S(1)}, u32[]{:S(2)}, u32[]{:S(2)}) %collective-permute-start.2) | collective-permute-done | bytes 262176 | tf_op jit(solution)/shard_map/ppermute | solution.py:359
  73.2 0.0 collective-permute-done.3.refs_3_
  73.2 0.4 collective-permute-done.4.refs_4_
  73.6 0.6 collective-permute-done.5.refs_5_
  74.2 0.8 collective-permute-done.6.refs_6_
  75.0 0.0 copy-done.4
  75.0 0.0 copy-done.2
  75.0 0.0 copy-done.3
  75.0 4.3 %shard_map.93 = (f32[2,4,32,128]{3,2,1,0:T(8,128)S(1)}, f32[2,4,32,128]{3,2,1,0:T(8,128)S(1)}, f32[2,4,32,128]{3,2,1,0:T(8,128)S(1)}, f32[2,4,32,128]{3,2,1,0:T(...) custom-call(s32[5]{0:T(128)S(1)} %stack.23.place_ref, ...), custom_call_target="tpu_custom_call" | custom-call | tf_op jit(solution)/shard_map/pallas_call | solution.py:284
  79.3 4.4 %collective-permute-start.7 = (f32[2,4,32,128]{3,2,1,0:T(8,128)S(1)}, f32[2,4,32,128]{3,2,1,0:T(8,128)S(1)}, u32[]{:S(2)}, u32[]{:S(2)}) collective-permute-start(f32[2,4,32,128]{3,2,1,0:T(8,128)S(1)} %get-tuple-element.30), channel_id=1, source_target_pairs={{0,76},{1,72},{8,68},{9,64},{64,12},{65,8},{72,4},{73,0},{16,92},{... | collective-permute-start | bytes 393224 | tf_op jit(solution)/shard_map/ppermute | solution.py:359
  83.7 0.0 collective-permute-start.8
  83.7 0.8 collective-permute-start.9
  84.5 0.0 collective-permute-start.10
  84.5 1.1 collective-permute-start.11
  85.6 0.0 collective-permute-done.7.refs_0_
  85.6 2.9 %collective-permute-start.12 = (f32[2,4,32,128]{3,2,1,0:T(8,128)S(1)}, f32[2,4,32,128]{3,2,1,0:T(8,128)S(1)}, u32[]{:S(2)}, u32[]{:S(2)}) collective-permute-start(f32[2,4,32,128]{3,2,1,0:T(8,128)S(1)} %get-tuple-element.35), channel_id=1, source_target_pairs={{0,8},{1,12},{8,0},{9,4},{64,72},{65,76},{72,64},{73,68},{16,24},{... | collective-permute-start | bytes 393224 | tf_op jit(solution)/shard_map/ppermute | solution.py:359
  88.6 1.8 %collective-permute-done.8.refs_1_ = f32[2,4,32,128]{3,2,1,0:T(8,128)S(1)} collective-permute-done((f32[2,4,32,128]{3,2,1,0:T(8,128)S(1)}, f32[2,4,32,128]{3,2,1,0:T(8,128)S(1)}, u32[]{:S(2)}, u32[]{:S(2)}) %collective-permute-start.8) | collective-permute-done | bytes 131104 | tf_op jit(solution)/shard_map/ppermute | solution.py:359
  90.4 0.9 collective-permute-start.13
  91.3 0.6 collective-permute-done.9.refs_2_
  91.9 2.7 %collective-permute-start.14 = (f32[2,4,32,128]{3,2,1,0:T(8,128)S(1)}, f32[2,4,32,128]{3,2,1,0:T(8,128)S(1)}, u32[]{:S(2)}, u32[]{:S(2)}) collective-permute-start(f32[2,4,32,128]{3,2,1,0:T(8,128)S(1)} %get-tuple-element.37), channel_id=1, source_target_pairs={{0,0},{1,4},{8,8},{9,12},{64,64},{65,68},{72,72},{73,76},{16,16},{... | collective-permute-start | bytes 393224 | tf_op jit(solution)/shard_map/ppermute | solution.py:359
  94.5 0.0 collective-permute-done.10.refs_3_
  94.5 0.0 collective-permute-done.11.refs_4_
  94.6 0.0 collective-permute-done.12.refs_5_
  94.6 0.0 collective-permute-done.13.refs_6_
  94.6 4.8 %collective-permute-done.14.refs_7_ = f32[2,4,32,128]{3,2,1,0:T(8,128)S(1)} collective-permute-done((f32[2,4,32,128]{3,2,1,0:T(8,128)S(1)}, f32[2,4,32,128]{3,2,1,0:T(8,128)S(1)}, u32[]{:S(2)}, u32[]{:S(2)}) %collective-permute-start.14) | collective-permute-done | bytes 131104 | tf_op jit(solution)/shard_map/ppermute | solution.py:359
  99.4 0.0 copy-done.1
  99.4 1.4 %shard_map.94 = f32[1024,128]{1,0:T(8,128)S(1)} custom-call(s32[5]{0:T(128)S(1)} %stack.23.place_ref, f32[2,4,32,128]{3,2,1,0:T(8,128)S(1)} %collective-permute-done.7.refs_0_, f32[2,4,32,128]{3,2,1,0:T(8,128)S(1)} %collective-permute-done.8.refs_1_, f32[2,4,32,128]{3,2,1,0:T(8,128)S(1)} %collective-permute-done.9.refs_2_, ...), custom_call_target="tpu_custom_call" | custom-call | tf_op jit(solution)/shard_map/pallas_call | solution.py:322
  100.8 21.2 %all_to_all.10 = f32[64,16,128]{2,1,0:T(8,128)S(1)} all-to-all(f32[64,16,128]{2,1,0:T(8,128)S(1)} %bitcast.22), channel_id=1, replica_groups=mesh['seq'=64,'tp'=4] {'seq'}, dimensions={0} | all-to-all | bytes 1048576 | tf_op jit(solution)/shard_map/all_to_all | solution.py:385
  122.0 1.7 %shard_map.95 = f32[8,16384]{1,0:T(8,128)} custom-call(s32[5]{0:T(128)S(1)} %stack.23.place_ref, f32[1024,128]{1,0:T(8,128)S(1)} %bitcast.21), custom_call_target="tpu_custom_call" | custom-call | tf_op jit(solution)/shard_map/pallas_call | solution.py:348
  (2 shorter events, 0.0 us)
Async XLA Ops:
  0.0 75.0 %copy-start.4 = (f32[64,128]{1,0:T(8,128)S(1)}, f32[64,128]{1,0:T(8,128)}, u32[]{:S(2)}) copy-start(f32[64,128]{1,0:T(8,128)} %constant.124.clone.refs_10_) | copy-start | bytes 98308
  0.0 75.0 %copy-start.2 = (bf16[256,512]{1,0:T(8,128)(2,1)S(1)}, bf16[256,512]{1,0:T(8,128)(2,1)}, u32[]{:S(2)}) copy-start(bf16[256,512]{1,0:T(8,128)(2,1)} %constant.123.clone.refs_9_) | copy-start | bytes 786436
  0.0 75.0 %copy-start.3 = (bf16[256,512]{1,0:T(8,128)(2,1)S(1)}, bf16[256,512]{1,0:T(8,128)(2,1)}, u32[]{:S(2)}) copy-start(bf16[256,512]{1,0:T(8,128)(2,1)} %constant.122.clone.refs_8_) | copy-start | bytes 786436
  2.5 48.1 %all-to-all-start = ((f32[256,8,128]{2,1,0:T(8,128)}), f32[256,8,128]{2,1,0:T(8,128)S(1)}, u32[]{:S(2)}, u32[]{:S(2)}) async-start(f32[256,8,128]{2,1,0:T(8,128)} %shard_map.91), calls=%async_computation | async-start | bytes 2097152 | tf_op jit(solution)/shard_map/all_to_all | solution.py:377
  50.6 1.0 copy-start
  51.6 47.8 %copy-start.1 = (bf16[256,1024]{1,0:T(8,128)(2,1)S(1)}, bf16[256,1024]{1,0:T(8,128)(2,1)}, u32[]{:S(2)}) copy-start(bf16[256,1024]{1,0:T(8,128)(2,1)} %constant.125.clone.refs_8_) | copy-start | bytes 1572868
  54.5 13.3 %collective-permute-start = (f32[2,2,4,32,128]{4,3,2,1,0:T(8,128)S(1)}, f32[2,2,4,32,128]{4,3,2,1,0:T(8,128)S(1)}, u32[]{:S(2)}, u32[]{:S(2)}) collective-permute-start(f32[2,2,4,32,128]{4,3,2,1,0:T(8,128)S(1)} %get-tuple-element.22), channel_id=1, source_target_pairs={{0,73},{1,72},{8,65},{9,64},{64,9},{65,8},{72,1},{73,0},{16,89},{1... | collective-permute-start | bytes 786440 | tf_op jit(solution)/shard_map/ppermute | solution.py:359
  55.5 13.0 %collective-permute-start.1 = (f32[2,2,4,32,128]{4,3,2,1,0:T(8,128)S(1)}, f32[2,2,4,32,128]{4,3,2,1,0:T(8,128)S(1)}, u32[]{:S(2)}, u32[]{:S(2)}) collective-permute-start(f32[2,2,4,32,128]{4,3,2,1,0:T(8,128)S(1)} %get-tuple-element.23), channel_id=1, source_target_pairs={{0,72},{1,73},{8,64},{9,65},{64,8},{65,9},{72,0},{73,1},{16,88},{1... | collective-permute-start | bytes 786440 | tf_op jit(solution)/shard_map/ppermute | solution.py:359
  59.1 14.2 %collective-permute-start.2 = (f32[2,2,4,32,128]{4,3,2,1,0:T(8,128)S(1)}, f32[2,2,4,32,128]{4,3,2,1,0:T(8,128)S(1)}, u32[]{:S(2)}, u32[]{:S(2)}) collective-permute-start(f32[2,2,4,32,128]{4,3,2,1,0:T(8,128)S(1)} %get-tuple-element.24), channel_id=1, source_target_pairs={{0,65},{1,64},{8,73},{9,72},{64,1},{65,0},{72,9},{73,8},{16,81},{1... | collective-permute-start | bytes 786440 | tf_op jit(solution)/shard_map/ppermute | solution.py:359
  62.0 11.3 %collective-permute-start.3 = (f32[2,2,4,32,128]{4,3,2,1,0:T(8,128)S(1)}, f32[2,2,4,32,128]{4,3,2,1,0:T(8,128)S(1)}, u32[]{:S(2)}, u32[]{:S(2)}) collective-permute-start(f32[2,2,4,32,128]{4,3,2,1,0:T(8,128)S(1)} %get-tuple-element.25), channel_id=1, source_target_pairs={{0,9},{1,8},{8,1},{9,0},{64,73},{65,72},{72,65},{73,64},{16,25},{1... | collective-permute-start | bytes 786440 | tf_op jit(solution)/shard_map/ppermute | solution.py:359
  62.7 10.9 %collective-permute-start.4 = (f32[2,2,4,32,128]{4,3,2,1,0:T(8,128)S(1)}, f32[2,2,4,32,128]{4,3,2,1,0:T(8,128)S(1)}, u32[]{:S(2)}, u32[]{:S(2)}) collective-permute-start(f32[2,2,4,32,128]{4,3,2,1,0:T(8,128)S(1)} %get-tuple-element.26), channel_id=1, source_target_pairs={{0,64},{1,65},{8,72},{9,73},{64,0},{65,1},{72,8},{73,9},{16,80},{1... | collective-permute-start | bytes 786440 | tf_op jit(solution)/shard_map/ppermute | solution.py:359
  67.8 6.4 %collective-permute-start.5 = (f32[2,2,4,32,128]{4,3,2,1,0:T(8,128)S(1)}, f32[2,2,4,32,128]{4,3,2,1,0:T(8,128)S(1)}, u32[]{:S(2)}, u32[]{:S(2)}) collective-permute-start(f32[2,2,4,32,128]{4,3,2,1,0:T(8,128)S(1)} %get-tuple-element.27), channel_id=1, source_target_pairs={{0,8},{1,9},{8,0},{9,1},{64,72},{65,73},{72,64},{73,65},{16,24},{1... | collective-permute-start | bytes 786440 | tf_op jit(solution)/shard_map/ppermute | solution.py:359
  68.5 6.4 %collective-permute-start.6 = (f32[2,2,4,32,128]{4,3,2,1,0:T(8,128)S(1)}, f32[2,2,4,32,128]{4,3,2,1,0:T(8,128)S(1)}, u32[]{:S(2)}, u32[]{:S(2)}) collective-permute-start(f32[2,2,4,32,128]{4,3,2,1,0:T(8,128)S(1)} %get-tuple-element.28), channel_id=1, source_target_pairs={{0,1},{1,0},{8,9},{9,8},{64,65},{65,64},{72,73},{73,72},{16,17},{1... | collective-permute-start | bytes 786440 | tf_op jit(solution)/shard_map/ppermute | solution.py:359
  79.3 6.4 %collective-permute-start.7 = (f32[2,4,32,128]{3,2,1,0:T(8,128)S(1)}, f32[2,4,32,128]{3,2,1,0:T(8,128)S(1)}, u32[]{:S(2)}, u32[]{:S(2)}) collective-permute-start(f32[2,4,32,128]{3,2,1,0:T(8,128)S(1)} %get-tuple-element.30), channel_id=1, source_target_pairs={{0,76},{1,72},{8,68},{9,64},{64,12},{65,8},{72,4},{73,0},{16,92},{... | collective-permute-start | bytes 393224 | tf_op jit(solution)/shard_map/ppermute | solution.py:359
  83.7 6.7 %collective-permute-start.8 = (f32[2,4,32,128]{3,2,1,0:T(8,128)S(1)}, f32[2,4,32,128]{3,2,1,0:T(8,128)S(1)}, u32[]{:S(2)}, u32[]{:S(2)}) collective-permute-start(f32[2,4,32,128]{3,2,1,0:T(8,128)S(1)} %get-tuple-element.31), channel_id=1, source_target_pairs={{0,72},{1,76},{8,64},{9,68},{64,8},{65,12},{72,0},{73,4},{16,88},{... | collective-permute-start | bytes 393224 | tf_op jit(solution)/shard_map/ppermute | solution.py:359
  83.7 8.2 %collective-permute-start.9 = (f32[2,4,32,128]{3,2,1,0:T(8,128)S(1)}, f32[2,4,32,128]{3,2,1,0:T(8,128)S(1)}, u32[]{:S(2)}, u32[]{:S(2)}) collective-permute-start(f32[2,4,32,128]{3,2,1,0:T(8,128)S(1)} %get-tuple-element.32), channel_id=1, source_target_pairs={{0,68},{1,64},{8,76},{9,72},{64,4},{65,0},{72,12},{73,8},{16,84},{... | collective-permute-start | bytes 393224 | tf_op jit(solution)/shard_map/ppermute | solution.py:359
  84.5 10.0 %collective-permute-start.10 = (f32[2,4,32,128]{3,2,1,0:T(8,128)S(1)}, f32[2,4,32,128]{3,2,1,0:T(8,128)S(1)}, u32[]{:S(2)}, u32[]{:S(2)}) collective-permute-start(f32[2,4,32,128]{3,2,1,0:T(8,128)S(1)} %get-tuple-element.33), channel_id=1, source_target_pairs={{0,12},{1,8},{8,4},{9,0},{64,76},{65,72},{72,68},{73,64},{16,28},{... | collective-permute-start | bytes 393224 | tf_op jit(solution)/shard_map/ppermute | solution.py:359
  84.5 10.0 %collective-permute-start.11 = (f32[2,4,32,128]{3,2,1,0:T(8,128)S(1)}, f32[2,4,32,128]{3,2,1,0:T(8,128)S(1)}, u32[]{:S(2)}, u32[]{:S(2)}) collective-permute-start(f32[2,4,32,128]{3,2,1,0:T(8,128)S(1)} %get-tuple-element.34), channel_id=1, source_target_pairs={{0,64},{1,68},{8,72},{9,76},{64,0},{65,4},{72,8},{73,12},{16,80},{... | collective-permute-start | bytes 393224 | tf_op jit(solution)/shard_map/ppermute | solution.py:359
  85.6 8.9 %collective-permute-start.12 = (f32[2,4,32,128]{3,2,1,0:T(8,128)S(1)}, f32[2,4,32,128]{3,2,1,0:T(8,128)S(1)}, u32[]{:S(2)}, u32[]{:S(2)}) collective-permute-start(f32[2,4,32,128]{3,2,1,0:T(8,128)S(1)} %get-tuple-element.35), channel_id=1, source_target_pairs={{0,8},{1,12},{8,0},{9,4},{64,72},{65,76},{72,64},{73,68},{16,24},{... | collective-permute-start | bytes 393224 | tf_op jit(solution)/shard_map/ppermute | solution.py:359
  90.4 4.2 %collective-permute-start.13 = (f32[2,4,32,128]{3,2,1,0:T(8,128)S(1)}, f32[2,4,32,128]{3,2,1,0:T(8,128)S(1)}, u32[]{:S(2)}, u32[]{:S(2)}) collective-permute-start(f32[2,4,32,128]{3,2,1,0:T(8,128)S(1)} %get-tuple-element.36), channel_id=1, source_target_pairs={{0,4},{1,0},{8,12},{9,8},{64,68},{65,64},{72,76},{73,72},{16,20},{... | collective-permute-start | bytes 393224 | tf_op jit(solution)/shard_map/ppermute | solution.py:359
  91.9 7.5 %collective-permute-start.14 = (f32[2,4,32,128]{3,2,1,0:T(8,128)S(1)}, f32[2,4,32,128]{3,2,1,0:T(8,128)S(1)}, u32[]{:S(2)}, u32[]{:S(2)}) collective-permute-start(f32[2,4,32,128]{3,2,1,0:T(8,128)S(1)} %get-tuple-element.37), channel_id=1, source_target_pairs={{0,0},{1,4},{8,8},{9,12},{64,64},{65,68},{72,72},{73,76},{16,16},{... | collective-permute-start | bytes 393224 | tf_op jit(solution)/shard_map/ppermute | solution.py:359

commit v3 on v2

--- a/solution.py
+++ b/solution.py
@@ -74,15 +74,13 @@
     angle = 2.0 * math.pi * ((b[:, None] * b[None, :]) % LANES) / LANES
     cos, sin = np.cos(angle), np.sin(angle)
     lane_high, lane_low = halves(np.block([[cos, -sin], [sin, cos]]))
-    unlane_high, unlane_low = halves(np.block([[cos, sin], [-sin, cos]]))
     angle = (2.0 * math.pi / 4096) * (np.arange(32)[:, None] * b[None, :])
     twist = np.stack([np.cos(angle), -np.sin(angle)], axis=1)
     return dict(
-        ahead=np.concatenate([ahead_high, ahead_low], axis=1),
+        ahead=np.stack([np.concatenate([ahead_high, ahead_low], axis=1)] * 2),
         back=np.concatenate([back_high, back_low], axis=1),
         turn=turn,
         lane=np.concatenate([lane_high, lane_low], axis=1),
-        unlane=np.concatenate([unlane_high, unlane_low], axis=1),
         twist=twist.astype(np.float32).reshape(64, LANES),
     )
 
@@ -92,12 +90,12 @@
     return high, (x - high.astype(jnp.float32)).astype(jnp.bfloat16)
 
 
-def dot(a, b):
-    return lax.dot_general(a, b, (((1,), (0,)), ((), ())), preferred_element_type=jnp.float32)
-
-
-def three(a_high, a_low, b_high, b_low):
-    return dot(a_high, b_high) + (dot(a_high, b_low) + dot(a_low, b_high))
+def dot(a, b, side=0):
+    return lax.dot_general(a, b, (((1,), (side,)), ((), ())), preferred_element_type=jnp.float32)
+
+
+def three(a_high, a_low, b_high, b_low, side=0):
+    return dot(a_high, b_high, side) + (dot(a_high, b_low, side) + dot(a_low, b_high, side))
 
 
 def times(re, im, factor):
@@ -134,24 +132,36 @@
     return complex(math.cos(angle), math.sin(angle))
 
 
-def pack_kernel(signal_ref, taps_ref, out_ref, rows_ref, sems):
+def pack_kernel(signal_ref, taps_ref, out_ref, rows_ref, packed_ref, sems):
     def load(at, ref, slab):
         rows = pl.ds(256 * slab, 256)
         return pltpu.make_async_copy(ref.at[rows, :], rows_ref.at[at, rows, :], sems.at[at, slab])
 
     copies = [[load(at, ref, slab) for slab in range(4)] for at, ref in enumerate((signal_ref, taps_ref))]
-    for slab in range(4):
+    order = (0, 2, 1, 3)
+    for slab in order:
         for at in range(2):
             copies[at][slab].start()
-    for slab in range(4):
+    stores = []
+    for slab in order:
         for at in range(2):
             copies[at][slab].wait()
+        core = slab % 2
         for row in range(8):
             for g in range(8):
                 to = member(slab, row, g)
                 for at in range(2):
                     start = (slab * 32 + 4 * g) * 8 + row
-                    out_ref[to, pl.ds(4 * at, 4), :] = rows_ref[at, pl.ds(start, 4, stride=8), :]
+                    rows = rows_ref[at, pl.ds(start, 4, stride=8), :]
+                    packed_ref[core, to // 8, to % 4, pl.ds(4 * at, 4), :] = rows
+        if slab >= 2:
+            for n in range(2):
+                part = pl.ds(16 * n, 16)
+                source, to = packed_ref.at[core, part], out_ref.at[part, core]
+                stores.append(pltpu.make_async_copy(source, to, sems.at[2 + core, n]))
+                stores[-1].start()
+    for copy in stores:
+        copy.wait()
 
 
 def tiles(x):
@@ -161,10 +171,14 @@
 def pack(signal, taps):
     return pl.pallas_call(
         pack_kernel,
-        out_shape=jax.ShapeDtypeStruct((256, 8, LANES), jnp.float32),
+        out_shape=jax.ShapeDtypeStruct((32, 2, 4, 8, LANES), jnp.float32),
         in_specs=[HBM, HBM],
-        out_specs=VMEM,
-        scratch_shapes=[pltpu.VMEM((2, 1024, LANES), jnp.float32), pltpu.SemaphoreType.DMA((2, 4))],
+        out_specs=HBM,
+        scratch_shapes=[
+            pltpu.VMEM((2, 1024, LANES), jnp.float32),
+            pltpu.VMEM((2, 32, 4, 8, LANES), jnp.float32),
+            pltpu.SemaphoreType.DMA((4, 4)),
+        ],
         compiler_params=pltpu.CompilerParams(vmem_limit_bytes=60 * 1024 * 1024),
     )(tiles(signal), tiles(taps))
 
@@ -178,11 +192,8 @@
 
 
 def ahead_kernel(place_ref, gain_ref, x_ref, ahead_ref, turn_ref, *rest):
-    outs, (angle_ref, x2_ref, y_ref, sems) = rest[:8], rest[8:]
+    outs, (x2_ref, y_ref) = rest[:8], rest[8:]
     g = place_ref[0]
-    copies = turn_copies(turn_ref, g, angle_ref, sems)
-    for copy in copies:
-        copy.start()
     for s in range(8):
         x = x_ref[pl.ds(s, 256, stride=8), :]
         if s == 4:
@@ -195,13 +206,11 @@
     for n in range(4):
         cols = pl.ds(256 * n, 256)
         y_ref[:, cols] = three(ahead_ref[:, :256], ahead_ref[:, 256:], x2_ref[:256, cols], x2_ref[256:, cols])
-    for copy in copies:
-        copy.wait()
     for i, flip in enumerate(FLIPS):
         to = pl.multiple_of((g ^ flip) * 32, 32)
         for a in range(4):
-            tr = angle_ref[0, pl.ds(to, 32), pl.ds(128 * a, 128)]
-            ti = angle_ref[1, pl.ds(to, 32), pl.ds(128 * a, 128)]
+            tr = turn_ref[0, pl.ds(to, 32), pl.ds(128 * a, 128)]
+            ti = turn_ref[1, pl.ds(to, 32), pl.ds(128 * a, 128)]
             for sf in range(2):
                 cols = pl.ds(512 * sf + 128 * a, 128)
                 re, im = y_ref[pl.ds(to, 32), cols], y_ref[pl.ds(256 + to, 32), cols]
@@ -214,21 +223,16 @@
     return pl.pallas_call(
         ahead_kernel,
         out_shape=[jax.ShapeDtypeStruct(block, jnp.float32)] * 8,
-        in_specs=[SMEM, SMEM, VMEM, VMEM, HBM],
+        in_specs=[SMEM, SMEM] + [VMEM] * 3,
         out_specs=[VMEM] * 8,
-        scratch_shapes=[
-            pltpu.VMEM((2, 256, 512), jnp.float32),
-            pltpu.VMEM((512, 1024), jnp.bfloat16),
-            pltpu.VMEM((512, 1024), jnp.float32),
-            pltpu.SemaphoreType.DMA((4,)),
-        ],
+        scratch_shapes=[pltpu.VMEM((512, 1024), jnp.bfloat16), pltpu.VMEM((512, 1024), jnp.float32)],
         compiler_params=PARAMS,
     )(place, gain, x, table, turn)
 
 
 def middle_kernel(place_ref, *refs):
-    ins, (lane_ref, unlane_ref, twist_ref, turn_ref) = refs[:8], refs[8:12]
-    outs, angle_ref, (x_ref, m_ref, d_ref, y_ref, sems) = refs[12:20], refs[20], refs[21:]
+    ins, (lane_ref, twist_ref, turn_ref) = refs[:8], refs[8:11]
+    outs, angle_ref, (x_ref, m_ref, d_ref, y_ref, sems) = refs[11:19], refs[19], refs[20:]
     g, o = place_ref[0], place_ref[1]
     copies = turn_copies(turn_ref, place_ref[3], angle_ref, sems)
     for copy in copies:
@@ -255,7 +259,7 @@
         d = three(high, low, lane_ref[:, :256], lane_ref[:, 256:])
         sr, si, fr, fi = d[:256, :128], d[:256, 128:], d[256:, :128], d[256:, 128:]
         high, low = split(jnp.concatenate([sr * fr - si * fi, sr * fi + si * fr], axis=1))
-        d_ref[pl.ds(0, 256), :] = three(high, low, unlane_ref[:, :256], unlane_ref[:, 256:])
+        d_ref[pl.ds(0, 256), :] = three(high, low, lane_ref[:, :256], lane_ref[:, 256:], 1)
         for m1 in range(8):
             values = []
             for m2 in range(4):
@@ -279,13 +283,13 @@
         copy.wait()
 
 
-def middle(place, blocks, lane, unlane, twist, turn):
+def middle(place, blocks, lane, twist, turn):
     block = (2, 4, 32, LANES)
     return pl.pallas_call(
         middle_kernel,
         out_shape=[jax.ShapeDtypeStruct(block, jnp.float32)] * 8
         + [jax.ShapeDtypeStruct((2, 256, 512), jnp.float32)],
-        in_specs=[SMEM] + [VMEM] * 11 + [HBM],
+        in_specs=[SMEM] + [VMEM] * 10 + [HBM],
         out_specs=[VMEM] * 9,
         scratch_shapes=[
             pltpu.VMEM((8, 2, 2, 4, 32, LANES), jnp.float32),
@@ -295,7 +299,7 @@
             pltpu.SemaphoreType.DMA((4,)),
         ],
         compiler_params=PARAMS,
-    )(place, *blocks, lane, unlane, twist, turn)
+    )(place, *blocks, lane, twist, turn)
 
 
 def back_kernel(place_ref, *refs):
@@ -329,19 +333,25 @@
     )(place, *blocks, table, turn)
 
 
-def unpack_kernel(place_ref, x_ref, out_ref, rows_ref):
+def unpack_kernel(place_ref, x_ref, out_ref, rows_ref, block_ref, sems):
     odd = place_ref[4]
     for y in range(4):
         for z in range(8):
             start = pl.multiple_of((((y + odd) & 3) * 8 + ((z + odd) & 7)) * 32, 32)
             rows_ref[pl.ds((y * 8 + z) * 32, 32), :] = x_ref[pl.ds(start, 32), :]
+    copies = []
     for jl in range(4):
         for o in range(8):
             for a in range(4):
                 start = (16 * (o >> 2) + 2 * ((o >> 1) & 1) + (o & 1)) * 16 + jl * 4 + a
-                cols = pl.ds(128 * (jl * 32 + 4 * o + a), 128)
+                cols = pl.ds(128 * (4 * o + a), 128)
                 for half in range(2):
-                    out_ref[pl.ds(4 * half, 4), cols] = rows_ref[pl.ds(start + 512 * half, 4, stride=64), :]
+                    rows = rows_ref[pl.ds(start + 512 * half, 4, stride=64), :]
+                    block_ref[jl, pl.ds(4 * half, 4), cols] = rows
+        copies.append(pltpu.make_async_copy(block_ref.at[jl], out_ref.at[:, pl.ds(4096 * jl, 4096)], sems.at[jl]))
+        copies[-1].start()
+    for copy in copies:
+        copy.wait()
 
 
 def unpack(place, x):
@@ -349,8 +359,12 @@
         unpack_kernel,
         out_shape=jax.ShapeDtypeStruct((8, 16384), jnp.float32),
         in_specs=[SMEM, VMEM],
-        out_specs=VMEM,
-        scratch_shapes=[pltpu.VMEM((1024, LANES), jnp.float32)],
+        out_specs=HBM,
+        scratch_shapes=[
+            pltpu.VMEM((1024, LANES), jnp.float32),
+            pltpu.VMEM((4, 8, 4096), jnp.float32),
+            pltpu.SemaphoreType.DMA((4,)),
+        ],
         compiler_params=PARAMS,
     )(place, x)
 
@@ -373,13 +387,15 @@
     place = jnp.stack([g, first, o ^ odd, o, odd]).astype(jnp.int32)
     gain = jnp.where(g == 0, skip_gain[row], 0.0).reshape(1)
 
-    packed = pack(signal, filter_taps)
+    packed = pack(signal, filter_taps).reshape(256, 8, LANES)
     tokens = lax.all_to_all(packed, AXES, split_axis=0, concat_axis=0, tiled=True)
-    names = ("turn", "ahead", "lane", "unlane", "twist", "back")
-    turn, table, lane, unlane, twist, untable = (jnp.asarray(known[name]) for name in names)
-    parts = ahead(place, gain, tokens.reshape(2048, LANES), table, turn)
+    names = ("turn", "ahead", "lane", "twist", "back")
+    turn, table, lane, twist, untable = (jnp.asarray(known[name]) for name in names)
+    table = lax.dynamic_index_in_dim(table, core, keepdims=False)
+    turn_in = lax.dynamic_index_in_dim(turn, g, keepdims=False)
+    parts = ahead(place, gain, tokens.reshape(2048, LANES), table, turn_in)
     parts = exchange(parts, among_members, 7)
-    *parts, turn = middle(place, parts, lane, unlane, twist, turn)
+    *parts, turn = middle(place, parts, lane, twist, turn)
     parts = exchange(parts, to_keepers, 8)
     result = back(place, parts, untable, turn)
     result = lax.all_to_all(result.reshape(64, 16, LANES), "seq", split_axis=0, concat_axis=0, tiled=True)

time: 124 us -> 122 us (0.984)
  waiting for transfers between devices: 47.5 us -> 45 us
  local copies, waits for them, and re-layouts: 2.41 us -> 3.81 us
    all_to_all x1, waiting for transfers between devices: 30.2 us -> 27.8 us  [body(): lax.all_to_all(packed, AXES, split_axis=0, concat_axis=0, tiled=True)]
    squeeze x0 -> x2, local copies, waits for them, and re-layouts: none -> 2.38 us  [the longest x1 1.3 us: body(): turn_in = lax.dynamic_index_in_dim(turn, g, keepdims=False)]
  transfers between devices with their start and end apart: 16 -> 16, of which waited for: 10 -> 10; matrix products, arithmetic and copies ran while one was open for 1% -> 3% of each run, Pallas kernels for 0% -> 0%
where the time goes in v3:
time: 122 us
  waiting for transfers between devices  45 us (37%)
  starting transfers between devices  39 us (32%)
  blocking collectives  21.2 us (17%)
  Pallas kernels  11.6 us (10%)
  local copies, waits for them, and re-layouts  3.81 us (3%)
    all_to_all x1, waiting for transfers between devices, body(): lax.all_to_all(packed, AXES, split_axis=0, concat_axis=0, tiled=True)  27.8 us
    ppermute x15, starting transfers between devices, exchange(): lax.ppermute(part, AXES, pairs(flip))  23.3 us
    all_to_all x1, blocking collectives, body(): lax.all_to_all(result.reshape(64, 16, LANES), 'seq', split_axis=0, concat...  21.2 us
    ppermute x15, waiting for transfers between devices, exchange(): lax.ppermute(part, AXES, pairs(flip))  17.2 us
    all_to_all x1, starting transfers between devices, body(): lax.all_to_all(packed, AXES, split_axis=0, concat_axis=0, tiled=True)  15.7 us
    pallas_call x1, Pallas kernels, middle(): pl.pallas_call(middle_kernel, out_shape=[jax.ShapeDtypeStruct(block, jnp....  4.27 us
  transfers between devices with their start and end apart: 16, of which 10 were waited for; matrix products, arithmetic and copies ran while one was open for 3% of the time, Pallas kernels for 0%

profile of v3, /device:TPU:1, one launch (start us, length us, event | category | flops | bytes accessed | tf_op | source)
XLA Modules:
  0.0 121.7 jit_solution(17001729501155134779)
XLA Ops:
  0.0 0.0 copy-start.2
  0.0 0.0 copy-start.1
  0.0 2.3 %shard_map.82 = f32[32,2,4,8,128]{4,3,2,1,0:T(8,128)} custom-call(f32[1024,128]{1,0:T(8,128)} %bitcast.29, f32[1024,128]{1,0:T(8,128)} %bitcast.30), custom_call_target="tpu_custom_call" | custom-call | tf_op jit(solution)/shard_map/pallas_call | solution.py:172
  2.4 15.7 %all-to-all-start = ((f32[256,8,128]{2,1,0:T(8,128)}), f32[256,8,128]{2,1,0:T(8,128)S(1)}, u32[]{:S(2)}, u32[]{:S(2)}) async-start(f32[256,8,128]{2,1,0:T(8,128)} %bitcast.28), calls=%async_computation | async-start | bytes 2097152 | tf_op jit(solution)/shard_map/all_to_all | solution.py:391
  18.1 0.0 copy-start
  18.3 1.3 %dynamic_slice.11 = f32[1]{0:T(128)} dynamic-slice(f32[8]{0:T(128)} %param.10, s32[]{:T(128)S(6)} %select_n.85), dynamic_slice_sizes={1} | dynamic-slice | bytes 12 | tf_op jit(solution)/shard_map/dynamic_slice | solution.py:388
  20.2 0.1 stack.23.place_ref
  20.3 1.1 dynamic-slice_bitcast_fusion.1.ahead_ref
  21.4 1.3 %dynamic-slice_bitcast_fusion.turn_ref = f32[2,256,512]{2,1,0:T(8,128)S(1)} fusion(f32[8,2,256,512]{3,2,1,0:T(8,128)} %constant.126.clone.refs_10_, s32[]{:T(128)S(6)} %select_n.88), kind=kLoop, calls=%fused_computation | loop fusion | bytes 2097156 | tf_op jit(solution)/shard_map/jit(dynamic_index_in_dim)/squeeze | solution.py:395
  22.7 27.8 %all-to-all-done = f32[256,8,128]{2,1,0:T(8,128)S(1)} async-done(((f32[256,8,128]{2,1,0:T(8,128)}), f32[256,8,128]{2,1,0:T(8,128)S(1)}, u32[]{:S(2)}, u32[]{:S(2)}) %all-to-all-start) | async-done | bytes 1048608 | tf_op jit(solution)/shard_map/all_to_all | solution.py:391
  50.5 2.0 %shard_map.83 = (f32[2,2,4,32,128]{4,3,2,1,0:T(8,128)S(1)}, f32[2,2,4,32,128]{4,3,2,1,0:T(8,128)S(1)}, f32[2,2,4,32,128]{4,3,2,1,0:T(8,128)S(1)}, f32[2,2,4,32,1...) custom-call(s32[5]{0:T(128)S(1)} %stack.23.place_ref, ...), custom_call_target="tpu_custom_call" | custom-call | tf_op jit(solution)/shard_map/pallas_call | solution.py:223
  52.4 1.1 collective-permute-start
  53.5 3.5 %collective-permute-start.1 = (f32[2,2,4,32,128]{4,3,2,1,0:T(8,128)S(1)}, f32[2,2,4,32,128]{4,3,2,1,0:T(8,128)S(1)}, u32[]{:S(2)}, u32[]{:S(2)}) collective-permute-start(f32[2,2,4,32,128]{4,3,2,1,0:T(8,128)S(1)} %get-tuple-element.23), channel_id=1, source_target_pairs={{0,72},{1,73},{8,64},{9,65},{64,8},{65,9},{72,0},{73,1},{16,88},{1... | collective-permute-start | bytes 786440 | tf_op jit(solution)/shard_map/ppermute | solution.py:373
  57.0 2.9 %collective-permute-start.2 = (f32[2,2,4,32,128]{4,3,2,1,0:T(8,128)S(1)}, f32[2,2,4,32,128]{4,3,2,1,0:T(8,128)S(1)}, u32[]{:S(2)}, u32[]{:S(2)}) collective-permute-start(f32[2,2,4,32,128]{4,3,2,1,0:T(8,128)S(1)} %get-tuple-element.24), channel_id=1, source_target_pairs={{0,65},{1,64},{8,73},{9,72},{64,1},{65,0},{72,9},{73,8},{16,81},{1... | collective-permute-start | bytes 786440 | tf_op jit(solution)/shard_map/ppermute | solution.py:373
  59.9 0.8 collective-permute-start.3
  60.7 1.6 %collective-permute-start.4 = (f32[2,2,4,32,128]{4,3,2,1,0:T(8,128)S(1)}, f32[2,2,4,32,128]{4,3,2,1,0:T(8,128)S(1)}, u32[]{:S(2)}, u32[]{:S(2)}) collective-permute-start(f32[2,2,4,32,128]{4,3,2,1,0:T(8,128)S(1)} %get-tuple-element.26), channel_id=1, source_target_pairs={{0,64},{1,65},{8,72},{9,73},{64,0},{65,1},{72,8},{73,9},{16,80},{1... | collective-permute-start | bytes 786440 | tf_op jit(solution)/shard_map/ppermute | solution.py:373
  62.3 3.4 %collective-permute-done.refs_0_ = f32[2,2,4,32,128]{4,3,2,1,0:T(8,128)S(1)} collective-permute-done((f32[2,2,4,32,128]{4,3,2,1,0:T(8,128)S(1)}, f32[2,2,4,32,128]{4,3,2,1,0:T(8,128)S(1)}, u32[]{:S(2)}, u32[]{:S(2)}) %collective-permute-start) | collective-permute-done | bytes 262176 | tf_op jit(solution)/shard_map/ppermute | solution.py:373
  65.7 0.0 collective-permute-start.5
  65.7 0.8 collective-permute-done.1.refs_1_
  66.5 0.7 collective-permute-start.6
  67.2 4.0 %collective-permute-done.2.refs_2_ = f32[2,2,4,32,128]{4,3,2,1,0:T(8,128)S(1)} collective-permute-done((f32[2,2,4,32,128]{4,3,2,1,0:T(8,128)S(1)}, f32[2,2,4,32,128]{4,3,2,1,0:T(8,128)S(1)}, u32[]{:S(2)}, u32[]{:S(2)}) %collective-permute-start.2) | collective-permute-done | bytes 262176 | tf_op jit(solution)/shard_map/ppermute | solution.py:373
  71.2 0.0 collective-permute-done.3.refs_3_
  71.2 0.4 collective-permute-done.4.refs_4_
  71.6 0.6 collective-permute-done.5.refs_5_
  72.2 0.8 collective-permute-done.6.refs_6_
  72.9 0.0 copy-done.2
  72.9 0.0 copy-done.1
  72.9 4.3 %shard_map.84 = (f32[2,4,32,128]{3,2,1,0:T(8,128)S(1)}, f32[2,4,32,128]{3,2,1,0:T(8,128)S(1)}, f32[2,4,32,128]{3,2,1,0:T(8,128)S(1)}, f32[2,4,32,128]{3,2,1,0:T(...) custom-call(s32[5]{0:T(128)S(1)} %stack.23.place_ref, ...), custom_call_target="tpu_custom_call" | custom-call | tf_op jit(solution)/shard_map/pallas_call | solution.py:288
  77.2 4.4 %collective-permute-start.7 = (f32[2,4,32,128]{3,2,1,0:T(8,128)S(1)}, f32[2,4,32,128]{3,2,1,0:T(8,128)S(1)}, u32[]{:S(2)}, u32[]{:S(2)}) collective-permute-start(f32[2,4,32,128]{3,2,1,0:T(8,128)S(1)} %get-tuple-element.30), channel_id=1, source_target_pairs={{0,76},{1,72},{8,68},{9,64},{64,12},{65,8},{72,4},{73,0},{16,92},{... | collective-permute-start | bytes 393224 | tf_op jit(solution)/shard_map/ppermute | solution.py:373
  81.6 0.0 collective-permute-start.8
  81.6 0.8 collective-permute-start.9
  82.4 0.0 collective-permute-start.10
  82.5 1.1 collective-permute-start.11
  83.5 0.0 collective-permute-done.7.refs_0_
  83.6 2.9 %collective-permute-start.12 = (f32[2,4,32,128]{3,2,1,0:T(8,128)S(1)}, f32[2,4,32,128]{3,2,1,0:T(8,128)S(1)}, u32[]{:S(2)}, u32[]{:S(2)}) collective-permute-start(f32[2,4,32,128]{3,2,1,0:T(8,128)S(1)} %get-tuple-element.35), channel_id=1, source_target_pairs={{0,8},{1,12},{8,0},{9,4},{64,72},{65,76},{72,64},{73,68},{16,24},{... | collective-permute-start | bytes 393224 | tf_op jit(solution)/shard_map/ppermute | solution.py:373
  86.5 1.8 %collective-permute-done.8.refs_1_ = f32[2,4,32,128]{3,2,1,0:T(8,128)S(1)} collective-permute-done((f32[2,4,32,128]{3,2,1,0:T(8,128)S(1)}, f32[2,4,32,128]{3,2,1,0:T(8,128)S(1)}, u32[]{:S(2)}, u32[]{:S(2)}) %collective-permute-start.8) | collective-permute-done | bytes 131104 | tf_op jit(solution)/shard_map/ppermute | solution.py:373
  88.3 0.9 collective-permute-start.13
  89.2 0.6 collective-permute-done.9.refs_2_
  89.8 2.7 %collective-permute-start.14 = (f32[2,4,32,128]{3,2,1,0:T(8,128)S(1)}, f32[2,4,32,128]{3,2,1,0:T(8,128)S(1)}, u32[]{:S(2)}, u32[]{:S(2)}) collective-permute-start(f32[2,4,32,128]{3,2,1,0:T(8,128)S(1)} %get-tuple-element.37), channel_id=1, source_target_pairs={{0,0},{1,4},{8,8},{9,12},{64,64},{65,68},{72,72},{73,76},{16,16},{... | collective-permute-start | bytes 393224 | tf_op jit(solution)/shard_map/ppermute | solution.py:373
  92.5 0.0 collective-permute-done.10.refs_3_
  92.5 0.0 collective-permute-done.11.refs_4_
  92.5 0.0 collective-permute-done.12.refs_5_
  92.5 0.0 collective-permute-done.13.refs_6_
  92.5 4.8 %collective-permute-done.14.refs_7_ = f32[2,4,32,128]{3,2,1,0:T(8,128)S(1)} collective-permute-done((f32[2,4,32,128]{3,2,1,0:T(8,128)S(1)}, f32[2,4,32,128]{3,2,1,0:T(8,128)S(1)}, u32[]{:S(2)}, u32[]{:S(2)}) %collective-permute-start.14) | collective-permute-done | bytes 131104 | tf_op jit(solution)/shard_map/ppermute | solution.py:373
  97.3 0.0 copy-done
  97.4 1.4 %shard_map.85 = f32[1024,128]{1,0:T(8,128)S(1)} custom-call(s32[5]{0:T(128)S(1)} %stack.23.place_ref, f32[2,4,32,128]{3,2,1,0:T(8,128)S(1)} %collective-permute-done.7.refs_0_, f32[2,4,32,128]{3,2,1,0:T(8,128)S(1)} %collective-permute-done.8.refs_1_, f32[2,4,32,128]{3,2,1,0:T(8,128)S(1)} %collective-permute-done.9.refs_2_, ...), custom_call_target="tpu_custom_call" | custom-call | tf_op jit(solution)/shard_map/pallas_call | solution.py:326
  98.7 21.2 %all_to_all.10 = f32[64,16,128]{2,1,0:T(8,128)S(1)} all-to-all(f32[64,16,128]{2,1,0:T(8,128)S(1)} %bitcast.27), channel_id=1, replica_groups=mesh['seq'=64,'tp'=4] {'seq'}, dimensions={0} | all-to-all | bytes 1048576 | tf_op jit(solution)/shard_map/all_to_all | solution.py:401
  120.0 1.6 %shard_map.86 = f32[8,16384]{1,0:T(8,128)} custom-call(s32[5]{0:T(128)S(1)} %stack.23.place_ref, f32[1024,128]{1,0:T(8,128)S(1)} %bitcast.26), custom_call_target="tpu_custom_call" | custom-call | tf_op jit(solution)/shard_map/pallas_call | solution.py:358
Async XLA Ops:
  0.0 72.9 %copy-start.2 = (f32[64,128]{1,0:T(8,128)S(1)}, f32[64,128]{1,0:T(8,128)}, u32[]{:S(2)}) copy-start(f32[64,128]{1,0:T(8,128)} %constant.129.clone.refs_9_) | copy-start | bytes 98308
  0.0 72.9 %copy-start.1 = (bf16[256,512]{1,0:T(8,128)(2,1)S(1)}, bf16[256,512]{1,0:T(8,128)(2,1)}, u32[]{:S(2)}) copy-start(bf16[256,512]{1,0:T(8,128)(2,1)} %constant.128.clone.refs_8_) | copy-start | bytes 786436
  2.4 48.1 %all-to-all-start = ((f32[256,8,128]{2,1,0:T(8,128)}), f32[256,8,128]{2,1,0:T(8,128)S(1)}, u32[]{:S(2)}, u32[]{:S(2)}) async-start(f32[256,8,128]{2,1,0:T(8,128)} %bitcast.28), calls=%async_computation | async-start | bytes 2097152 | tf_op jit(solution)/shard_map/all_to_all | solution.py:391
  18.1 79.2 %copy-start = (bf16[256,1024]{1,0:T(8,128)(2,1)S(1)}, bf16[256,1024]{1,0:T(8,128)(2,1)}, u32[]{:S(2)}) copy-start(bf16[256,1024]{1,0:T(8,128)(2,1)} %constant.130.clone.refs_8_) | copy-start | bytes 1572868
  52.4 13.3 %collective-permute-start = (f32[2,2,4,32,128]{4,3,2,1,0:T(8,128)S(1)}, f32[2,2,4,32,128]{4,3,2,1,0:T(8,128)S(1)}, u32[]{:S(2)}, u32[]{:S(2)}) collective-permute-start(f32[2,2,4,32,128]{4,3,2,1,0:T(8,128)S(1)} %get-tuple-element.22), channel_id=1, source_target_pairs={{0,73},{1,72},{8,65},{9,64},{64,9},{65,8},{72,1},{73,0},{16,89},{1... | collective-permute-start | bytes 786440 | tf_op jit(solution)/shard_map/ppermute | solution.py:373
  53.5 13.0 %collective-permute-start.1 = (f32[2,2,4,32,128]{4,3,2,1,0:T(8,128)S(1)}, f32[2,2,4,32,128]{4,3,2,1,0:T(8,128)S(1)}, u32[]{:S(2)}, u32[]{:S(2)}) collective-permute-start(f32[2,2,4,32,128]{4,3,2,1,0:T(8,128)S(1)} %get-tuple-element.23), channel_id=1, source_target_pairs={{0,72},{1,73},{8,64},{9,65},{64,8},{65,9},{72,0},{73,1},{16,88},{1... | collective-permute-start | bytes 786440 | tf_op jit(solution)/shard_map/ppermute | solution.py:373
  57.0 14.2 %collective-permute-start.2 = (f32[2,2,4,32,128]{4,3,2,1,0:T(8,128)S(1)}, f32[2,2,4,32,128]{4,3,2,1,0:T(8,128)S(1)}, u32[]{:S(2)}, u32[]{:S(2)}) collective-permute-start(f32[2,2,4,32,128]{4,3,2,1,0:T(8,128)S(1)} %get-tuple-element.24), channel_id=1, source_target_pairs={{0,65},{1,64},{8,73},{9,72},{64,1},{65,0},{72,9},{73,8},{16,81},{1... | collective-permute-start | bytes 786440 | tf_op jit(solution)/shard_map/ppermute | solution.py:373
  59.9 11.3 %collective-permute-start.3 = (f32[2,2,4,32,128]{4,3,2,1,0:T(8,128)S(1)}, f32[2,2,4,32,128]{4,3,2,1,0:T(8,128)S(1)}, u32[]{:S(2)}, u32[]{:S(2)}) collective-permute-start(f32[2,2,4,32,128]{4,3,2,1,0:T(8,128)S(1)} %get-tuple-element.25), channel_id=1, source_target_pairs={{0,9},{1,8},{8,1},{9,0},{64,73},{65,72},{72,65},{73,64},{16,25},{1... | collective-permute-start | bytes 786440 | tf_op jit(solution)/shard_map/ppermute | solution.py:373
  60.7 10.9 %collective-permute-start.4 = (f32[2,2,4,32,128]{4,3,2,1,0:T(8,128)S(1)}, f32[2,2,4,32,128]{4,3,2,1,0:T(8,128)S(1)}, u32[]{:S(2)}, u32[]{:S(2)}) collective-permute-start(f32[2,2,4,32,128]{4,3,2,1,0:T(8,128)S(1)} %get-tuple-element.26), channel_id=1, source_target_pairs={{0,64},{1,65},{8,72},{9,73},{64,0},{65,1},{72,8},{73,9},{16,80},{1... | collective-permute-start | bytes 786440 | tf_op jit(solution)/shard_map/ppermute | solution.py:373
  65.7 6.4 %collective-permute-start.5 = (f32[2,2,4,32,128]{4,3,2,1,0:T(8,128)S(1)}, f32[2,2,4,32,128]{4,3,2,1,0:T(8,128)S(1)}, u32[]{:S(2)}, u32[]{:S(2)}) collective-permute-start(f32[2,2,4,32,128]{4,3,2,1,0:T(8,128)S(1)} %get-tuple-element.27), channel_id=1, source_target_pairs={{0,8},{1,9},{8,0},{9,1},{64,72},{65,73},{72,64},{73,65},{16,24},{1... | collective-permute-start | bytes 786440 | tf_op jit(solution)/shard_map/ppermute | solution.py:373
  66.5 6.4 %collective-permute-start.6 = (f32[2,2,4,32,128]{4,3,2,1,0:T(8,128)S(1)}, f32[2,2,4,32,128]{4,3,2,1,0:T(8,128)S(1)}, u32[]{:S(2)}, u32[]{:S(2)}) collective-permute-start(f32[2,2,4,32,128]{4,3,2,1,0:T(8,128)S(1)} %get-tuple-element.28), channel_id=1, source_target_pairs={{0,1},{1,0},{8,9},{9,8},{64,65},{65,64},{72,73},{73,72},{16,17},{1... | collective-permute-start | bytes 786440 | tf_op jit(solution)/shard_map/ppermute | solution.py:373
  77.2 6.4 %collective-permute-start.7 = (f32[2,4,32,128]{3,2,1,0:T(8,128)S(1)}, f32[2,4,32,128]{3,2,1,0:T(8,128)S(1)}, u32[]{:S(2)}, u32[]{:S(2)}) collective-permute-start(f32[2,4,32,128]{3,2,1,0:T(8,128)S(1)} %get-tuple-element.30), channel_id=1, source_target_pairs={{0,76},{1,72},{8,68},{9,64},{64,12},{65,8},{72,4},{73,0},{16,92},{... | collective-permute-start | bytes 393224 | tf_op jit(solution)/shard_map/ppermute | solution.py:373
  81.6 6.7 %collective-permute-start.8 = (f32[2,4,32,128]{3,2,1,0:T(8,128)S(1)}, f32[2,4,32,128]{3,2,1,0:T(8,128)S(1)}, u32[]{:S(2)}, u32[]{:S(2)}) collective-permute-start(f32[2,4,32,128]{3,2,1,0:T(8,128)S(1)} %get-tuple-element.31), channel_id=1, source_target_pairs={{0,72},{1,76},{8,64},{9,68},{64,8},{65,12},{72,0},{73,4},{16,88},{... | collective-permute-start | bytes 393224 | tf_op jit(solution)/shard_map/ppermute | solution.py:373
  81.6 8.2 %collective-permute-start.9 = (f32[2,4,32,128]{3,2,1,0:T(8,128)S(1)}, f32[2,4,32,128]{3,2,1,0:T(8,128)S(1)}, u32[]{:S(2)}, u32[]{:S(2)}) collective-permute-start(f32[2,4,32,128]{3,2,1,0:T(8,128)S(1)} %get-tuple-element.32), channel_id=1, source_target_pairs={{0,68},{1,64},{8,76},{9,72},{64,4},{65,0},{72,12},{73,8},{16,84},{... | collective-permute-start | bytes 393224 | tf_op jit(solution)/shard_map/ppermute | solution.py:373
  82.4 10.0 %collective-permute-start.10 = (f32[2,4,32,128]{3,2,1,0:T(8,128)S(1)}, f32[2,4,32,128]{3,2,1,0:T(8,128)S(1)}, u32[]{:S(2)}, u32[]{:S(2)}) collective-permute-start(f32[2,4,32,128]{3,2,1,0:T(8,128)S(1)} %get-tuple-element.33), channel_id=1, source_target_pairs={{0,12},{1,8},{8,4},{9,0},{64,76},{65,72},{72,68},{73,64},{16,28},{... | collective-permute-start | bytes 393224 | tf_op jit(solution)/shard_map/ppermute | solution.py:373
  82.5 10.0 %collective-permute-start.11 = (f32[2,4,32,128]{3,2,1,0:T(8,128)S(1)}, f32[2,4,32,128]{3,2,1,0:T(8,128)S(1)}, u32[]{:S(2)}, u32[]{:S(2)}) collective-permute-start(f32[2,4,32,128]{3,2,1,0:T(8,128)S(1)} %get-tuple-element.34), channel_id=1, source_target_pairs={{0,64},{1,68},{8,72},{9,76},{64,0},{65,4},{72,8},{73,12},{16,80},{... | collective-permute-start | bytes 393224 | tf_op jit(solution)/shard_map/ppermute | solution.py:373
  83.6 8.9 %collective-permute-start.12 = (f32[2,4,32,128]{3,2,1,0:T(8,128)S(1)}, f32[2,4,32,128]{3,2,1,0:T(8,128)S(1)}, u32[]{:S(2)}, u32[]{:S(2)}) collective-permute-start(f32[2,4,32,128]{3,2,1,0:T(8,128)S(1)} %get-tuple-element.35), channel_id=1, source_target_pairs={{0,8},{1,12},{8,0},{9,4},{64,72},{65,76},{72,64},{73,68},{16,24},{... | collective-permute-start | bytes 393224 | tf_op jit(solution)/shard_map/ppermute | solution.py:373
  88.3 4.2 %collective-permute-start.13 = (f32[2,4,32,128]{3,2,1,0:T(8,128)S(1)}, f32[2,4,32,128]{3,2,1,0:T(8,128)S(1)}, u32[]{:S(2)}, u32[]{:S(2)}) collective-permute-start(f32[2,4,32,128]{3,2,1,0:T(8,128)S(1)} %get-tuple-element.36), channel_id=1, source_target_pairs={{0,4},{1,0},{8,12},{9,8},{64,68},{65,64},{72,76},{73,72},{16,20},{... | collective-permute-start | bytes 393224 | tf_op jit(solution)/shard_map/ppermute | solution.py:373
  89.8 7.5 %collective-permute-start.14 = (f32[2,4,32,128]{3,2,1,0:T(8,128)S(1)}, f32[2,4,32,128]{3,2,1,0:T(8,128)S(1)}, u32[]{:S(2)}, u32[]{:S(2)}) collective-permute-start(f32[2,4,32,128]{3,2,1,0:T(8,128)S(1)} %get-tuple-element.37), channel_id=1, source_target_pairs={{0,0},{1,4},{8,8},{9,12},{64,64},{65,68},{72,72},{73,76},{16,16},{... | collective-permute-start | bytes 393224 | tf_op jit(solution)/shard_map/ppermute | solution.py:373

commit v4 on v3

--- a/solution.py
+++ b/solution.py
@@ -241,7 +241,7 @@
         x_ref[g ^ flip] = ins[i][...]
 
     def step(kb, carry):
-        rows = pl.ds(pl.multiple_of(kb * 8, 8), 8)
+        rows = pl.ds(pl.multiple_of(kb * 16, 16), 16)
         for sf in range(2):
             for a in range(4):
                 values = [(x_ref[s, 0, sf, a, rows, :], x_ref[s, 1, sf, a, rows, :]) for s in range(8)]
@@ -253,19 +253,19 @@
                 for m2, (re, im) in enumerate(values):
                     m = m1 + 8 * m2
                     tr, ti = twist_ref[2 * m : 2 * m + 1, :], twist_ref[2 * m + 1 : 2 * m + 2, :]
-                    d_ref[pl.ds(256 * sf + 8 * m, 8), :128] = re * tr - im * ti
-                    d_ref[pl.ds(256 * sf + 8 * m, 8), 128:] = re * ti + im * tr
+                    d_ref[pl.ds(512 * sf + 16 * m, 16), :128] = re * tr - im * ti
+                    d_ref[pl.ds(512 * sf + 16 * m, 16), 128:] = re * ti + im * tr
         high, low = split(d_ref[...])
         d = three(high, low, lane_ref[:, :256], lane_ref[:, 256:])
-        sr, si, fr, fi = d[:256, :128], d[:256, 128:], d[256:, :128], d[256:, 128:]
+        sr, si, fr, fi = d[:512, :128], d[:512, 128:], d[512:, :128], d[512:, 128:]
         high, low = split(jnp.concatenate([sr * fr - si * fi, sr * fi + si * fr], axis=1))
-        d_ref[pl.ds(0, 256), :] = three(high, low, lane_ref[:, :256], lane_ref[:, 256:], 1)
+        d_ref[pl.ds(0, 512), :] = three(high, low, lane_ref[:, :256], lane_ref[:, 256:], 1)
         for m1 in range(8):
             values = []
             for m2 in range(4):
                 m = m1 + 8 * m2
                 tr, ti = twist_ref[2 * m : 2 * m + 1, :], twist_ref[2 * m + 1 : 2 * m + 2, :]
-                re, im = d_ref[pl.ds(8 * m, 8), :128], d_ref[pl.ds(8 * m, 8), 128:]
+                re, im = d_ref[pl.ds(16 * m, 16), :128], d_ref[pl.ds(16 * m, 16), 128:]
                 values.append((re * tr + im * ti, im * tr - re * ti))
             for a, value in enumerate(fourier(values, 1)):
                 re, im = times(*value, unit(1, a * m1, 32))
@@ -276,7 +276,7 @@
                 y_ref[at, 0, a, rows, :], y_ref[at, 1, a, rows, :] = re, im
         return carry
 
-    lax.fori_loop(0, 4, step, 0)
+    lax.fori_loop(0, 2, step, 0)
     for i, flip in enumerate(FLIPS):
         outs[i][...] = y_ref[o ^ flip]
     for copy in copies:
@@ -293,8 +293,8 @@
         out_specs=[VMEM] * 9,
         scratch_shapes=[
             pltpu.VMEM((8, 2, 2, 4, 32, LANES), jnp.float32),
-            pltpu.VMEM((8, 4, 2, 8, LANES), jnp.float32),
-            pltpu.VMEM((512, 256), jnp.float32),
+            pltpu.VMEM((8, 4, 2, 16, LANES), jnp.float32),
+            pltpu.VMEM((1024, 256), jnp.float32),
             pltpu.VMEM((8, 2, 4, 32, LANES), jnp.float32),
             pltpu.SemaphoreType.DMA((4,)),
         ],
@@ -335,19 +335,17 @@
 
 def unpack_kernel(place_ref, x_ref, out_ref, rows_ref, block_ref, sems):
     odd = place_ref[4]
-    for y in range(4):
-        for z in range(8):
+    for o in range(4):
+        for row in range(8):
+            y, z = 2 * (row >> 2) + (o >> 1), 2 * (row & 3) + (o & 1)
             start = pl.multiple_of((((y + odd) & 3) * 8 + ((z + odd) & 7)) * 32, 32)
-            rows_ref[pl.ds((y * 8 + z) * 32, 32), :] = x_ref[pl.ds(start, 32), :]
+            rows_ref[pl.ds((o * 8 + row) * 32, 32), :] = x_ref[pl.ds(start, 32), :]
     copies = []
     for jl in range(4):
         for o in range(8):
             for a in range(4):
-                start = (16 * (o >> 2) + 2 * ((o >> 1) & 1) + (o & 1)) * 16 + jl * 4 + a
-                cols = pl.ds(128 * (4 * o + a), 128)
-                for half in range(2):
-                    rows = rows_ref[pl.ds(start + 512 * half, 4, stride=64), :]
-                    block_ref[jl, pl.ds(4 * half, 4), cols] = rows
+                start = (o >> 1) * 256 + (o & 1) * 16 + jl * 4 + a
+                block_ref[jl, :, pl.ds(128 * (4 * o + a), 128)] = rows_ref[pl.ds(start, 8, stride=32), :]
         copies.append(pltpu.make_async_copy(block_ref.at[jl], out_ref.at[:, pl.ds(4096 * jl, 4096)], sems.at[jl]))
         copies[-1].start()
     for copy in copies:

time: 122 us -> 121 us (level)
  no operation moved by 1% of the time
where the time goes in v4:
time: 121 us
  waiting for transfers between devices  45 us (37%)
  starting transfers between devices  39 us (32%)
  blocking collectives  21.2 us (18%)
  Pallas kernels  11 us (9%)
  local copies, waits for them, and re-layouts  3.81 us (3%)
    all_to_all x1, waiting for transfers between devices, body(): lax.all_to_all(packed, AXES, split_axis=0, concat_axis=0, tiled=True)  27.8 us
    ppermute x15, starting transfers between devices, exchange(): lax.ppermute(part, AXES, pairs(flip))  23.3 us
    all_to_all x1, blocking collectives, body(): lax.all_to_all(result.reshape(64, 16, LANES), 'seq', split_axis=0, concat...  21.2 us
    ppermute x15, waiting for transfers between devices, exchange(): lax.ppermute(part, AXES, pairs(flip))  17.2 us
    all_to_all x1, starting transfers between devices, body(): lax.all_to_all(packed, AXES, split_axis=0, concat_axis=0, tiled=True)  15.7 us
    pallas_call x1, Pallas kernels, middle(): pl.pallas_call(middle_kernel, out_shape=[jax.ShapeDtypeStruct(block, jnp....  3.73 us
  transfers between devices with their start and end apart: 16, of which 10 were waited for; matrix products, arithmetic and copies ran while one was open for 3% of the time, Pallas kernels for 0%

profile of v4, /device:TPU:1, one launch (start us, length us, event | category | flops | bytes accessed | tf_op | source)
XLA Modules:
  0.0 121.2 jit_solution(2248618599875354606)
XLA Ops:
  0.0 0.0 copy-start.2
  0.0 0.0 copy-start.1
  0.0 2.3 %shard_map.82 = f32[32,2,4,8,128]{4,3,2,1,0:T(8,128)} custom-call(f32[1024,128]{1,0:T(8,128)} %bitcast.29, f32[1024,128]{1,0:T(8,128)} %bitcast.30), custom_call_target="tpu_custom_call" | custom-call | tf_op jit(solution)/shard_map/pallas_call | solution.py:172
  2.4 15.7 %all-to-all-start = ((f32[256,8,128]{2,1,0:T(8,128)}), f32[256,8,128]{2,1,0:T(8,128)S(1)}, u32[]{:S(2)}, u32[]{:S(2)}) async-start(f32[256,8,128]{2,1,0:T(8,128)} %bitcast.28), calls=%async_computation | async-start | bytes 2097152 | tf_op jit(solution)/shard_map/all_to_all | solution.py:389
  18.1 0.0 copy-start
  18.3 1.3 %dynamic_slice.11 = f32[1]{0:T(128)} dynamic-slice(f32[8]{0:T(128)} %param.10, s32[]{:T(128)S(6)} %select_n.85), dynamic_slice_sizes={1} | dynamic-slice | bytes 12 | tf_op jit(solution)/shard_map/dynamic_slice | solution.py:386
  20.2 0.1 stack.23.place_ref
  20.3 1.1 dynamic-slice_bitcast_fusion.1.ahead_ref
  21.4 1.3 %dynamic-slice_bitcast_fusion.turn_ref = f32[2,256,512]{2,1,0:T(8,128)S(1)} fusion(f32[8,2,256,512]{3,2,1,0:T(8,128)} %constant.126.clone.refs_10_, s32[]{:T(128)S(6)} %select_n.88), kind=kLoop, calls=%fused_computation | loop fusion | bytes 2097156 | tf_op jit(solution)/shard_map/jit(dynamic_index_in_dim)/squeeze | solution.py:393
  22.7 27.8 %all-to-all-done = f32[256,8,128]{2,1,0:T(8,128)S(1)} async-done(((f32[256,8,128]{2,1,0:T(8,128)}), f32[256,8,128]{2,1,0:T(8,128)S(1)}, u32[]{:S(2)}, u32[]{:S(2)}) %all-to-all-start) | async-done | bytes 1048608 | tf_op jit(solution)/shard_map/all_to_all | solution.py:389
  50.5 2.0 %shard_map.83 = (f32[2,2,4,32,128]{4,3,2,1,0:T(8,128)S(1)}, f32[2,2,4,32,128]{4,3,2,1,0:T(8,128)S(1)}, f32[2,2,4,32,128]{4,3,2,1,0:T(8,128)S(1)}, f32[2,2,4,32,1...) custom-call(s32[5]{0:T(128)S(1)} %stack.23.place_ref, ...), custom_call_target="tpu_custom_call" | custom-call | tf_op jit(solution)/shard_map/pallas_call | solution.py:223
  52.4 1.1 collective-permute-start
  53.5 3.5 %collective-permute-start.1 = (f32[2,2,4,32,128]{4,3,2,1,0:T(8,128)S(1)}, f32[2,2,4,32,128]{4,3,2,1,0:T(8,128)S(1)}, u32[]{:S(2)}, u32[]{:S(2)}) collective-permute-start(f32[2,2,4,32,128]{4,3,2,1,0:T(8,128)S(1)} %get-tuple-element.23), channel_id=1, source_target_pairs={{0,72},{1,73},{8,64},{9,65},{64,8},{65,9},{72,0},{73,1},{16,88},{1... | collective-permute-start | bytes 786440 | tf_op jit(solution)/shard_map/ppermute | solution.py:371
  57.0 2.9 %collective-permute-start.2 = (f32[2,2,4,32,128]{4,3,2,1,0:T(8,128)S(1)}, f32[2,2,4,32,128]{4,3,2,1,0:T(8,128)S(1)}, u32[]{:S(2)}, u32[]{:S(2)}) collective-permute-start(f32[2,2,4,32,128]{4,3,2,1,0:T(8,128)S(1)} %get-tuple-element.24), channel_id=1, source_target_pairs={{0,65},{1,64},{8,73},{9,72},{64,1},{65,0},{72,9},{73,8},{16,81},{1... | collective-permute-start | bytes 786440 | tf_op jit(solution)/shard_map/ppermute | solution.py:371
  59.9 0.8 collective-permute-start.3
  60.7 1.6 %collective-permute-start.4 = (f32[2,2,4,32,128]{4,3,2,1,0:T(8,128)S(1)}, f32[2,2,4,32,128]{4,3,2,1,0:T(8,128)S(1)}, u32[]{:S(2)}, u32[]{:S(2)}) collective-permute-start(f32[2,2,4,32,128]{4,3,2,1,0:T(8,128)S(1)} %get-tuple-element.26), channel_id=1, source_target_pairs={{0,64},{1,65},{8,72},{9,73},{64,0},{65,1},{72,8},{73,9},{16,80},{1... | collective-permute-start | bytes 786440 | tf_op jit(solution)/shard_map/ppermute | solution.py:371
  62.3 3.4 %collective-permute-done.refs_0_ = f32[2,2,4,32,128]{4,3,2,1,0:T(8,128)S(1)} collective-permute-done((f32[2,2,4,32,128]{4,3,2,1,0:T(8,128)S(1)}, f32[2,2,4,32,128]{4,3,2,1,0:T(8,128)S(1)}, u32[]{:S(2)}, u32[]{:S(2)}) %collective-permute-start) | collective-permute-done | bytes 262176 | tf_op jit(solution)/shard_map/ppermute | solution.py:371
  65.7 0.0 collective-permute-start.5
  65.7 0.8 collective-permute-done.1.refs_1_
  66.5 0.7 collective-permute-start.6
  67.2 4.0 %collective-permute-done.2.refs_2_ = f32[2,2,4,32,128]{4,3,2,1,0:T(8,128)S(1)} collective-permute-done((f32[2,2,4,32,128]{4,3,2,1,0:T(8,128)S(1)}, f32[2,2,4,32,128]{4,3,2,1,0:T(8,128)S(1)}, u32[]{:S(2)}, u32[]{:S(2)}) %collective-permute-start.2) | collective-permute-done | bytes 262176 | tf_op jit(solution)/shard_map/ppermute | solution.py:371
  71.2 0.0 collective-permute-done.3.refs_3_
  71.2 0.4 collective-permute-done.4.refs_4_
  71.6 0.6 collective-permute-done.5.refs_5_
  72.2 0.8 collective-permute-done.6.refs_6_
  72.9 0.0 copy-done.2
  72.9 0.0 copy-done.1
  72.9 3.7 %shard_map.84 = (f32[2,4,32,128]{3,2,1,0:T(8,128)S(1)}, f32[2,4,32,128]{3,2,1,0:T(8,128)S(1)}, f32[2,4,32,128]{3,2,1,0:T(8,128)S(1)}, f32[2,4,32,128]{3,2,1,0:T(...) custom-call(s32[5]{0:T(128)S(1)} %stack.23.place_ref, ...), custom_call_target="tpu_custom_call" | custom-call | tf_op jit(solution)/shard_map/pallas_call | solution.py:288
  76.7 4.4 %collective-permute-start.7 = (f32[2,4,32,128]{3,2,1,0:T(8,128)S(1)}, f32[2,4,32,128]{3,2,1,0:T(8,128)S(1)}, u32[]{:S(2)}, u32[]{:S(2)}) collective-permute-start(f32[2,4,32,128]{3,2,1,0:T(8,128)S(1)} %get-tuple-element.30), channel_id=1, source_target_pairs={{0,76},{1,72},{8,68},{9,64},{64,12},{65,8},{72,4},{73,0},{16,92},{... | collective-permute-start | bytes 393224 | tf_op jit(solution)/shard_map/ppermute | solution.py:371
  81.1 0.0 collective-permute-start.8
  81.1 0.8 collective-permute-start.9
  81.9 0.0 collective-permute-start.10
  81.9 1.1 collective-permute-start.11
  83.0 0.0 collective-permute-done.7.refs_0_
  83.0 2.9 %collective-permute-start.12 = (f32[2,4,32,128]{3,2,1,0:T(8,128)S(1)}, f32[2,4,32,128]{3,2,1,0:T(8,128)S(1)}, u32[]{:S(2)}, u32[]{:S(2)}) collective-permute-start(f32[2,4,32,128]{3,2,1,0:T(8,128)S(1)} %get-tuple-element.35), channel_id=1, source_target_pairs={{0,8},{1,12},{8,0},{9,4},{64,72},{65,76},{72,64},{73,68},{16,24},{... | collective-permute-start | bytes 393224 | tf_op jit(solution)/shard_map/ppermute | solution.py:371
  86.0 1.8 %collective-permute-done.8.refs_1_ = f32[2,4,32,128]{3,2,1,0:T(8,128)S(1)} collective-permute-done((f32[2,4,32,128]{3,2,1,0:T(8,128)S(1)}, f32[2,4,32,128]{3,2,1,0:T(8,128)S(1)}, u32[]{:S(2)}, u32[]{:S(2)}) %collective-permute-start.8) | collective-permute-done | bytes 131104 | tf_op jit(solution)/shard_map/ppermute | solution.py:371
  87.8 0.9 collective-permute-start.13
  88.7 0.6 collective-permute-done.9.refs_2_
  89.3 2.7 %collective-permute-start.14 = (f32[2,4,32,128]{3,2,1,0:T(8,128)S(1)}, f32[2,4,32,128]{3,2,1,0:T(8,128)S(1)}, u32[]{:S(2)}, u32[]{:S(2)}) collective-permute-start(f32[2,4,32,128]{3,2,1,0:T(8,128)S(1)} %get-tuple-element.37), channel_id=1, source_target_pairs={{0,0},{1,4},{8,8},{9,12},{64,64},{65,68},{72,72},{73,76},{16,16},{... | collective-permute-start | bytes 393224 | tf_op jit(solution)/shard_map/ppermute | solution.py:371
  91.9 0.0 collective-permute-done.10.refs_3_
  91.9 0.0 collective-permute-done.11.refs_4_
  91.9 0.0 collective-permute-done.12.refs_5_
  92.0 0.0 collective-permute-done.13.refs_6_
  92.0 4.8 %collective-permute-done.14.refs_7_ = f32[2,4,32,128]{3,2,1,0:T(8,128)S(1)} collective-permute-done((f32[2,4,32,128]{3,2,1,0:T(8,128)S(1)}, f32[2,4,32,128]{3,2,1,0:T(8,128)S(1)}, u32[]{:S(2)}, u32[]{:S(2)}) %collective-permute-start.14) | collective-permute-done | bytes 131104 | tf_op jit(solution)/shard_map/ppermute | solution.py:371
  96.8 0.0 copy-done
  96.8 1.4 %shard_map.85 = f32[1024,128]{1,0:T(8,128)S(1)} custom-call(s32[5]{0:T(128)S(1)} %stack.23.place_ref, f32[2,4,32,128]{3,2,1,0:T(8,128)S(1)} %collective-permute-done.7.refs_0_, f32[2,4,32,128]{3,2,1,0:T(8,128)S(1)} %collective-permute-done.8.refs_1_, f32[2,4,32,128]{3,2,1,0:T(8,128)S(1)} %collective-permute-done.9.refs_2_, ...), custom_call_target="tpu_custom_call" | custom-call | tf_op jit(solution)/shard_map/pallas_call | solution.py:326
  98.2 21.2 %all_to_all.10 = f32[64,16,128]{2,1,0:T(8,128)S(1)} all-to-all(f32[64,16,128]{2,1,0:T(8,128)S(1)} %bitcast.27), channel_id=1, replica_groups=mesh['seq'=64,'tp'=4] {'seq'}, dimensions={0} | all-to-all | bytes 1048576 | tf_op jit(solution)/shard_map/all_to_all | solution.py:399
  119.4 1.6 %shard_map.86 = f32[8,16384]{1,0:T(8,128)} custom-call(s32[5]{0:T(128)S(1)} %stack.23.place_ref, f32[1024,128]{1,0:T(8,128)S(1)} %bitcast.26), custom_call_target="tpu_custom_call" | custom-call | tf_op jit(solution)/shard_map/pallas_call | solution.py:356
Async XLA Ops:
  0.0 72.9 %copy-start.2 = (f32[64,128]{1,0:T(8,128)S(1)}, f32[64,128]{1,0:T(8,128)}, u32[]{:S(2)}) copy-start(f32[64,128]{1,0:T(8,128)} %constant.129.clone.refs_9_) | copy-start | bytes 98308
  0.0 72.9 %copy-start.1 = (bf16[256,512]{1,0:T(8,128)(2,1)S(1)}, bf16[256,512]{1,0:T(8,128)(2,1)}, u32[]{:S(2)}) copy-start(bf16[256,512]{1,0:T(8,128)(2,1)} %constant.128.clone.refs_8_) | copy-start | bytes 786436
  2.4 48.1 %all-to-all-start = ((f32[256,8,128]{2,1,0:T(8,128)}), f32[256,8,128]{2,1,0:T(8,128)S(1)}, u32[]{:S(2)}, u32[]{:S(2)}) async-start(f32[256,8,128]{2,1,0:T(8,128)} %bitcast.28), calls=%async_computation | async-start | bytes 2097152 | tf_op jit(solution)/shard_map/all_to_all | solution.py:389
  18.1 78.7 %copy-start = (bf16[256,1024]{1,0:T(8,128)(2,1)S(1)}, bf16[256,1024]{1,0:T(8,128)(2,1)}, u32[]{:S(2)}) copy-start(bf16[256,1024]{1,0:T(8,128)(2,1)} %constant.130.clone.refs_8_) | copy-start | bytes 1572868
  52.4 13.3 %collective-permute-start = (f32[2,2,4,32,128]{4,3,2,1,0:T(8,128)S(1)}, f32[2,2,4,32,128]{4,3,2,1,0:T(8,128)S(1)}, u32[]{:S(2)}, u32[]{:S(2)}) collective-permute-start(f32[2,2,4,32,128]{4,3,2,1,0:T(8,128)S(1)} %get-tuple-element.22), channel_id=1, source_target_pairs={{0,73},{1,72},{8,65},{9,64},{64,9},{65,8},{72,1},{73,0},{16,89},{1... | collective-permute-start | bytes 786440 | tf_op jit(solution)/shard_map/ppermute | solution.py:371
  53.5 13.0 %collective-permute-start.1 = (f32[2,2,4,32,128]{4,3,2,1,0:T(8,128)S(1)}, f32[2,2,4,32,128]{4,3,2,1,0:T(8,128)S(1)}, u32[]{:S(2)}, u32[]{:S(2)}) collective-permute-start(f32[2,2,4,32,128]{4,3,2,1,0:T(8,128)S(1)} %get-tuple-element.23), channel_id=1, source_target_pairs={{0,72},{1,73},{8,64},{9,65},{64,8},{65,9},{72,0},{73,1},{16,88},{1... | collective-permute-start | bytes 786440 | tf_op jit(solution)/shard_map/ppermute | solution.py:371
  57.0 14.2 %collective-permute-start.2 = (f32[2,2,4,32,128]{4,3,2,1,0:T(8,128)S(1)}, f32[2,2,4,32,128]{4,3,2,1,0:T(8,128)S(1)}, u32[]{:S(2)}, u32[]{:S(2)}) collective-permute-start(f32[2,2,4,32,128]{4,3,2,1,0:T(8,128)S(1)} %get-tuple-element.24), channel_id=1, source_target_pairs={{0,65},{1,64},{8,73},{9,72},{64,1},{65,0},{72,9},{73,8},{16,81},{1... | collective-permute-start | bytes 786440 | tf_op jit(solution)/shard_map/ppermute | solution.py:371
  59.9 11.3 %collective-permute-start.3 = (f32[2,2,4,32,128]{4,3,2,1,0:T(8,128)S(1)}, f32[2,2,4,32,128]{4,3,2,1,0:T(8,128)S(1)}, u32[]{:S(2)}, u32[]{:S(2)}) collective-permute-start(f32[2,2,4,32,128]{4,3,2,1,0:T(8,128)S(1)} %get-tuple-element.25), channel_id=1, source_target_pairs={{0,9},{1,8},{8,1},{9,0},{64,73},{65,72},{72,65},{73,64},{16,25},{1... | collective-permute-start | bytes 786440 | tf_op jit(solution)/shard_map/ppermute | solution.py:371
  60.7 10.9 %collective-permute-start.4 = (f32[2,2,4,32,128]{4,3,2,1,0:T(8,128)S(1)}, f32[2,2,4,32,128]{4,3,2,1,0:T(8,128)S(1)}, u32[]{:S(2)}, u32[]{:S(2)}) collective-permute-start(f32[2,2,4,32,128]{4,3,2,1,0:T(8,128)S(1)} %get-tuple-element.26), channel_id=1, source_target_pairs={{0,64},{1,65},{8,72},{9,73},{64,0},{65,1},{72,8},{73,9},{16,80},{1... | collective-permute-start | bytes 786440 | tf_op jit(solution)/shard_map/ppermute | solution.py:371
  65.7 6.4 %collective-permute-start.5 = (f32[2,2,4,32,128]{4,3,2,1,0:T(8,128)S(1)}, f32[2,2,4,32,128]{4,3,2,1,0:T(8,128)S(1)}, u32[]{:S(2)}, u32[]{:S(2)}) collective-permute-start(f32[2,2,4,32,128]{4,3,2,1,0:T(8,128)S(1)} %get-tuple-element.27), channel_id=1, source_target_pairs={{0,8},{1,9},{8,0},{9,1},{64,72},{65,73},{72,64},{73,65},{16,24},{1... | collective-permute-start | bytes 786440 | tf_op jit(solution)/shard_map/ppermute | solution.py:371
  66.5 6.4 %collective-permute-start.6 = (f32[2,2,4,32,128]{4,3,2,1,0:T(8,128)S(1)}, f32[2,2,4,32,128]{4,3,2,1,0:T(8,128)S(1)}, u32[]{:S(2)}, u32[]{:S(2)}) collective-permute-start(f32[2,2,4,32,128]{4,3,2,1,0:T(8,128)S(1)} %get-tuple-element.28), channel_id=1, source_target_pairs={{0,1},{1,0},{8,9},{9,8},{64,65},{65,64},{72,73},{73,72},{16,17},{1... | collective-permute-start | bytes 786440 | tf_op jit(solution)/shard_map/ppermute | solution.py:371
  76.7 6.4 %collective-permute-start.7 = (f32[2,4,32,128]{3,2,1,0:T(8,128)S(1)}, f32[2,4,32,128]{3,2,1,0:T(8,128)S(1)}, u32[]{:S(2)}, u32[]{:S(2)}) collective-permute-start(f32[2,4,32,128]{3,2,1,0:T(8,128)S(1)} %get-tuple-element.30), channel_id=1, source_target_pairs={{0,76},{1,72},{8,68},{9,64},{64,12},{65,8},{72,4},{73,0},{16,92},{... | collective-permute-start | bytes 393224 | tf_op jit(solution)/shard_map/ppermute | solution.py:371
  81.1 6.7 %collective-permute-start.8 = (f32[2,4,32,128]{3,2,1,0:T(8,128)S(1)}, f32[2,4,32,128]{3,2,1,0:T(8,128)S(1)}, u32[]{:S(2)}, u32[]{:S(2)}) collective-permute-start(f32[2,4,32,128]{3,2,1,0:T(8,128)S(1)} %get-tuple-element.31), channel_id=1, source_target_pairs={{0,72},{1,76},{8,64},{9,68},{64,8},{65,12},{72,0},{73,4},{16,88},{... | collective-permute-start | bytes 393224 | tf_op jit(solution)/shard_map/ppermute | solution.py:371
  81.1 8.2 %collective-permute-start.9 = (f32[2,4,32,128]{3,2,1,0:T(8,128)S(1)}, f32[2,4,32,128]{3,2,1,0:T(8,128)S(1)}, u32[]{:S(2)}, u32[]{:S(2)}) collective-permute-start(f32[2,4,32,128]{3,2,1,0:T(8,128)S(1)} %get-tuple-element.32), channel_id=1, source_target_pairs={{0,68},{1,64},{8,76},{9,72},{64,4},{65,0},{72,12},{73,8},{16,84},{... | collective-permute-start | bytes 393224 | tf_op jit(solution)/shard_map/ppermute | solution.py:371
  81.9 10.0 %collective-permute-start.10 = (f32[2,4,32,128]{3,2,1,0:T(8,128)S(1)}, f32[2,4,32,128]{3,2,1,0:T(8,128)S(1)}, u32[]{:S(2)}, u32[]{:S(2)}) collective-permute-start(f32[2,4,32,128]{3,2,1,0:T(8,128)S(1)} %get-tuple-element.33), channel_id=1, source_target_pairs={{0,12},{1,8},{8,4},{9,0},{64,76},{65,72},{72,68},{73,64},{16,28},{... | collective-permute-start | bytes 393224 | tf_op jit(solution)/shard_map/ppermute | solution.py:371
  81.9 10.0 %collective-permute-start.11 = (f32[2,4,32,128]{3,2,1,0:T(8,128)S(1)}, f32[2,4,32,128]{3,2,1,0:T(8,128)S(1)}, u32[]{:S(2)}, u32[]{:S(2)}) collective-permute-start(f32[2,4,32,128]{3,2,1,0:T(8,128)S(1)} %get-tuple-element.34), channel_id=1, source_target_pairs={{0,64},{1,68},{8,72},{9,76},{64,0},{65,4},{72,8},{73,12},{16,80},{... | collective-permute-start | bytes 393224 | tf_op jit(solution)/shard_map/ppermute | solution.py:371
  83.0 8.9 %collective-permute-start.12 = (f32[2,4,32,128]{3,2,1,0:T(8,128)S(1)}, f32[2,4,32,128]{3,2,1,0:T(8,128)S(1)}, u32[]{:S(2)}, u32[]{:S(2)}) collective-permute-start(f32[2,4,32,128]{3,2,1,0:T(8,128)S(1)} %get-tuple-element.35), channel_id=1, source_target_pairs={{0,8},{1,12},{8,0},{9,4},{64,72},{65,76},{72,64},{73,68},{16,24},{... | collective-permute-start | bytes 393224 | tf_op jit(solution)/shard_map/ppermute | solution.py:371
  87.8 4.2 %collective-permute-start.13 = (f32[2,4,32,128]{3,2,1,0:T(8,128)S(1)}, f32[2,4,32,128]{3,2,1,0:T(8,128)S(1)}, u32[]{:S(2)}, u32[]{:S(2)}) collective-permute-start(f32[2,4,32,128]{3,2,1,0:T(8,128)S(1)} %get-tuple-element.36), channel_id=1, source_target_pairs={{0,4},{1,0},{8,12},{9,8},{64,68},{65,64},{72,76},{73,72},{16,20},{... | collective-permute-start | bytes 393224 | tf_op jit(solution)/shard_map/ppermute | solution.py:371
  89.3 7.5 %collective-permute-start.14 = (f32[2,4,32,128]{3,2,1,0:T(8,128)S(1)}, f32[2,4,32,128]{3,2,1,0:T(8,128)S(1)}, u32[]{:S(2)}, u32[]{:S(2)}) collective-permute-start(f32[2,4,32,128]{3,2,1,0:T(8,128)S(1)} %get-tuple-element.37), channel_id=1, source_target_pairs={{0,0},{1,4},{8,8},{9,12},{64,64},{65,68},{72,72},{73,76},{16,16},{... | collective-permute-start | bytes 393224 | tf_op jit(solution)/shard_map/ppermute | solution.py:371

commit v5 on v4

--- a/solution.py
+++ b/solution.py
@@ -15,6 +15,7 @@
 LANES = 128
 AXES = ("seq", "tp")
 FLIPS = (7, 6, 5, 3, 4, 2, 1, 0)
+BACK_FLIPS = (6, 7, 4, 5, 2, 3, 0, 1)
 VMEM = pl.BlockSpec(memory_space=pltpu.VMEM)
 HBM = pl.BlockSpec(memory_space=pltpu.HBM)
 SMEM = pl.BlockSpec(memory_space=pltpu.SMEM)
@@ -277,7 +278,7 @@
         return carry
 
     lax.fori_loop(0, 2, step, 0)
-    for i, flip in enumerate(FLIPS):
+    for i, flip in enumerate(BACK_FLIPS):
         outs[i][...] = y_ref[o ^ flip]
     for copy in copies:
         copy.wait()
@@ -305,7 +306,7 @@
 def back_kernel(place_ref, *refs):
     ins, (back_ref, turn_ref), out_ref, (y2_ref,) = refs[:8], refs[8:10], refs[10], refs[11:]
     g = place_ref[2]
-    for i, flip in enumerate(FLIPS):
+    for i, flip in enumerate(BACK_FLIPS):
         at = pl.multiple_of((g ^ flip) * 32, 32)
         for a in range(4):
             cols = pl.ds(128 * a, 128)
@@ -367,9 +368,9 @@
     )(place, x)
 
 
-def exchange(parts, pairs, count):
-    moved = [lax.ppermute(part, AXES, pairs(flip)) for part, flip in zip(parts[:count], FLIPS)]
-    return moved + list(parts[count:])
+def exchange(parts, pairs, flips):
+    moved = [lax.ppermute(part, AXES, pairs(flip)) for part, flip in zip(parts, flips)]
+    return moved + list(parts[len(flips) :])
 
 
 def body(signal, filter_taps, skip_gain):
@@ -392,9 +393,9 @@
     table = lax.dynamic_index_in_dim(table, core, keepdims=False)
     turn_in = lax.dynamic_index_in_dim(turn, g, keepdims=False)
     parts = ahead(place, gain, tokens.reshape(2048, LANES), table, turn_in)
-    parts = exchange(parts, among_members, 7)
+    parts = exchange(parts, among_members, FLIPS[:7])
     *parts, turn = middle(place, parts, lane, twist, turn)
-    parts = exchange(parts, to_keepers, 8)
+    parts = exchange(parts, to_keepers, BACK_FLIPS)
     result = back(place, parts, untable, turn)
     result = lax.all_to_all(result.reshape(64, 16, LANES), "seq", split_axis=0, concat_axis=0, tiled=True)
     return unpack(place, result.reshape(1024, LANES))

time: 121 us -> 121 us (level)
  waiting for transfers between devices: 45 us -> 40.8 us
  starting transfers between devices: 39 us -> 41.1 us
    ppermute x15, waiting for transfers between devices: 17.2 us -> 13 us  [exchange(): lax.ppermute(part, AXES, pairs(flip))]
    ppermute x15, starting transfers between devices: 23.3 us -> 25.4 us  [exchange(): lax.ppermute(part, AXES, pairs(flip))]
    all_to_all x1, blocking collectives: 21.2 us -> 22.4 us  [body(): lax.all_to_all(result.reshape(64, 16, LANES), 'seq', split_axis=0, concat...]
where the time goes in v5:
time: 121 us; the launch traced here: 120 us
  starting transfers between devices  41.1 us (34%)
  waiting for transfers between devices  40.8 us (34%)
  blocking collectives  22.4 us (19%)
  Pallas kernels  11 us (9%)
  local copies, waits for them, and re-layouts  3.81 us (3%)
    all_to_all x1, waiting for transfers between devices, body(): lax.all_to_all(packed, AXES, split_axis=0, concat_axis=0, tiled=True)  27.8 us
    ppermute x15, starting transfers between devices, exchange(): lax.ppermute(part, AXES, pairs(flip))  25.4 us
    all_to_all x1, blocking collectives, body(): lax.all_to_all(result.reshape(64, 16, LANES), 'seq', split_axis=0, concat...  22.4 us
    all_to_all x1, starting transfers between devices, body(): lax.all_to_all(packed, AXES, split_axis=0, concat_axis=0, tiled=True)  15.7 us
    ppermute x15, waiting for transfers between devices, exchange(): lax.ppermute(part, AXES, pairs(flip))  13 us
    pallas_call x1, Pallas kernels, middle(): pl.pallas_call(middle_kernel, out_shape=[jax.ShapeDtypeStruct(block, jnp....  3.73 us
  transfers between devices with their start and end apart: 16, of which 10 were waited for; matrix products, arithmetic and copies ran while one was open for 3% of the time, Pallas kernels for 0%

profile of v5, /device:TPU:1, one launch (start us, length us, event | category | flops | bytes accessed | tf_op | source)
XLA Modules:
  0.0 120.2 jit_solution(1122680003981832263)
XLA Ops:
  0.0 0.0 copy-start.2
  0.0 0.0 copy-start.1
  0.0 2.3 %shard_map.82 = f32[32,2,4,8,128]{4,3,2,1,0:T(8,128)} custom-call(f32[1024,128]{1,0:T(8,128)} %bitcast.29, f32[1024,128]{1,0:T(8,128)} %bitcast.30), custom_call_target="tpu_custom_call" | custom-call | tf_op jit(solution)/shard_map/pallas_call | solution.py:173
  2.4 15.7 %all-to-all-start = ((f32[256,8,128]{2,1,0:T(8,128)}), f32[256,8,128]{2,1,0:T(8,128)S(1)}, u32[]{:S(2)}, u32[]{:S(2)}) async-start(f32[256,8,128]{2,1,0:T(8,128)} %bitcast.28), calls=%async_computation | async-start | bytes 2097152 | tf_op jit(solution)/shard_map/all_to_all | solution.py:390
  18.1 0.0 copy-start
  18.3 1.3 %dynamic_slice.11 = f32[1]{0:T(128)} dynamic-slice(f32[8]{0:T(128)} %param.10, s32[]{:T(128)S(6)} %select_n.85), dynamic_slice_sizes={1} | dynamic-slice | bytes 12 | tf_op jit(solution)/shard_map/dynamic_slice | solution.py:387
  20.2 0.1 stack.23.place_ref
  20.3 1.1 dynamic-slice_bitcast_fusion.1.ahead_ref
  21.4 1.3 %dynamic-slice_bitcast_fusion.turn_ref = f32[2,256,512]{2,1,0:T(8,128)S(1)} fusion(f32[8,2,256,512]{3,2,1,0:T(8,128)} %constant.126.clone.refs_10_, s32[]{:T(128)S(6)} %select_n.88), kind=kLoop, calls=%fused_computation | loop fusion | bytes 2097156 | tf_op jit(solution)/shard_map/jit(dynamic_index_in_dim)/squeeze | solution.py:394
  22.7 27.8 %all-to-all-done = f32[256,8,128]{2,1,0:T(8,128)S(1)} async-done(((f32[256,8,128]{2,1,0:T(8,128)}), f32[256,8,128]{2,1,0:T(8,128)S(1)}, u32[]{:S(2)}, u32[]{:S(2)}) %all-to-all-start) | async-done | bytes 1048608 | tf_op jit(solution)/shard_map/all_to_all | solution.py:390
  50.5 2.0 %shard_map.83 = (f32[2,2,4,32,128]{4,3,2,1,0:T(8,128)S(1)}, f32[2,2,4,32,128]{4,3,2,1,0:T(8,128)S(1)}, f32[2,2,4,32,128]{4,3,2,1,0:T(8,128)S(1)}, f32[2,2,4,32,1...) custom-call(s32[5]{0:T(128)S(1)} %stack.23.place_ref, ...), custom_call_target="tpu_custom_call" | custom-call | tf_op jit(solution)/shard_map/pallas_call | solution.py:224
  52.4 1.1 collective-permute-start
  53.5 3.5 %collective-permute-start.1 = (f32[2,2,4,32,128]{4,3,2,1,0:T(8,128)S(1)}, f32[2,2,4,32,128]{4,3,2,1,0:T(8,128)S(1)}, u32[]{:S(2)}, u32[]{:S(2)}) collective-permute-start(f32[2,2,4,32,128]{4,3,2,1,0:T(8,128)S(1)} %get-tuple-element.23), channel_id=1, source_target_pairs={{0,72},{1,73},{8,64},{9,65},{64,8},{65,9},{72,0},{73,1},{16,88},{1... | collective-permute-start | bytes 786440 | tf_op jit(solution)/shard_map/ppermute | solution.py:372
  57.0 2.9 %collective-permute-start.2 = (f32[2,2,4,32,128]{4,3,2,1,0:T(8,128)S(1)}, f32[2,2,4,32,128]{4,3,2,1,0:T(8,128)S(1)}, u32[]{:S(2)}, u32[]{:S(2)}) collective-permute-start(f32[2,2,4,32,128]{4,3,2,1,0:T(8,128)S(1)} %get-tuple-element.24), channel_id=1, source_target_pairs={{0,65},{1,64},{8,73},{9,72},{64,1},{65,0},{72,9},{73,8},{16,81},{1... | collective-permute-start | bytes 786440 | tf_op jit(solution)/shard_map/ppermute | solution.py:372
  59.9 0.8 collective-permute-start.3
  60.7 1.6 %collective-permute-start.4 = (f32[2,2,4,32,128]{4,3,2,1,0:T(8,128)S(1)}, f32[2,2,4,32,128]{4,3,2,1,0:T(8,128)S(1)}, u32[]{:S(2)}, u32[]{:S(2)}) collective-permute-start(f32[2,2,4,32,128]{4,3,2,1,0:T(8,128)S(1)} %get-tuple-element.26), channel_id=1, source_target_pairs={{0,64},{1,65},{8,72},{9,73},{64,0},{65,1},{72,8},{73,9},{16,80},{1... | collective-permute-start | bytes 786440 | tf_op jit(solution)/shard_map/ppermute | solution.py:372
  62.3 3.4 %collective-permute-done.refs_0_ = f32[2,2,4,32,128]{4,3,2,1,0:T(8,128)S(1)} collective-permute-done((f32[2,2,4,32,128]{4,3,2,1,0:T(8,128)S(1)}, f32[2,2,4,32,128]{4,3,2,1,0:T(8,128)S(1)}, u32[]{:S(2)}, u32[]{:S(2)}) %collective-permute-start) | collective-permute-done | bytes 262176 | tf_op jit(solution)/shard_map/ppermute | solution.py:372
  65.7 0.0 collective-permute-start.5
  65.7 0.8 collective-permute-done.1.refs_1_
  66.5 0.7 collective-permute-start.6
  67.2 4.0 %collective-permute-done.2.refs_2_ = f32[2,2,4,32,128]{4,3,2,1,0:T(8,128)S(1)} collective-permute-done((f32[2,2,4,32,128]{4,3,2,1,0:T(8,128)S(1)}, f32[2,2,4,32,128]{4,3,2,1,0:T(8,128)S(1)}, u32[]{:S(2)}, u32[]{:S(2)}) %collective-permute-start.2) | collective-permute-done | bytes 262176 | tf_op jit(solution)/shard_map/ppermute | solution.py:372
  71.2 0.0 collective-permute-done.3.refs_3_
  71.2 0.4 collective-permute-done.4.refs_4_
  71.6 0.6 collective-permute-done.5.refs_5_
  72.2 0.8 collective-permute-done.6.refs_6_
  72.9 0.0 copy-done.2
  72.9 0.0 copy-done.1
  72.9 3.7 %shard_map.84 = (f32[2,4,32,128]{3,2,1,0:T(8,128)S(1)}, f32[2,4,32,128]{3,2,1,0:T(8,128)S(1)}, f32[2,4,32,128]{3,2,1,0:T(8,128)S(1)}, f32[2,4,32,128]{3,2,1,0:T(...) custom-call(s32[5]{0:T(128)S(1)} %stack.23.place_ref, ...), custom_call_target="tpu_custom_call" | custom-call | tf_op jit(solution)/shard_map/pallas_call | solution.py:289
  76.7 0.1 collective-permute-start.7
  76.8 5.2 %collective-permute-start.8 = (f32[2,4,32,128]{3,2,1,0:T(8,128)S(1)}, f32[2,4,32,128]{3,2,1,0:T(8,128)S(1)}, u32[]{:S(2)}, u32[]{:S(2)}) collective-permute-start(f32[2,4,32,128]{3,2,1,0:T(8,128)S(1)} %get-tuple-element.31), channel_id=1, source_target_pairs={{0,76},{1,72},{8,68},{9,64},{64,12},{65,8},{72,4},{73,0},{16,92},{... | collective-permute-start | bytes 393224 | tf_op jit(solution)/shard_map/ppermute | solution.py:372
  82.0 0.0 collective-permute-start.9
  82.0 1.8 %collective-permute-start.10 = (f32[2,4,32,128]{3,2,1,0:T(8,128)S(1)}, f32[2,4,32,128]{3,2,1,0:T(8,128)S(1)}, u32[]{:S(2)}, u32[]{:S(2)}) collective-permute-start(f32[2,4,32,128]{3,2,1,0:T(8,128)S(1)} %get-tuple-element.33), channel_id=1, source_target_pairs={{0,68},{1,64},{8,76},{9,72},{64,4},{65,0},{72,12},{73,8},{16,84},{... | collective-permute-start | bytes 393224 | tf_op jit(solution)/shard_map/ppermute | solution.py:372
  83.8 0.0 collective-permute-start.11
  83.8 0.6 collective-permute-done.7.refs_0_
  84.3 2.0 %collective-permute-start.12 = (f32[2,4,32,128]{3,2,1,0:T(8,128)S(1)}, f32[2,4,32,128]{3,2,1,0:T(8,128)S(1)}, u32[]{:S(2)}, u32[]{:S(2)}) collective-permute-start(f32[2,4,32,128]{3,2,1,0:T(8,128)S(1)} %get-tuple-element.35), channel_id=1, source_target_pairs={{0,12},{1,8},{8,4},{9,0},{64,76},{65,72},{72,68},{73,64},{16,28},{... | collective-permute-start | bytes 393224 | tf_op jit(solution)/shard_map/ppermute | solution.py:372
  86.4 0.0 collective-permute-done.8.refs_1_
  86.4 3.6 %collective-permute-start.13 = (f32[2,4,32,128]{3,2,1,0:T(8,128)S(1)}, f32[2,4,32,128]{3,2,1,0:T(8,128)S(1)}, u32[]{:S(2)}, u32[]{:S(2)}) collective-permute-start(f32[2,4,32,128]{3,2,1,0:T(8,128)S(1)} %get-tuple-element.36), channel_id=1, source_target_pairs={{0,0},{1,4},{8,8},{9,12},{64,64},{65,68},{72,72},{73,76},{16,16},{... | collective-permute-start | bytes 393224 | tf_op jit(solution)/shard_map/ppermute | solution.py:372
  90.0 0.5 collective-permute-done.9.refs_2_
  90.5 2.1 %collective-permute-start.14 = (f32[2,4,32,128]{3,2,1,0:T(8,128)S(1)}, f32[2,4,32,128]{3,2,1,0:T(8,128)S(1)}, u32[]{:S(2)}, u32[]{:S(2)}) collective-permute-start(f32[2,4,32,128]{3,2,1,0:T(8,128)S(1)} %get-tuple-element.37), channel_id=1, source_target_pairs={{0,4},{1,0},{8,12},{9,8},{64,68},{65,64},{72,76},{73,72},{16,20},{... | collective-permute-start | bytes 393224 | tf_op jit(solution)/shard_map/ppermute | solution.py:372
  92.7 0.0 collective-permute-done.10.refs_3_
  92.7 0.0 collective-permute-done.11.refs_4_
  92.7 0.0 collective-permute-done.12.refs_5_
  92.7 0.0 collective-permute-done.13.refs_6_
  92.7 1.9 %collective-permute-done.14.refs_7_ = f32[2,4,32,128]{3,2,1,0:T(8,128)S(1)} collective-permute-done((f32[2,4,32,128]{3,2,1,0:T(8,128)S(1)}, f32[2,4,32,128]{3,2,1,0:T(8,128)S(1)}, u32[]{:S(2)}, u32[]{:S(2)}) %collective-permute-start.14) | collective-permute-done | bytes 131104 | tf_op jit(solution)/shard_map/ppermute | solution.py:372
  94.6 0.0 copy-done
  94.6 1.4 %shard_map.85 = f32[1024,128]{1,0:T(8,128)S(1)} custom-call(s32[5]{0:T(128)S(1)} %stack.23.place_ref, f32[2,4,32,128]{3,2,1,0:T(8,128)S(1)} %collective-permute-done.7.refs_0_, f32[2,4,32,128]{3,2,1,0:T(8,128)S(1)} %collective-permute-done.8.refs_1_, f32[2,4,32,128]{3,2,1,0:T(8,128)S(1)} %collective-permute-done.9.refs_2_, ...), custom_call_target="tpu_custom_call" | custom-call | tf_op jit(solution)/shard_map/pallas_call | solution.py:327
  96.0 22.4 %all_to_all.10 = f32[64,16,128]{2,1,0:T(8,128)S(1)} all-to-all(f32[64,16,128]{2,1,0:T(8,128)S(1)} %bitcast.27), channel_id=1, replica_groups=mesh['seq'=64,'tp'=4] {'seq'}, dimensions={0} | all-to-all | bytes 1048576 | tf_op jit(solution)/shard_map/all_to_all | solution.py:400
  118.5 1.6 %shard_map.86 = f32[8,16384]{1,0:T(8,128)} custom-call(s32[5]{0:T(128)S(1)} %stack.23.place_ref, f32[1024,128]{1,0:T(8,128)S(1)} %bitcast.26), custom_call_target="tpu_custom_call" | custom-call | tf_op jit(solution)/shard_map/pallas_call | solution.py:357
Async XLA Ops:
  0.0 72.9 %copy-start.2 = (f32[64,128]{1,0:T(8,128)S(1)}, f32[64,128]{1,0:T(8,128)}, u32[]{:S(2)}) copy-start(f32[64,128]{1,0:T(8,128)} %constant.129.clone.refs_9_) | copy-start | bytes 98308
  0.0 72.9 %copy-start.1 = (bf16[256,512]{1,0:T(8,128)(2,1)S(1)}, bf16[256,512]{1,0:T(8,128)(2,1)}, u32[]{:S(2)}) copy-start(bf16[256,512]{1,0:T(8,128)(2,1)} %constant.128.clone.refs_8_) | copy-start | bytes 786436
  2.4 48.1 %all-to-all-start = ((f32[256,8,128]{2,1,0:T(8,128)}), f32[256,8,128]{2,1,0:T(8,128)S(1)}, u32[]{:S(2)}, u32[]{:S(2)}) async-start(f32[256,8,128]{2,1,0:T(8,128)} %bitcast.28), calls=%async_computation | async-start | bytes 2097152 | tf_op jit(solution)/shard_map/all_to_all | solution.py:390
  18.1 76.5 %copy-start = (bf16[256,1024]{1,0:T(8,128)(2,1)S(1)}, bf16[256,1024]{1,0:T(8,128)(2,1)}, u32[]{:S(2)}) copy-start(bf16[256,1024]{1,0:T(8,128)(2,1)} %constant.130.clone.refs_8_) | copy-start | bytes 1572868
  52.4 13.3 %collective-permute-start = (f32[2,2,4,32,128]{4,3,2,1,0:T(8,128)S(1)}, f32[2,2,4,32,128]{4,3,2,1,0:T(8,128)S(1)}, u32[]{:S(2)}, u32[]{:S(2)}) collective-permute-start(f32[2,2,4,32,128]{4,3,2,1,0:T(8,128)S(1)} %get-tuple-element.22), channel_id=1, source_target_pairs={{0,73},{1,72},{8,65},{9,64},{64,9},{65,8},{72,1},{73,0},{16,89},{1... | collective-permute-start | bytes 786440 | tf_op jit(solution)/shard_map/ppermute | solution.py:372
  53.5 13.0 %collective-permute-start.1 = (f32[2,2,4,32,128]{4,3,2,1,0:T(8,128)S(1)}, f32[2,2,4,32,128]{4,3,2,1,0:T(8,128)S(1)}, u32[]{:S(2)}, u32[]{:S(2)}) collective-permute-start(f32[2,2,4,32,128]{4,3,2,1,0:T(8,128)S(1)} %get-tuple-element.23), channel_id=1, source_target_pairs={{0,72},{1,73},{8,64},{9,65},{64,8},{65,9},{72,0},{73,1},{16,88},{1... | collective-permute-start | bytes 786440 | tf_op jit(solution)/shard_map/ppermute | solution.py:372
  57.0 14.2 %collective-permute-start.2 = (f32[2,2,4,32,128]{4,3,2,1,0:T(8,128)S(1)}, f32[2,2,4,32,128]{4,3,2,1,0:T(8,128)S(1)}, u32[]{:S(2)}, u32[]{:S(2)}) collective-permute-start(f32[2,2,4,32,128]{4,3,2,1,0:T(8,128)S(1)} %get-tuple-element.24), channel_id=1, source_target_pairs={{0,65},{1,64},{8,73},{9,72},{64,1},{65,0},{72,9},{73,8},{16,81},{1... | collective-permute-start | bytes 786440 | tf_op jit(solution)/shard_map/ppermute | solution.py:372
  59.9 11.3 %collective-permute-start.3 = (f32[2,2,4,32,128]{4,3,2,1,0:T(8,128)S(1)}, f32[2,2,4,32,128]{4,3,2,1,0:T(8,128)S(1)}, u32[]{:S(2)}, u32[]{:S(2)}) collective-permute-start(f32[2,2,4,32,128]{4,3,2,1,0:T(8,128)S(1)} %get-tuple-element.25), channel_id=1, source_target_pairs={{0,9},{1,8},{8,1},{9,0},{64,73},{65,72},{72,65},{73,64},{16,25},{1... | collective-permute-start | bytes 786440 | tf_op jit(solution)/shard_map/ppermute | solution.py:372
  60.7 10.9 %collective-permute-start.4 = (f32[2,2,4,32,128]{4,3,2,1,0:T(8,128)S(1)}, f32[2,2,4,32,128]{4,3,2,1,0:T(8,128)S(1)}, u32[]{:S(2)}, u32[]{:S(2)}) collective-permute-start(f32[2,2,4,32,128]{4,3,2,1,0:T(8,128)S(1)} %get-tuple-element.26), channel_id=1, source_target_pairs={{0,64},{1,65},{8,72},{9,73},{64,0},{65,1},{72,8},{73,9},{16,80},{1... | collective-permute-start | bytes 786440 | tf_op jit(solution)/shard_map/ppermute | solution.py:372
  65.7 6.4 %collective-permute-start.5 = (f32[2,2,4,32,128]{4,3,2,1,0:T(8,128)S(1)}, f32[2,2,4,32,128]{4,3,2,1,0:T(8,128)S(1)}, u32[]{:S(2)}, u32[]{:S(2)}) collective-permute-start(f32[2,2,4,32,128]{4,3,2,1,0:T(8,128)S(1)} %get-tuple-element.27), channel_id=1, source_target_pairs={{0,8},{1,9},{8,0},{9,1},{64,72},{65,73},{72,64},{73,65},{16,24},{1... | collective-permute-start | bytes 786440 | tf_op jit(solution)/shard_map/ppermute | solution.py:372
  66.5 6.4 %collective-permute-start.6 = (f32[2,2,4,32,128]{4,3,2,1,0:T(8,128)S(1)}, f32[2,2,4,32,128]{4,3,2,1,0:T(8,128)S(1)}, u32[]{:S(2)}, u32[]{:S(2)}) collective-permute-start(f32[2,2,4,32,128]{4,3,2,1,0:T(8,128)S(1)} %get-tuple-element.28), channel_id=1, source_target_pairs={{0,1},{1,0},{8,9},{9,8},{64,65},{65,64},{72,73},{73,72},{16,17},{1... | collective-permute-start | bytes 786440 | tf_op jit(solution)/shard_map/ppermute | solution.py:372
  76.7 7.7 %collective-permute-start.7 = (f32[2,4,32,128]{3,2,1,0:T(8,128)S(1)}, f32[2,4,32,128]{3,2,1,0:T(8,128)S(1)}, u32[]{:S(2)}, u32[]{:S(2)}) collective-permute-start(f32[2,4,32,128]{3,2,1,0:T(8,128)S(1)} %get-tuple-element.30), channel_id=1, source_target_pairs={{0,72},{1,76},{8,64},{9,68},{64,8},{65,12},{72,0},{73,4},{16,88},{... | collective-permute-start | bytes 393224 | tf_op jit(solution)/shard_map/ppermute | solution.py:372
  76.8 9.6 %collective-permute-start.8 = (f32[2,4,32,128]{3,2,1,0:T(8,128)S(1)}, f32[2,4,32,128]{3,2,1,0:T(8,128)S(1)}, u32[]{:S(2)}, u32[]{:S(2)}) collective-permute-start(f32[2,4,32,128]{3,2,1,0:T(8,128)S(1)} %get-tuple-element.31), channel_id=1, source_target_pairs={{0,76},{1,72},{8,68},{9,64},{64,12},{65,8},{72,4},{73,0},{16,92},{... | collective-permute-start | bytes 393224 | tf_op jit(solution)/shard_map/ppermute | solution.py:372
  82.0 8.6 %collective-permute-start.9 = (f32[2,4,32,128]{3,2,1,0:T(8,128)S(1)}, f32[2,4,32,128]{3,2,1,0:T(8,128)S(1)}, u32[]{:S(2)}, u32[]{:S(2)}) collective-permute-start(f32[2,4,32,128]{3,2,1,0:T(8,128)S(1)} %get-tuple-element.32), channel_id=1, source_target_pairs={{0,64},{1,68},{8,72},{9,76},{64,0},{65,4},{72,8},{73,12},{16,80},{... | collective-permute-start | bytes 393224 | tf_op jit(solution)/shard_map/ppermute | solution.py:372
  82.0 10.7 %collective-permute-start.10 = (f32[2,4,32,128]{3,2,1,0:T(8,128)S(1)}, f32[2,4,32,128]{3,2,1,0:T(8,128)S(1)}, u32[]{:S(2)}, u32[]{:S(2)}) collective-permute-start(f32[2,4,32,128]{3,2,1,0:T(8,128)S(1)} %get-tuple-element.33), channel_id=1, source_target_pairs={{0,68},{1,64},{8,76},{9,72},{64,4},{65,0},{72,12},{73,8},{16,84},{... | collective-permute-start | bytes 393224 | tf_op jit(solution)/shard_map/ppermute | solution.py:372
  83.8 8.9 %collective-permute-start.11 = (f32[2,4,32,128]{3,2,1,0:T(8,128)S(1)}, f32[2,4,32,128]{3,2,1,0:T(8,128)S(1)}, u32[]{:S(2)}, u32[]{:S(2)}) collective-permute-start(f32[2,4,32,128]{3,2,1,0:T(8,128)S(1)} %get-tuple-element.34), channel_id=1, source_target_pairs={{0,8},{1,12},{8,0},{9,4},{64,72},{65,76},{72,64},{73,68},{16,24},{... | collective-permute-start | bytes 393224 | tf_op jit(solution)/shard_map/ppermute | solution.py:372
  84.3 8.3 %collective-permute-start.12 = (f32[2,4,32,128]{3,2,1,0:T(8,128)S(1)}, f32[2,4,32,128]{3,2,1,0:T(8,128)S(1)}, u32[]{:S(2)}, u32[]{:S(2)}) collective-permute-start(f32[2,4,32,128]{3,2,1,0:T(8,128)S(1)} %get-tuple-element.35), channel_id=1, source_target_pairs={{0,12},{1,8},{8,4},{9,0},{64,76},{65,72},{72,68},{73,64},{16,28},{... | collective-permute-start | bytes 393224 | tf_op jit(solution)/shard_map/ppermute | solution.py:372
  86.4 6.3 %collective-permute-start.13 = (f32[2,4,32,128]{3,2,1,0:T(8,128)S(1)}, f32[2,4,32,128]{3,2,1,0:T(8,128)S(1)}, u32[]{:S(2)}, u32[]{:S(2)}) collective-permute-start(f32[2,4,32,128]{3,2,1,0:T(8,128)S(1)} %get-tuple-element.36), channel_id=1, source_target_pairs={{0,0},{1,4},{8,8},{9,12},{64,64},{65,68},{72,72},{73,76},{16,16},{... | collective-permute-start | bytes 393224 | tf_op jit(solution)/shard_map/ppermute | solution.py:372
  90.5 4.1 %collective-permute-start.14 = (f32[2,4,32,128]{3,2,1,0:T(8,128)S(1)}, f32[2,4,32,128]{3,2,1,0:T(8,128)S(1)}, u32[]{:S(2)}, u32[]{:S(2)}) collective-permute-start(f32[2,4,32,128]{3,2,1,0:T(8,128)S(1)} %get-tuple-element.37), channel_id=1, source_target_pairs={{0,4},{1,0},{8,12},{9,8},{64,68},{65,64},{72,76},{73,72},{16,20},{... | collective-permute-start | bytes 393224 | tf_op jit(solution)/shard_map/ppermute | solution.py:372

commit v6 on v5

--- a/solution.py
+++ b/solution.py
@@ -15,7 +15,7 @@
 LANES = 128
 AXES = ("seq", "tp")
 FLIPS = (7, 6, 5, 3, 4, 2, 1, 0)
-BACK_FLIPS = (6, 7, 4, 5, 2, 3, 0, 1)
+BACK_FLIPS = (6, 7, 2, 3, 4, 5, 0, 1)
 VMEM = pl.BlockSpec(memory_space=pltpu.VMEM)
 HBM = pl.BlockSpec(memory_space=pltpu.HBM)
 SMEM = pl.BlockSpec(memory_space=pltpu.SMEM)

time: 121 us -> 121 us (level)
  transfers between devices with their start and end apart: 16 -> 16, of which waited for: 10 -> 11; matrix products, arithmetic and copies ran while one was open for 3% -> 3% of each run, Pallas kernels for 0% -> 0%
where the time goes in v6:
time: 121 us; the launch traced here: 120 us
  waiting for transfers between devices  40.5 us (33%)
  starting transfers between devices  40.1 us (33%)
  blocking collectives  23.4 us (19%)
  Pallas kernels  11 us (9%)
  local copies, waits for them, and re-layouts  3.81 us (3%)
    all_to_all x1, waiting for transfers between devices, body(): lax.all_to_all(packed, AXES, split_axis=0, concat_axis=0, tiled=True)  27.8 us
    ppermute x15, starting transfers between devices, exchange(): lax.ppermute(part, AXES, pairs(flip))  24.5 us
    all_to_all x1, blocking collectives, body(): lax.all_to_all(result.reshape(64, 16, LANES), 'seq', split_axis=0, concat...  23.4 us
    all_to_all x1, starting transfers between devices, body(): lax.all_to_all(packed, AXES, split_axis=0, concat_axis=0, tiled=True)  15.7 us
    ppermute x15, waiting for transfers between devices, exchange(): lax.ppermute(part, AXES, pairs(flip))  12.7 us
    pallas_call x1, Pallas kernels, middle(): pl.pallas_call(middle_kernel, out_shape=[jax.ShapeDtypeStruct(block, jnp....  3.73 us
  transfers between devices with their start and end apart: 16, of which 11 were waited for; matrix products, arithmetic and copies ran while one was open for 3% of the time, Pallas kernels for 0%

profile of v6, /device:TPU:1, one launch (start us, length us, event | category | flops | bytes accessed | tf_op | source)
XLA Modules:
  0.0 119.9 jit_solution(10553312408571335908)
XLA Ops:
  0.0 0.0 copy-start.2
  0.0 0.0 copy-start.1
  0.0 2.3 %shard_map.82 = f32[32,2,4,8,128]{4,3,2,1,0:T(8,128)} custom-call(f32[1024,128]{1,0:T(8,128)} %bitcast.29, f32[1024,128]{1,0:T(8,128)} %bitcast.30), custom_call_target="tpu_custom_call" | custom-call | tf_op jit(solution)/shard_map/pallas_call | solution.py:173
  2.4 15.7 %all-to-all-start = ((f32[256,8,128]{2,1,0:T(8,128)}), f32[256,8,128]{2,1,0:T(8,128)S(1)}, u32[]{:S(2)}, u32[]{:S(2)}) async-start(f32[256,8,128]{2,1,0:T(8,128)} %bitcast.28), calls=%async_computation | async-start | bytes 2097152 | tf_op jit(solution)/shard_map/all_to_all | solution.py:390
  18.1 0.0 copy-start
  18.3 1.3 %dynamic_slice.11 = f32[1]{0:T(128)} dynamic-slice(f32[8]{0:T(128)} %param.10, s32[]{:T(128)S(6)} %select_n.85), dynamic_slice_sizes={1} | dynamic-slice | bytes 12 | tf_op jit(solution)/shard_map/dynamic_slice | solution.py:387
  20.2 0.1 stack.23.place_ref
  20.3 1.1 dynamic-slice_bitcast_fusion.1.ahead_ref
  21.4 1.3 %dynamic-slice_bitcast_fusion.turn_ref = f32[2,256,512]{2,1,0:T(8,128)S(1)} fusion(f32[8,2,256,512]{3,2,1,0:T(8,128)} %constant.126.clone.refs_10_, s32[]{:T(128)S(6)} %select_n.88), kind=kLoop, calls=%fused_computation | loop fusion | bytes 2097156 | tf_op jit(solution)/shard_map/jit(dynamic_index_in_dim)/squeeze | solution.py:394
  22.7 27.8 %all-to-all-done = f32[256,8,128]{2,1,0:T(8,128)S(1)} async-done(((f32[256,8,128]{2,1,0:T(8,128)}), f32[256,8,128]{2,1,0:T(8,128)S(1)}, u32[]{:S(2)}, u32[]{:S(2)}) %all-to-all-start) | async-done | bytes 1048608 | tf_op jit(solution)/shard_map/all_to_all | solution.py:390
  50.5 2.0 %shard_map.83 = (f32[2,2,4,32,128]{4,3,2,1,0:T(8,128)S(1)}, f32[2,2,4,32,128]{4,3,2,1,0:T(8,128)S(1)}, f32[2,2,4,32,128]{4,3,2,1,0:T(8,128)S(1)}, f32[2,2,4,32,1...) custom-call(s32[5]{0:T(128)S(1)} %stack.23.place_ref, ...), custom_call_target="tpu_custom_call" | custom-call | tf_op jit(solution)/shard_map/pallas_call | solution.py:224
  52.4 1.1 collective-permute-start
  53.5 3.5 %collective-permute-start.1 = (f32[2,2,4,32,128]{4,3,2,1,0:T(8,128)S(1)}, f32[2,2,4,32,128]{4,3,2,1,0:T(8,128)S(1)}, u32[]{:S(2)}, u32[]{:S(2)}) collective-permute-start(f32[2,2,4,32,128]{4,3,2,1,0:T(8,128)S(1)} %get-tuple-element.23), channel_id=1, source_target_pairs={{0,72},{1,73},{8,64},{9,65},{64,8},{65,9},{72,0},{73,1},{16,88},{1... | collective-permute-start | bytes 786440 | tf_op jit(solution)/shard_map/ppermute | solution.py:372
  57.0 2.9 %collective-permute-start.2 = (f32[2,2,4,32,128]{4,3,2,1,0:T(8,128)S(1)}, f32[2,2,4,32,128]{4,3,2,1,0:T(8,128)S(1)}, u32[]{:S(2)}, u32[]{:S(2)}) collective-permute-start(f32[2,2,4,32,128]{4,3,2,1,0:T(8,128)S(1)} %get-tuple-element.24), channel_id=1, source_target_pairs={{0,65},{1,64},{8,73},{9,72},{64,1},{65,0},{72,9},{73,8},{16,81},{1... | collective-permute-start | bytes 786440 | tf_op jit(solution)/shard_map/ppermute | solution.py:372
  59.9 0.8 collective-permute-start.3
  60.7 1.6 %collective-permute-start.4 = (f32[2,2,4,32,128]{4,3,2,1,0:T(8,128)S(1)}, f32[2,2,4,32,128]{4,3,2,1,0:T(8,128)S(1)}, u32[]{:S(2)}, u32[]{:S(2)}) collective-permute-start(f32[2,2,4,32,128]{4,3,2,1,0:T(8,128)S(1)} %get-tuple-element.26), channel_id=1, source_target_pairs={{0,64},{1,65},{8,72},{9,73},{64,0},{65,1},{72,8},{73,9},{16,80},{1... | collective-permute-start | bytes 786440 | tf_op jit(solution)/shard_map/ppermute | solution.py:372
  62.3 3.4 %collective-permute-done.refs_0_ = f32[2,2,4,32,128]{4,3,2,1,0:T(8,128)S(1)} collective-permute-done((f32[2,2,4,32,128]{4,3,2,1,0:T(8,128)S(1)}, f32[2,2,4,32,128]{4,3,2,1,0:T(8,128)S(1)}, u32[]{:S(2)}, u32[]{:S(2)}) %collective-permute-start) | collective-permute-done | bytes 262176 | tf_op jit(solution)/shard_map/ppermute | solution.py:372
  65.7 0.0 collective-permute-start.5
  65.7 0.8 collective-permute-done.1.refs_1_
  66.5 0.7 collective-permute-start.6
  67.2 4.0 %collective-permute-done.2.refs_2_ = f32[2,2,4,32,128]{4,3,2,1,0:T(8,128)S(1)} collective-permute-done((f32[2,2,4,32,128]{4,3,2,1,0:T(8,128)S(1)}, f32[2,2,4,32,128]{4,3,2,1,0:T(8,128)S(1)}, u32[]{:S(2)}, u32[]{:S(2)}) %collective-permute-start.2) | collective-permute-done | bytes 262176 | tf_op jit(solution)/shard_map/ppermute | solution.py:372
  71.2 0.0 collective-permute-done.3.refs_3_
  71.2 0.4 collective-permute-done.4.refs_4_
  71.6 0.6 collective-permute-done.5.refs_5_
  72.2 0.8 collective-permute-done.6.refs_6_
  72.9 0.0 copy-done.2
  72.9 0.0 copy-done.1
  72.9 3.7 %shard_map.84 = (f32[2,4,32,128]{3,2,1,0:T(8,128)S(1)}, f32[2,4,32,128]{3,2,1,0:T(8,128)S(1)}, f32[2,4,32,128]{3,2,1,0:T(8,128)S(1)}, f32[2,4,32,128]{3,2,1,0:T(...) custom-call(s32[5]{0:T(128)S(1)} %stack.23.place_ref, ...), custom_call_target="tpu_custom_call" | custom-call | tf_op jit(solution)/shard_map/pallas_call | solution.py:289
  76.7 0.1 collective-permute-start.7
  76.8 5.2 %collective-permute-start.8 = (f32[2,4,32,128]{3,2,1,0:T(8,128)S(1)}, f32[2,4,32,128]{3,2,1,0:T(8,128)S(1)}, u32[]{:S(2)}, u32[]{:S(2)}) collective-permute-start(f32[2,4,32,128]{3,2,1,0:T(8,128)S(1)} %get-tuple-element.31), channel_id=1, source_target_pairs={{0,76},{1,72},{8,68},{9,64},{64,12},{65,8},{72,4},{73,0},{16,92},{... | collective-permute-start | bytes 393224 | tf_op jit(solution)/shard_map/ppermute | solution.py:372
  82.0 0.0 collective-permute-start.9
  82.0 1.8 %collective-permute-start.10 = (f32[2,4,32,128]{3,2,1,0:T(8,128)S(1)}, f32[2,4,32,128]{3,2,1,0:T(8,128)S(1)}, u32[]{:S(2)}, u32[]{:S(2)}) collective-permute-start(f32[2,4,32,128]{3,2,1,0:T(8,128)S(1)} %get-tuple-element.33), channel_id=1, source_target_pairs={{0,12},{1,8},{8,4},{9,0},{64,76},{65,72},{72,68},{73,64},{16,28},{... | collective-permute-start | bytes 393224 | tf_op jit(solution)/shard_map/ppermute | solution.py:372
  83.8 0.0 collective-permute-start.11
  83.8 0.5 collective-permute-done.7.refs_0_
  84.3 0.6 collective-permute-start.12
  84.8 0.3 collective-permute-done.8.refs_1_
  85.1 4.8 %collective-permute-start.13 = (f32[2,4,32,128]{3,2,1,0:T(8,128)S(1)}, f32[2,4,32,128]{3,2,1,0:T(8,128)S(1)}, u32[]{:S(2)}, u32[]{:S(2)}) collective-permute-start(f32[2,4,32,128]{3,2,1,0:T(8,128)S(1)} %get-tuple-element.36), channel_id=1, source_target_pairs={{0,0},{1,4},{8,8},{9,12},{64,64},{65,68},{72,72},{73,76},{16,16},{... | collective-permute-start | bytes 393224 | tf_op jit(solution)/shard_map/ppermute | solution.py:372
  90.0 0.0 collective-permute-done.9.refs_2_
  90.0 1.4 %collective-permute-start.14 = (f32[2,4,32,128]{3,2,1,0:T(8,128)S(1)}, f32[2,4,32,128]{3,2,1,0:T(8,128)S(1)}, u32[]{:S(2)}, u32[]{:S(2)}) collective-permute-start(f32[2,4,32,128]{3,2,1,0:T(8,128)S(1)} %get-tuple-element.37), channel_id=1, source_target_pairs={{0,4},{1,0},{8,12},{9,8},{64,68},{65,64},{72,76},{73,72},{16,20},{... | collective-permute-start | bytes 393224 | tf_op jit(solution)/shard_map/ppermute | solution.py:372
  91.4 0.0 collective-permute-done.10.refs_3_
  91.4 0.0 collective-permute-done.11.refs_4_
  91.4 0.0 collective-permute-done.12.refs_5_
  91.4 0.6 collective-permute-done.13.refs_6_
  92.0 1.4 %collective-permute-done.14.refs_7_ = f32[2,4,32,128]{3,2,1,0:T(8,128)S(1)} collective-permute-done((f32[2,4,32,128]{3,2,1,0:T(8,128)S(1)}, f32[2,4,32,128]{3,2,1,0:T(8,128)S(1)}, u32[]{:S(2)}, u32[]{:S(2)}) %collective-permute-start.14) | collective-permute-done | bytes 131104 | tf_op jit(solution)/shard_map/ppermute | solution.py:372
  93.4 0.0 copy-done
  93.4 1.4 %shard_map.85 = f32[1024,128]{1,0:T(8,128)S(1)} custom-call(s32[5]{0:T(128)S(1)} %stack.23.place_ref, f32[2,4,32,128]{3,2,1,0:T(8,128)S(1)} %collective-permute-done.7.refs_0_, f32[2,4,32,128]{3,2,1,0:T(8,128)S(1)} %collective-permute-done.8.refs_1_, f32[2,4,32,128]{3,2,1,0:T(8,128)S(1)} %collective-permute-done.9.refs_2_, ...), custom_call_target="tpu_custom_call" | custom-call | tf_op jit(solution)/shard_map/pallas_call | solution.py:327
  94.8 23.4 %all_to_all.10 = f32[64,16,128]{2,1,0:T(8,128)S(1)} all-to-all(f32[64,16,128]{2,1,0:T(8,128)S(1)} %bitcast.27), channel_id=1, replica_groups=mesh['seq'=64,'tp'=4] {'seq'}, dimensions={0} | all-to-all | bytes 1048576 | tf_op jit(solution)/shard_map/all_to_all | solution.py:400
  118.2 1.6 %shard_map.86 = f32[8,16384]{1,0:T(8,128)} custom-call(s32[5]{0:T(128)S(1)} %stack.23.place_ref, f32[1024,128]{1,0:T(8,128)S(1)} %bitcast.26), custom_call_target="tpu_custom_call" | custom-call | tf_op jit(solution)/shard_map/pallas_call | solution.py:357
Async XLA Ops:
  0.0 72.9 %copy-start.2 = (f32[64,128]{1,0:T(8,128)S(1)}, f32[64,128]{1,0:T(8,128)}, u32[]{:S(2)}) copy-start(f32[64,128]{1,0:T(8,128)} %constant.129.clone.refs_9_) | copy-start | bytes 98308
  0.0 72.9 %copy-start.1 = (bf16[256,512]{1,0:T(8,128)(2,1)S(1)}, bf16[256,512]{1,0:T(8,128)(2,1)}, u32[]{:S(2)}) copy-start(bf16[256,512]{1,0:T(8,128)(2,1)} %constant.128.clone.refs_8_) | copy-start | bytes 786436
  2.4 48.1 %all-to-all-start = ((f32[256,8,128]{2,1,0:T(8,128)}), f32[256,8,128]{2,1,0:T(8,128)S(1)}, u32[]{:S(2)}, u32[]{:S(2)}) async-start(f32[256,8,128]{2,1,0:T(8,128)} %bitcast.28), calls=%async_computation | async-start | bytes 2097152 | tf_op jit(solution)/shard_map/all_to_all | solution.py:390
  18.1 75.3 %copy-start = (bf16[256,1024]{1,0:T(8,128)(2,1)S(1)}, bf16[256,1024]{1,0:T(8,128)(2,1)}, u32[]{:S(2)}) copy-start(bf16[256,1024]{1,0:T(8,128)(2,1)} %constant.130.clone.refs_8_) | copy-start | bytes 1572868
  52.4 13.3 %collective-permute-start = (f32[2,2,4,32,128]{4,3,2,1,0:T(8,128)S(1)}, f32[2,2,4,32,128]{4,3,2,1,0:T(8,128)S(1)}, u32[]{:S(2)}, u32[]{:S(2)}) collective-permute-start(f32[2,2,4,32,128]{4,3,2,1,0:T(8,128)S(1)} %get-tuple-element.22), channel_id=1, source_target_pairs={{0,73},{1,72},{8,65},{9,64},{64,9},{65,8},{72,1},{73,0},{16,89},{1... | collective-permute-start | bytes 786440 | tf_op jit(solution)/shard_map/ppermute | solution.py:372
  53.5 13.0 %collective-permute-start.1 = (f32[2,2,4,32,128]{4,3,2,1,0:T(8,128)S(1)}, f32[2,2,4,32,128]{4,3,2,1,0:T(8,128)S(1)}, u32[]{:S(2)}, u32[]{:S(2)}) collective-permute-start(f32[2,2,4,32,128]{4,3,2,1,0:T(8,128)S(1)} %get-tuple-element.23), channel_id=1, source_target_pairs={{0,72},{1,73},{8,64},{9,65},{64,8},{65,9},{72,0},{73,1},{16,88},{1... | collective-permute-start | bytes 786440 | tf_op jit(solution)/shard_map/ppermute | solution.py:372
  57.0 14.2 %collective-permute-start.2 = (f32[2,2,4,32,128]{4,3,2,1,0:T(8,128)S(1)}, f32[2,2,4,32,128]{4,3,2,1,0:T(8,128)S(1)}, u32[]{:S(2)}, u32[]{:S(2)}) collective-permute-start(f32[2,2,4,32,128]{4,3,2,1,0:T(8,128)S(1)} %get-tuple-element.24), channel_id=1, source_target_pairs={{0,65},{1,64},{8,73},{9,72},{64,1},{65,0},{72,9},{73,8},{16,81},{1... | collective-permute-start | bytes 786440 | tf_op jit(solution)/shard_map/ppermute | solution.py:372
  59.9 11.3 %collective-permute-start.3 = (f32[2,2,4,32,128]{4,3,2,1,0:T(8,128)S(1)}, f32[2,2,4,32,128]{4,3,2,1,0:T(8,128)S(1)}, u32[]{:S(2)}, u32[]{:S(2)}) collective-permute-start(f32[2,2,4,32,128]{4,3,2,1,0:T(8,128)S(1)} %get-tuple-element.25), channel_id=1, source_target_pairs={{0,9},{1,8},{8,1},{9,0},{64,73},{65,72},{72,65},{73,64},{16,25},{1... | collective-permute-start | bytes 786440 | tf_op jit(solution)/shard_map/ppermute | solution.py:372
  60.7 10.9 %collective-permute-start.4 = (f32[2,2,4,32,128]{4,3,2,1,0:T(8,128)S(1)}, f32[2,2,4,32,128]{4,3,2,1,0:T(8,128)S(1)}, u32[]{:S(2)}, u32[]{:S(2)}) collective-permute-start(f32[2,2,4,32,128]{4,3,2,1,0:T(8,128)S(1)} %get-tuple-element.26), channel_id=1, source_target_pairs={{0,64},{1,65},{8,72},{9,73},{64,0},{65,1},{72,8},{73,9},{16,80},{1... | collective-permute-start | bytes 786440 | tf_op jit(solution)/shard_map/ppermute | solution.py:372
  65.7 6.4 %collective-permute-start.5 = (f32[2,2,4,32,128]{4,3,2,1,0:T(8,128)S(1)}, f32[2,2,4,32,128]{4,3,2,1,0:T(8,128)S(1)}, u32[]{:S(2)}, u32[]{:S(2)}) collective-permute-start(f32[2,2,4,32,128]{4,3,2,1,0:T(8,128)S(1)} %get-tuple-element.27), channel_id=1, source_target_pairs={{0,8},{1,9},{8,0},{9,1},{64,72},{65,73},{72,64},{73,65},{16,24},{1... | collective-permute-start | bytes 786440 | tf_op jit(solution)/shard_map/ppermute | solution.py:372
  66.5 6.4 %collective-permute-start.6 = (f32[2,2,4,32,128]{4,3,2,1,0:T(8,128)S(1)}, f32[2,2,4,32,128]{4,3,2,1,0:T(8,128)S(1)}, u32[]{:S(2)}, u32[]{:S(2)}) collective-permute-start(f32[2,2,4,32,128]{4,3,2,1,0:T(8,128)S(1)} %get-tuple-element.28), channel_id=1, source_target_pairs={{0,1},{1,0},{8,9},{9,8},{64,65},{65,64},{72,73},{73,72},{16,17},{1... | collective-permute-start | bytes 786440 | tf_op jit(solution)/shard_map/ppermute | solution.py:372
  76.7 7.6 %collective-permute-start.7 = (f32[2,4,32,128]{3,2,1,0:T(8,128)S(1)}, f32[2,4,32,128]{3,2,1,0:T(8,128)S(1)}, u32[]{:S(2)}, u32[]{:S(2)}) collective-permute-start(f32[2,4,32,128]{3,2,1,0:T(8,128)S(1)} %get-tuple-element.30), channel_id=1, source_target_pairs={{0,72},{1,76},{8,64},{9,68},{64,8},{65,12},{72,0},{73,4},{16,88},{... | collective-permute-start | bytes 393224 | tf_op jit(solution)/shard_map/ppermute | solution.py:372
  76.8 8.4 %collective-permute-start.8 = (f32[2,4,32,128]{3,2,1,0:T(8,128)S(1)}, f32[2,4,32,128]{3,2,1,0:T(8,128)S(1)}, u32[]{:S(2)}, u32[]{:S(2)}) collective-permute-start(f32[2,4,32,128]{3,2,1,0:T(8,128)S(1)} %get-tuple-element.31), channel_id=1, source_target_pairs={{0,76},{1,72},{8,68},{9,64},{64,12},{65,8},{72,4},{73,0},{16,92},{... | collective-permute-start | bytes 393224 | tf_op jit(solution)/shard_map/ppermute | solution.py:372
  82.0 8.0 %collective-permute-start.9 = (f32[2,4,32,128]{3,2,1,0:T(8,128)S(1)}, f32[2,4,32,128]{3,2,1,0:T(8,128)S(1)}, u32[]{:S(2)}, u32[]{:S(2)}) collective-permute-start(f32[2,4,32,128]{3,2,1,0:T(8,128)S(1)} %get-tuple-element.32), channel_id=1, source_target_pairs={{0,8},{1,12},{8,0},{9,4},{64,72},{65,76},{72,64},{73,68},{16,24},{... | collective-permute-start | bytes 393224 | tf_op jit(solution)/shard_map/ppermute | solution.py:372
  82.0 9.5 %collective-permute-start.10 = (f32[2,4,32,128]{3,2,1,0:T(8,128)S(1)}, f32[2,4,32,128]{3,2,1,0:T(8,128)S(1)}, u32[]{:S(2)}, u32[]{:S(2)}) collective-permute-start(f32[2,4,32,128]{3,2,1,0:T(8,128)S(1)} %get-tuple-element.33), channel_id=1, source_target_pairs={{0,12},{1,8},{8,4},{9,0},{64,76},{65,72},{72,68},{73,64},{16,28},{... | collective-permute-start | bytes 393224 | tf_op jit(solution)/shard_map/ppermute | solution.py:372
  83.8 7.7 %collective-permute-start.11 = (f32[2,4,32,128]{3,2,1,0:T(8,128)S(1)}, f32[2,4,32,128]{3,2,1,0:T(8,128)S(1)}, u32[]{:S(2)}, u32[]{:S(2)}) collective-permute-start(f32[2,4,32,128]{3,2,1,0:T(8,128)S(1)} %get-tuple-element.34), channel_id=1, source_target_pairs={{0,64},{1,68},{8,72},{9,76},{64,0},{65,4},{72,8},{73,12},{16,80},{... | collective-permute-start | bytes 393224 | tf_op jit(solution)/shard_map/ppermute | solution.py:372
  84.3 7.2 %collective-permute-start.12 = (f32[2,4,32,128]{3,2,1,0:T(8,128)S(1)}, f32[2,4,32,128]{3,2,1,0:T(8,128)S(1)}, u32[]{:S(2)}, u32[]{:S(2)}) collective-permute-start(f32[2,4,32,128]{3,2,1,0:T(8,128)S(1)} %get-tuple-element.35), channel_id=1, source_target_pairs={{0,68},{1,64},{8,76},{9,72},{64,4},{65,0},{72,12},{73,8},{16,84},{... | collective-permute-start | bytes 393224 | tf_op jit(solution)/shard_map/ppermute | solution.py:372
  85.1 6.9 %collective-permute-start.13 = (f32[2,4,32,128]{3,2,1,0:T(8,128)S(1)}, f32[2,4,32,128]{3,2,1,0:T(8,128)S(1)}, u32[]{:S(2)}, u32[]{:S(2)}) collective-permute-start(f32[2,4,32,128]{3,2,1,0:T(8,128)S(1)} %get-tuple-element.36), channel_id=1, source_target_pairs={{0,0},{1,4},{8,8},{9,12},{64,64},{65,68},{72,72},{73,76},{16,16},{... | collective-permute-start | bytes 393224 | tf_op jit(solution)/shard_map/ppermute | solution.py:372
  90.0 3.4 %collective-permute-start.14 = (f32[2,4,32,128]{3,2,1,0:T(8,128)S(1)}, f32[2,4,32,128]{3,2,1,0:T(8,128)S(1)}, u32[]{:S(2)}, u32[]{:S(2)}) collective-permute-start(f32[2,4,32,128]{3,2,1,0:T(8,128)S(1)} %get-tuple-element.37), channel_id=1, source_target_pairs={{0,4},{1,0},{8,12},{9,8},{64,68},{65,64},{72,76},{73,72},{16,20},{... | collective-permute-start | bytes 393224 | tf_op jit(solution)/shard_map/ppermute | solution.py:372

commit v7 on v6

--- a/solution.py
+++ b/solution.py
@@ -15,7 +15,7 @@
 LANES = 128
 AXES = ("seq", "tp")
 FLIPS = (7, 6, 5, 3, 4, 2, 1, 0)
-BACK_FLIPS = (6, 7, 2, 3, 4, 5, 0, 1)
+BACK_FLIPS = (7, 6, 5, 4, 3, 2, 1, 0)
 VMEM = pl.BlockSpec(memory_space=pltpu.VMEM)
 HBM = pl.BlockSpec(memory_space=pltpu.HBM)
 SMEM = pl.BlockSpec(memory_space=pltpu.SMEM)

time: 121 us -> 121 us (level)
  waiting for transfers between devices: 40.5 us -> 45.6 us
  starting transfers between devices: 40.1 us -> 37.4 us
  blocking collectives: 23.4 us -> 21.4 us
    ppermute x15, waiting for transfers between devices: 12.7 us -> 17.8 us  [exchange(): lax.ppermute(part, AXES, pairs(flip))]
    ppermute x15, starting transfers between devices: 24.5 us -> 21.8 us  [exchange(): lax.ppermute(part, AXES, pairs(flip))]
    all_to_all x1, blocking collectives: 23.4 us -> 21.4 us  [body(): lax.all_to_all(result.reshape(64, 16, LANES), 'seq', split_axis=0, concat...]
where the time goes in v7:
time: 121 us; the launch traced here: 120 us
  waiting for transfers between devices  45.6 us (38%)
  starting transfers between devices  37.4 us (31%)
  blocking collectives  21.4 us (18%)
  Pallas kernels  11 us (9%)
  local copies, waits for them, and re-layouts  3.81 us (3%)
    all_to_all x1, waiting for transfers between devices, body(): lax.all_to_all(packed, AXES, split_axis=0, concat_axis=0, tiled=True)  27.8 us
    ppermute x15, starting transfers between devices, exchange(): lax.ppermute(part, AXES, pairs(flip))  21.8 us
    all_to_all x1, blocking collectives, body(): lax.all_to_all(result.reshape(64, 16, LANES), 'seq', split_axis=0, concat...  21.4 us
    ppermute x15, waiting for transfers between devices, exchange(): lax.ppermute(part, AXES, pairs(flip))  17.8 us
    all_to_all x1, starting transfers between devices, body(): lax.all_to_all(packed, AXES, split_axis=0, concat_axis=0, tiled=True)  15.7 us
    pallas_call x1, Pallas kernels, middle(): pl.pallas_call(middle_kernel, out_shape=[jax.ShapeDtypeStruct(block, jnp....  3.73 us
  transfers between devices with their start and end apart: 16, of which 11 were waited for; matrix products, arithmetic and copies ran while one was open for 3% of the time, Pallas kernels for 0%

profile of v7, /device:TPU:1, one launch (start us, length us, event | category | flops | bytes accessed | tf_op | source)
XLA Modules:
  0.0 120.4 jit_solution(17654388434333851147)
XLA Ops:
  0.0 0.0 copy-start.2
  0.0 0.0 copy-start.1
  0.0 2.3 %shard_map.82 = f32[32,2,4,8,128]{4,3,2,1,0:T(8,128)} custom-call(f32[1024,128]{1,0:T(8,128)} %bitcast.29, f32[1024,128]{1,0:T(8,128)} %bitcast.30), custom_call_target="tpu_custom_call" | custom-call | tf_op jit(solution)/shard_map/pallas_call | solution.py:173
  2.4 15.7 %all-to-all-start = ((f32[256,8,128]{2,1,0:T(8,128)}), f32[256,8,128]{2,1,0:T(8,128)S(1)}, u32[]{:S(2)}, u32[]{:S(2)}) async-start(f32[256,8,128]{2,1,0:T(8,128)} %bitcast.28), calls=%async_computation | async-start | bytes 2097152 | tf_op jit(solution)/shard_map/all_to_all | solution.py:390
  18.1 0.0 copy-start
  18.3 1.3 %dynamic_slice.11 = f32[1]{0:T(128)} dynamic-slice(f32[8]{0:T(128)} %param.10, s32[]{:T(128)S(6)} %select_n.85), dynamic_slice_sizes={1} | dynamic-slice | bytes 12 | tf_op jit(solution)/shard_map/dynamic_slice | solution.py:387
  20.2 0.1 stack.23.place_ref
  20.3 1.1 dynamic-slice_bitcast_fusion.1.ahead_ref
  21.4 1.3 %dynamic-slice_bitcast_fusion.turn_ref = f32[2,256,512]{2,1,0:T(8,128)S(1)} fusion(f32[8,2,256,512]{3,2,1,0:T(8,128)} %constant.126.clone.refs_10_, s32[]{:T(128)S(6)} %select_n.88), kind=kLoop, calls=%fused_computation | loop fusion | bytes 2097156 | tf_op jit(solution)/shard_map/jit(dynamic_index_in_dim)/squeeze | solution.py:394
  22.7 27.8 %all-to-all-done = f32[256,8,128]{2,1,0:T(8,128)S(1)} async-done(((f32[256,8,128]{2,1,0:T(8,128)}), f32[256,8,128]{2,1,0:T(8,128)S(1)}, u32[]{:S(2)}, u32[]{:S(2)}) %all-to-all-start) | async-done | bytes 1048608 | tf_op jit(solution)/shard_map/all_to_all | solution.py:390
  50.5 2.0 %shard_map.83 = (f32[2,2,4,32,128]{4,3,2,1,0:T(8,128)S(1)}, f32[2,2,4,32,128]{4,3,2,1,0:T(8,128)S(1)}, f32[2,2,4,32,128]{4,3,2,1,0:T(8,128)S(1)}, f32[2,2,4,32,1...) custom-call(s32[5]{0:T(128)S(1)} %stack.23.place_ref, ...), custom_call_target="tpu_custom_call" | custom-call | tf_op jit(solution)/shard_map/pallas_call | solution.py:224
  52.4 1.1 collective-permute-start
  53.5 3.5 %collective-permute-start.1 = (f32[2,2,4,32,128]{4,3,2,1,0:T(8,128)S(1)}, f32[2,2,4,32,128]{4,3,2,1,0:T(8,128)S(1)}, u32[]{:S(2)}, u32[]{:S(2)}) collective-permute-start(f32[2,2,4,32,128]{4,3,2,1,0:T(8,128)S(1)} %get-tuple-element.23), channel_id=1, source_target_pairs={{0,72},{1,73},{8,64},{9,65},{64,8},{65,9},{72,0},{73,1},{16,88},{1... | collective-permute-start | bytes 786440 | tf_op jit(solution)/shard_map/ppermute | solution.py:372
  57.0 2.9 %collective-permute-start.2 = (f32[2,2,4,32,128]{4,3,2,1,0:T(8,128)S(1)}, f32[2,2,4,32,128]{4,3,2,1,0:T(8,128)S(1)}, u32[]{:S(2)}, u32[]{:S(2)}) collective-permute-start(f32[2,2,4,32,128]{4,3,2,1,0:T(8,128)S(1)} %get-tuple-element.24), channel_id=1, source_target_pairs={{0,65},{1,64},{8,73},{9,72},{64,1},{65,0},{72,9},{73,8},{16,81},{1... | collective-permute-start | bytes 786440 | tf_op jit(solution)/shard_map/ppermute | solution.py:372
  59.9 0.8 collective-permute-start.3
  60.7 1.6 %collective-permute-start.4 = (f32[2,2,4,32,128]{4,3,2,1,0:T(8,128)S(1)}, f32[2,2,4,32,128]{4,3,2,1,0:T(8,128)S(1)}, u32[]{:S(2)}, u32[]{:S(2)}) collective-permute-start(f32[2,2,4,32,128]{4,3,2,1,0:T(8,128)S(1)} %get-tuple-element.26), channel_id=1, source_target_pairs={{0,64},{1,65},{8,72},{9,73},{64,0},{65,1},{72,8},{73,9},{16,80},{1... | collective-permute-start | bytes 786440 | tf_op jit(solution)/shard_map/ppermute | solution.py:372
  62.3 3.4 %collective-permute-done.refs_0_ = f32[2,2,4,32,128]{4,3,2,1,0:T(8,128)S(1)} collective-permute-done((f32[2,2,4,32,128]{4,3,2,1,0:T(8,128)S(1)}, f32[2,2,4,32,128]{4,3,2,1,0:T(8,128)S(1)}, u32[]{:S(2)}, u32[]{:S(2)}) %collective-permute-start) | collective-permute-done | bytes 262176 | tf_op jit(solution)/shard_map/ppermute | solution.py:372
  65.7 0.0 collective-permute-start.5
  65.7 0.8 collective-permute-done.1.refs_1_
  66.5 0.7 collective-permute-start.6
  67.2 4.0 %collective-permute-done.2.refs_2_ = f32[2,2,4,32,128]{4,3,2,1,0:T(8,128)S(1)} collective-permute-done((f32[2,2,4,32,128]{4,3,2,1,0:T(8,128)S(1)}, f32[2,2,4,32,128]{4,3,2,1,0:T(8,128)S(1)}, u32[]{:S(2)}, u32[]{:S(2)}) %collective-permute-start.2) | collective-permute-done | bytes 262176 | tf_op jit(solution)/shard_map/ppermute | solution.py:372
  71.2 0.0 collective-permute-done.3.refs_3_
  71.2 0.4 collective-permute-done.4.refs_4_
  71.6 0.6 collective-permute-done.5.refs_5_
  72.2 0.8 collective-permute-done.6.refs_6_
  72.9 0.0 copy-done.2
  72.9 0.0 copy-done.1
  72.9 3.7 %shard_map.84 = (f32[2,4,32,128]{3,2,1,0:T(8,128)S(1)}, f32[2,4,32,128]{3,2,1,0:T(8,128)S(1)}, f32[2,4,32,128]{3,2,1,0:T(8,128)S(1)}, f32[2,4,32,128]{3,2,1,0:T(...) custom-call(s32[5]{0:T(128)S(1)} %stack.23.place_ref, ...), custom_call_target="tpu_custom_call" | custom-call | tf_op jit(solution)/shard_map/pallas_call | solution.py:289
  76.7 4.4 %collective-permute-start.7 = (f32[2,4,32,128]{3,2,1,0:T(8,128)S(1)}, f32[2,4,32,128]{3,2,1,0:T(8,128)S(1)}, u32[]{:S(2)}, u32[]{:S(2)}) collective-permute-start(f32[2,4,32,128]{3,2,1,0:T(8,128)S(1)} %get-tuple-element.30), channel_id=1, source_target_pairs={{0,76},{1,72},{8,68},{9,64},{64,12},{65,8},{72,4},{73,0},{16,92},{... | collective-permute-start | bytes 393224 | tf_op jit(solution)/shard_map/ppermute | solution.py:372
  81.1 0.0 collective-permute-start.8
  81.1 0.8 collective-permute-start.9
  81.9 0.0 collective-permute-start.10
  81.9 0.4 collective-permute-start.11
  82.3 0.7 collective-permute-done.7.refs_0_
  83.0 0.5 collective-permute-start.12
  83.6 4.2 %collective-permute-done.8.refs_1_ = f32[2,4,32,128]{3,2,1,0:T(8,128)S(1)} collective-permute-done((f32[2,4,32,128]{3,2,1,0:T(8,128)S(1)}, f32[2,4,32,128]{3,2,1,0:T(8,128)S(1)}, u32[]{:S(2)}, u32[]{:S(2)}) %collective-permute-start.8) | collective-permute-done | bytes 131104 | tf_op jit(solution)/shard_map/ppermute | solution.py:372
  87.8 0.9 collective-permute-start.13
  88.7 0.6 collective-permute-done.9.refs_2_
  89.3 4.1 %collective-permute-start.14 = (f32[2,4,32,128]{3,2,1,0:T(8,128)S(1)}, f32[2,4,32,128]{3,2,1,0:T(8,128)S(1)}, u32[]{:S(2)}, u32[]{:S(2)}) collective-permute-start(f32[2,4,32,128]{3,2,1,0:T(8,128)S(1)} %get-tuple-element.37), channel_id=1, source_target_pairs={{0,0},{1,4},{8,8},{9,12},{64,64},{65,68},{72,72},{73,76},{16,16},{... | collective-permute-start | bytes 393224 | tf_op jit(solution)/shard_map/ppermute | solution.py:372
  93.4 0.0 collective-permute-done.10.refs_3_
  93.4 0.0 collective-permute-done.11.refs_4_
  93.4 0.0 collective-permute-done.12.refs_5_
  93.4 0.0 collective-permute-done.13.refs_6_
  93.4 2.4 %collective-permute-done.14.refs_7_ = f32[2,4,32,128]{3,2,1,0:T(8,128)S(1)} collective-permute-done((f32[2,4,32,128]{3,2,1,0:T(8,128)S(1)}, f32[2,4,32,128]{3,2,1,0:T(8,128)S(1)}, u32[]{:S(2)}, u32[]{:S(2)}) %collective-permute-start.14) | collective-permute-done | bytes 131104 | tf_op jit(solution)/shard_map/ppermute | solution.py:372
  95.8 0.0 copy-done
  95.8 1.4 %shard_map.85 = f32[1024,128]{1,0:T(8,128)S(1)} custom-call(s32[5]{0:T(128)S(1)} %stack.23.place_ref, f32[2,4,32,128]{3,2,1,0:T(8,128)S(1)} %collective-permute-done.7.refs_0_, f32[2,4,32,128]{3,2,1,0:T(8,128)S(1)} %collective-permute-done.8.refs_1_, f32[2,4,32,128]{3,2,1,0:T(8,128)S(1)} %collective-permute-done.9.refs_2_, ...), custom_call_target="tpu_custom_call" | custom-call | tf_op jit(solution)/shard_map/pallas_call | solution.py:327
  97.2 21.4 %all_to_all.10 = f32[64,16,128]{2,1,0:T(8,128)S(1)} all-to-all(f32[64,16,128]{2,1,0:T(8,128)S(1)} %bitcast.27), channel_id=1, replica_groups=mesh['seq'=64,'tp'=4] {'seq'}, dimensions={0} | all-to-all | bytes 1048576 | tf_op jit(solution)/shard_map/all_to_all | solution.py:400
  118.7 1.6 %shard_map.86 = f32[8,16384]{1,0:T(8,128)} custom-call(s32[5]{0:T(128)S(1)} %stack.23.place_ref, f32[1024,128]{1,0:T(8,128)S(1)} %bitcast.26), custom_call_target="tpu_custom_call" | custom-call | tf_op jit(solution)/shard_map/pallas_call | solution.py:357
Async XLA Ops:
  0.0 72.9 %copy-start.2 = (f32[64,128]{1,0:T(8,128)S(1)}, f32[64,128]{1,0:T(8,128)}, u32[]{:S(2)}) copy-start(f32[64,128]{1,0:T(8,128)} %constant.129.clone.refs_9_) | copy-start | bytes 98308
  0.0 72.9 %copy-start.1 = (bf16[256,512]{1,0:T(8,128)(2,1)S(1)}, bf16[256,512]{1,0:T(8,128)(2,1)}, u32[]{:S(2)}) copy-start(bf16[256,512]{1,0:T(8,128)(2,1)} %constant.128.clone.refs_8_) | copy-start | bytes 786436
  2.4 48.1 %all-to-all-start = ((f32[256,8,128]{2,1,0:T(8,128)}), f32[256,8,128]{2,1,0:T(8,128)S(1)}, u32[]{:S(2)}, u32[]{:S(2)}) async-start(f32[256,8,128]{2,1,0:T(8,128)} %bitcast.28), calls=%async_computation | async-start | bytes 2097152 | tf_op jit(solution)/shard_map/all_to_all | solution.py:390
  18.1 77.7 %copy-start = (bf16[256,1024]{1,0:T(8,128)(2,1)S(1)}, bf16[256,1024]{1,0:T(8,128)(2,1)}, u32[]{:S(2)}) copy-start(bf16[256,1024]{1,0:T(8,128)(2,1)} %constant.130.clone.refs_8_) | copy-start | bytes 1572868
  52.4 13.3 %collective-permute-start = (f32[2,2,4,32,128]{4,3,2,1,0:T(8,128)S(1)}, f32[2,2,4,32,128]{4,3,2,1,0:T(8,128)S(1)}, u32[]{:S(2)}, u32[]{:S(2)}) collective-permute-start(f32[2,2,4,32,128]{4,3,2,1,0:T(8,128)S(1)} %get-tuple-element.22), channel_id=1, source_target_pairs={{0,73},{1,72},{8,65},{9,64},{64,9},{65,8},{72,1},{73,0},{16,89},{1... | collective-permute-start | bytes 786440 | tf_op jit(solution)/shard_map/ppermute | solution.py:372
  53.5 13.0 %collective-permute-start.1 = (f32[2,2,4,32,128]{4,3,2,1,0:T(8,128)S(1)}, f32[2,2,4,32,128]{4,3,2,1,0:T(8,128)S(1)}, u32[]{:S(2)}, u32[]{:S(2)}) collective-permute-start(f32[2,2,4,32,128]{4,3,2,1,0:T(8,128)S(1)} %get-tuple-element.23), channel_id=1, source_target_pairs={{0,72},{1,73},{8,64},{9,65},{64,8},{65,9},{72,0},{73,1},{16,88},{1... | collective-permute-start | bytes 786440 | tf_op jit(solution)/shard_map/ppermute | solution.py:372
  57.0 14.2 %collective-permute-start.2 = (f32[2,2,4,32,128]{4,3,2,1,0:T(8,128)S(1)}, f32[2,2,4,32,128]{4,3,2,1,0:T(8,128)S(1)}, u32[]{:S(2)}, u32[]{:S(2)}) collective-permute-start(f32[2,2,4,32,128]{4,3,2,1,0:T(8,128)S(1)} %get-tuple-element.24), channel_id=1, source_target_pairs={{0,65},{1,64},{8,73},{9,72},{64,1},{65,0},{72,9},{73,8},{16,81},{1... | collective-permute-start | bytes 786440 | tf_op jit(solution)/shard_map/ppermute | solution.py:372
  59.9 11.3 %collective-permute-start.3 = (f32[2,2,4,32,128]{4,3,2,1,0:T(8,128)S(1)}, f32[2,2,4,32,128]{4,3,2,1,0:T(8,128)S(1)}, u32[]{:S(2)}, u32[]{:S(2)}) collective-permute-start(f32[2,2,4,32,128]{4,3,2,1,0:T(8,128)S(1)} %get-tuple-element.25), channel_id=1, source_target_pairs={{0,9},{1,8},{8,1},{9,0},{64,73},{65,72},{72,65},{73,64},{16,25},{1... | collective-permute-start | bytes 786440 | tf_op jit(solution)/shard_map/ppermute | solution.py:372
  60.7 10.9 %collective-permute-start.4 = (f32[2,2,4,32,128]{4,3,2,1,0:T(8,128)S(1)}, f32[2,2,4,32,128]{4,3,2,1,0:T(8,128)S(1)}, u32[]{:S(2)}, u32[]{:S(2)}) collective-permute-start(f32[2,2,4,32,128]{4,3,2,1,0:T(8,128)S(1)} %get-tuple-element.26), channel_id=1, source_target_pairs={{0,64},{1,65},{8,72},{9,73},{64,0},{65,1},{72,8},{73,9},{16,80},{1... | collective-permute-start | bytes 786440 | tf_op jit(solution)/shard_map/ppermute | solution.py:372
  65.7 6.4 %collective-permute-start.5 = (f32[2,2,4,32,128]{4,3,2,1,0:T(8,128)S(1)}, f32[2,2,4,32,128]{4,3,2,1,0:T(8,128)S(1)}, u32[]{:S(2)}, u32[]{:S(2)}) collective-permute-start(f32[2,2,4,32,128]{4,3,2,1,0:T(8,128)S(1)} %get-tuple-element.27), channel_id=1, source_target_pairs={{0,8},{1,9},{8,0},{9,1},{64,72},{65,73},{72,64},{73,65},{16,24},{1... | collective-permute-start | bytes 786440 | tf_op jit(solution)/shard_map/ppermute | solution.py:372
  66.5 6.4 %collective-permute-start.6 = (f32[2,2,4,32,128]{4,3,2,1,0:T(8,128)S(1)}, f32[2,2,4,32,128]{4,3,2,1,0:T(8,128)S(1)}, u32[]{:S(2)}, u32[]{:S(2)}) collective-permute-start(f32[2,2,4,32,128]{4,3,2,1,0:T(8,128)S(1)} %get-tuple-element.28), channel_id=1, source_target_pairs={{0,1},{1,0},{8,9},{9,8},{64,65},{65,64},{72,73},{73,72},{16,17},{1... | collective-permute-start | bytes 786440 | tf_op jit(solution)/shard_map/ppermute | solution.py:372
  76.7 6.4 %collective-permute-start.7 = (f32[2,4,32,128]{3,2,1,0:T(8,128)S(1)}, f32[2,4,32,128]{3,2,1,0:T(8,128)S(1)}, u32[]{:S(2)}, u32[]{:S(2)}) collective-permute-start(f32[2,4,32,128]{3,2,1,0:T(8,128)S(1)} %get-tuple-element.30), channel_id=1, source_target_pairs={{0,76},{1,72},{8,68},{9,64},{64,12},{65,8},{72,4},{73,0},{16,92},{... | collective-permute-start | bytes 393224 | tf_op jit(solution)/shard_map/ppermute | solution.py:372
  81.1 6.7 %collective-permute-start.8 = (f32[2,4,32,128]{3,2,1,0:T(8,128)S(1)}, f32[2,4,32,128]{3,2,1,0:T(8,128)S(1)}, u32[]{:S(2)}, u32[]{:S(2)}) collective-permute-start(f32[2,4,32,128]{3,2,1,0:T(8,128)S(1)} %get-tuple-element.31), channel_id=1, source_target_pairs={{0,72},{1,76},{8,64},{9,68},{64,8},{65,12},{72,0},{73,4},{16,88},{... | collective-permute-start | bytes 393224 | tf_op jit(solution)/shard_map/ppermute | solution.py:372
  81.1 8.2 %collective-permute-start.9 = (f32[2,4,32,128]{3,2,1,0:T(8,128)S(1)}, f32[2,4,32,128]{3,2,1,0:T(8,128)S(1)}, u32[]{:S(2)}, u32[]{:S(2)}) collective-permute-start(f32[2,4,32,128]{3,2,1,0:T(8,128)S(1)} %get-tuple-element.32), channel_id=1, source_target_pairs={{0,68},{1,64},{8,76},{9,72},{64,4},{65,0},{72,12},{73,8},{16,84},{... | collective-permute-start | bytes 393224 | tf_op jit(solution)/shard_map/ppermute | solution.py:372
  81.9 11.5 %collective-permute-start.10 = (f32[2,4,32,128]{3,2,1,0:T(8,128)S(1)}, f32[2,4,32,128]{3,2,1,0:T(8,128)S(1)}, u32[]{:S(2)}, u32[]{:S(2)}) collective-permute-start(f32[2,4,32,128]{3,2,1,0:T(8,128)S(1)} %get-tuple-element.33), channel_id=1, source_target_pairs={{0,64},{1,68},{8,72},{9,76},{64,0},{65,4},{72,8},{73,12},{16,80},{... | collective-permute-start | bytes 393224 | tf_op jit(solution)/shard_map/ppermute | solution.py:372
  81.9 11.5 %collective-permute-start.11 = (f32[2,4,32,128]{3,2,1,0:T(8,128)S(1)}, f32[2,4,32,128]{3,2,1,0:T(8,128)S(1)}, u32[]{:S(2)}, u32[]{:S(2)}) collective-permute-start(f32[2,4,32,128]{3,2,1,0:T(8,128)S(1)} %get-tuple-element.34), channel_id=1, source_target_pairs={{0,12},{1,8},{8,4},{9,0},{64,76},{65,72},{72,68},{73,64},{16,28},{... | collective-permute-start | bytes 393224 | tf_op jit(solution)/shard_map/ppermute | solution.py:372
  83.0 10.4 %collective-permute-start.12 = (f32[2,4,32,128]{3,2,1,0:T(8,128)S(1)}, f32[2,4,32,128]{3,2,1,0:T(8,128)S(1)}, u32[]{:S(2)}, u32[]{:S(2)}) collective-permute-start(f32[2,4,32,128]{3,2,1,0:T(8,128)S(1)} %get-tuple-element.35), channel_id=1, source_target_pairs={{0,8},{1,12},{8,0},{9,4},{64,72},{65,76},{72,64},{73,68},{16,24},{... | collective-permute-start | bytes 393224 | tf_op jit(solution)/shard_map/ppermute | solution.py:372
  87.8 5.6 %collective-permute-start.13 = (f32[2,4,32,128]{3,2,1,0:T(8,128)S(1)}, f32[2,4,32,128]{3,2,1,0:T(8,128)S(1)}, u32[]{:S(2)}, u32[]{:S(2)}) collective-permute-start(f32[2,4,32,128]{3,2,1,0:T(8,128)S(1)} %get-tuple-element.36), channel_id=1, source_target_pairs={{0,4},{1,0},{8,12},{9,8},{64,68},{65,64},{72,76},{73,72},{16,20},{... | collective-permute-start | bytes 393224 | tf_op jit(solution)/shard_map/ppermute | solution.py:372
  89.3 6.6 %collective-permute-start.14 = (f32[2,4,32,128]{3,2,1,0:T(8,128)S(1)}, f32[2,4,32,128]{3,2,1,0:T(8,128)S(1)}, u32[]{:S(2)}, u32[]{:S(2)}) collective-permute-start(f32[2,4,32,128]{3,2,1,0:T(8,128)S(1)} %get-tuple-element.37), channel_id=1, source_target_pairs={{0,0},{1,4},{8,8},{9,12},{64,64},{65,68},{72,72},{73,76},{16,16},{... | collective-permute-start | bytes 393224 | tf_op jit(solution)/shard_map/ppermute | solution.py:372
